TPU v7x, 32 devices: a whole 2x2x4 slice. The times are simulated.
32 devices in a mesh: seq: 16 (over z, y, core), head: 2 (over x).
Axes of the slice: x: 2, y: 2, z: 4, core: 2. Of those that a mesh axis runs over, the one named last changes fastest.
Arguments:
- queries: bfloat16 [2048, 1024], P('seq', 'head'), may hold values from -8 to 8
- keys: bfloat16 [2048, 1024], P('seq', 'head'), may hold values from -8 to 8
- values: bfloat16 [2048, 1024], P('seq', 'head'), may hold values from -6 to 6
- out_grad: bfloat16 [2048, 1024], P('seq', 'head'), may hold values from -6 to 6
- rel_emb: bfloat16 [512, 1024], replicated, may hold values from -6 to 6
- w_query: bfloat16 [1024, 1024], P(None, 'head'), may hold values from -0.1875 to 0.1875
- w_key: bfloat16 [1024, 1024], P(None, 'head'), may hold values from -0.1875 to 0.1875
- doc_lengths: int32 [8], replicated, may hold values from 1 to 512, 2048 in all
- bucket_table: int32 [1024], replicated, may hold values from 0 to 511, as said below
Outputs:
- query_grad: bfloat16 [2048, 1024], P('seq', 'head')
- key_grad: bfloat16 [2048, 1024], P('seq', 'head')
- value_grad: bfloat16 [2048, 1024], P('seq', 'head')
- rel_emb_grad: float32 [512, 1024], P(None, 'head')
- w_query_grad: float32 [1024, 1024], P('seq', 'head')
- w_key_grad: float32 [1024, 1024], P('seq', 'head')
Inputs may be any that keep to these rules, and one draw needn't show every extreme that they name: `doc_lengths`: the lengths sum to 2048 and the longest is exactly 512. `bucket_table`: entry o is the bucket of the relative offset o - 512; entries never fall as o grows, and equal o - 512 + 512 // 2 wherever o - 512 lies between -128 and 128.
All inputs are finite; a program needn't handle non-finite values.
Results may differ from a plain program's by a relative error of at most 0.01.
Values may be sent and summed in bfloat16 or wider, within the bound.
No kernel may reach another device: no remote copies, remote signals or barrier semaphores. Data moves between devices by JAX's collectives and lax.ppermute only.
A program may use at most 64 MiB of HBM per device.

v0:
```python
import math

import jax
import jax.numpy as jnp
from jax import lax
from jax.sharding import PartitionSpec as P

HD = 64
SPAN = 4


masked_score = -1e30


def shifted(block, axis, distance):
    devices = range(lax.axis_size(axis))
    route = [(i - distance, i) for i in devices if i - distance in devices]
    return lax.ppermute(block, axis, route)


def contract(left, right, left_dim, right_dim):
    return lax.dot_general(
        left, right, (((left_dim,), (right_dim,)), ((), ())), preferred_element_type=jnp.float32
    )


def doc_index(position, doc_ends, extent):
    inside = (position >= 0) & (position < extent)
    owner = jnp.sum((doc_ends[None, :] <= position[:, None]).astype(jnp.int32), axis=1)
    return jnp.where(inside, owner, -1)


def same_document(row_pos, col_pos, doc_ends, extent):
    return (
        doc_index(row_pos, doc_ends, extent)[:, None]
        == doc_index(col_pos, doc_ends, extent)[None, :]
    )


def tile_tables(bucket_table, shift, rows, buckets):
    offset_span = bucket_table.shape[0] // 2
    spread = jnp.arange(2 * rows - 1, dtype=jnp.int32) - (rows - 1)
    ahead_index = bucket_table[jnp.clip(shift - spread + offset_span, 0, 2 * offset_span - 1)]
    behind_index = bucket_table[jnp.clip(offset_span - shift - spread, 0, 2 * offset_span - 1)]
    bucket_ids = jnp.arange(buckets, dtype=jnp.int32)[None, :]
    ahead_onehot = (ahead_index[:, None] == bucket_ids).astype(jnp.bfloat16)
    behind_onehot = (behind_index[:, None] == bucket_ids).astype(jnp.bfloat16)
    return (ahead_index, behind_index, ahead_onehot, behind_onehot)


def skew_in(spread, width):
    rows = spread.shape[0]
    line = rows + width - 1
    flat = jnp.pad(spread, ((0, 0), (0, 1))).reshape(-1)
    return flat[rows - 1 : rows - 1 + rows * line].reshape(rows, line)[:, :width]


def skew_out(dense):
    rows, width = dense.shape
    line = rows + width - 1
    padded = jnp.pad(dense, ((0, 0), (0, rows - 1))).reshape(-1)
    flat = jnp.pad(padded, (rows - 1, 1))
    return flat.reshape(rows, line + 1)[:, :line]


def tile_scores(
    query_rows, key_rows, pos_keys, pos_queries, ahead_onehot, behind_onehot, score_scale
):
    content = contract(query_rows, key_rows, 1, 1)
    ahead_band = contract(ahead_onehot, pos_keys, 1, 0).astype(jnp.bfloat16)
    behind_band = contract(behind_onehot, pos_queries, 1, 0).astype(jnp.bfloat16)
    query_term = skew_in(contract(query_rows, ahead_band, 1, 1), key_rows.shape[0])
    key_term = skew_in(contract(key_rows, behind_band, 1, 1), query_rows.shape[0]).T
    return score_scale * (content + query_term + key_term)


def query_side(
    query_rows,
    key_rows,
    value_rows,
    grad_rows,
    pos_keys,
    pos_queries,
    same_doc,
    tables,
    score_scale,
):
    tile_rows = query_rows.shape[0]
    tile_count = key_rows.shape[0] // tile_rows
    pieces = []
    for tile in range(tile_count):
        key_tile = key_rows[tile * tile_rows : (tile + 1) * tile_rows]
        pieces.append(
            tile_scores(
                query_rows,
                key_tile,
                pos_keys,
                pos_queries,
                tables[tile][2],
                tables[tile][3],
                score_scale,
            )
        )
    scores = jnp.where(same_doc, jnp.concatenate(pieces, 1), masked_score)
    row_max = jnp.max(scores, axis=1, keepdims=True)
    expd = jnp.where(same_doc, jnp.exp(scores - row_max), 0.0)
    row_sum = jnp.sum(expd, axis=1, keepdims=True)
    probs = expd / row_sum
    dprobs = contract(grad_rows, value_rows, 1, 1)
    row_dot = jnp.sum(probs * dprobs, axis=1, keepdims=True)
    dscores = probs * (dprobs - row_dot)
    dscores_low = dscores.astype(jnp.bfloat16)
    ahead_grad = jnp.zeros((tile_rows, pos_keys.shape[0]), jnp.float32)
    for tile in range(tile_count):
        band = dscores_low[:, tile * tile_rows : (tile + 1) * tile_rows]
        ahead_grad = ahead_grad + contract(skew_out(band), tables[tile][2], 1, 0)
    ahead_low = ahead_grad.astype(jnp.bfloat16)
    query_grad = score_scale * (
        contract(dscores_low, key_rows, 1, 0) + contract(ahead_low, pos_keys, 1, 0)
    )
    bucket_key = score_scale * contract(ahead_low, query_rows, 0, 0)
    probs_low = probs.astype(jnp.bfloat16)
    behind_parts = []
    for tile in range(tile_count):
        band = dscores_low[:, tile * tile_rows : (tile + 1) * tile_rows]
        behind_parts.append(contract(skew_out(band.T), tables[tile][3], 1, 0).astype(jnp.bfloat16))
    behind_low = jnp.concatenate(behind_parts, 0)
    key_grad = score_scale * (
        contract(dscores_low, query_rows, 0, 0) + contract(behind_low, pos_queries, 1, 0)
    )
    value_grad = contract(probs_low, grad_rows, 0, 0)
    bucket_query = score_scale * contract(behind_low, key_rows, 0, 0)
    return (query_grad, key_grad, value_grad, bucket_key, bucket_query)


def split_heads(matrix):
    return matrix.reshape(matrix.shape[0], matrix.shape[1] // HD, HD).transpose(1, 0, 2)


def join_heads(stacked):
    return stacked.transpose(1, 0, 2).reshape(stacked.shape[1], stacked.shape[0] * HD)


def body(queries, keys, values, out_grad, rel_emb, w_query, w_key, doc_lengths, bucket_table):
    tokens_dev = queries.shape[0]
    seq_count = lax.axis_size("seq")
    neighbours = min(SPAN, seq_count // 4)
    extent = tokens_dev * seq_count
    seq_index = lax.axis_index("seq")
    first_token = seq_index * tokens_dev
    score_scale = 1.0 / math.sqrt(3.0 * HD)
    pos_key = jnp.dot(rel_emb, w_key, preferred_element_type=jnp.float32).astype(jnp.bfloat16)
    pos_query = jnp.dot(rel_emb, w_query, preferred_element_type=jnp.float32).astype(jnp.bfloat16)
    doc_ends = jnp.cumsum(doc_lengths)
    buckets = rel_emb.shape[0]
    tables = [
        tile_tables(bucket_table, (neighbours - tile) * tokens_dev, tokens_dev, buckets)
        for tile in range(2 * neighbours + 1)
    ]
    hop_list = list(range(neighbours, 0, -1)) + list(range(-1, -neighbours - 1, -1))
    fetched = []
    for distance in hop_list:
        fetched.append(shifted((keys, values), "seq", distance))
    lower_side = fetched[:neighbours]
    upper_side = fetched[neighbours:]
    key_window = jnp.concatenate(
        [pair[0] for pair in lower_side] + [keys] + [pair[0] for pair in upper_side], 0
    )
    value_window = jnp.concatenate(
        [pair[1] for pair in lower_side] + [values] + [pair[1] for pair in upper_side], 0
    )
    window = key_window.shape[0]
    query_pos = first_token + jnp.arange(tokens_dev, dtype=jnp.int32)
    window_pos = first_token - neighbours * tokens_dev + jnp.arange(window, dtype=jnp.int32)
    same_doc = same_document(query_pos, window_pos, doc_ends, extent)
    query_heads = split_heads(queries)
    grad_heads = split_heads(out_grad)
    pos_key_heads = split_heads(pos_key)
    pos_query_heads = split_heads(pos_query)

    def every_pair(operands):
        query_rows, key_rows, value_rows, grad_rows, pos_keys, pos_queries = operands
        return query_side(
            query_rows,
            key_rows,
            value_rows,
            grad_rows,
            pos_keys,
            pos_queries,
            same_doc,
            tables,
            score_scale,
        )

    query_grad, key_part, value_part, bucket_key, bucket_query = lax.map(
        every_pair,
        (
            query_heads,
            split_heads(key_window),
            split_heads(value_window),
            grad_heads,
            pos_key_heads,
            pos_query_heads,
        ),
    )
    key_flat = join_heads(key_part)
    value_flat = join_heads(value_part)
    key_total = key_flat[neighbours * tokens_dev : (neighbours + 1) * tokens_dev]
    value_total = value_flat[neighbours * tokens_dev : (neighbours + 1) * tokens_dev]
    for distance in hop_list:
        segment = neighbours - distance
        returned = (
            key_flat[segment * tokens_dev : (segment + 1) * tokens_dev],
            value_flat[segment * tokens_dev : (segment + 1) * tokens_dev],
        )
        arrived = shifted((returned[0], returned[1]), "seq", -distance)
        key_total = key_total + arrived[0]
        value_total = value_total + arrived[1]
    key_grad = key_total.astype(jnp.bfloat16)
    value_grad = value_total.astype(jnp.bfloat16)
    query_out = join_heads(query_grad).astype(jnp.bfloat16)
    summed = lax.psum((join_heads(bucket_key), join_heads(bucket_query)), "seq")
    bucket_key_low = summed[0].astype(jnp.bfloat16)
    bucket_query_low = summed[1].astype(jnp.bfloat16)
    rows_dev = rel_emb.shape[1] // seq_count
    rel_columns = lax.dynamic_slice_in_dim(rel_emb, seq_index * rows_dev, rows_dev, 1)
    w_key_grad = contract(rel_columns, bucket_key_low, 0, 0)
    w_query_grad = contract(rel_columns, bucket_query_low, 0, 0)
    rel_partial = contract(bucket_key_low, w_key, 1, 1) + contract(bucket_query_low, w_query, 1, 1)
    rel_emb_grad = lax.psum_scatter(
        rel_partial.astype(jnp.bfloat16), "head", scatter_dimension=1, tiled=True
    ).astype(jnp.float32)
    return (query_out, key_grad, value_grad, rel_emb_grad, w_query_grad, w_key_grad)


def solution(mesh):
    in_specs = (
        P("seq", "head"),
        P("seq", "head"),
        P("seq", "head"),
        P("seq", "head"),
        P(),
        P(None, "head"),
        P(None, "head"),
        P(),
        P(),
    )
    out_specs = (
        P("seq", "head"),
        P("seq", "head"),
        P("seq", "head"),
        P(None, "head"),
        P("seq", "head"),
        P("seq", "head"),
    )
    return jax.shard_map(body, mesh=mesh, in_specs=in_specs, out_specs=out_specs, check_vma=False)
```

profile of v0, /device:TPU:0, one launch (start us, length us, event | category | flops | bytes accessed | tf_op | source)
XLA Modules:
  0.0 825.2 jit_solution(365845510317824854)
XLA Ops:
  13.3 6.2 collective-permute-start.1
  19.5 5.4 collective-permute-start
  27.1 2.4 convolution_convert_fusion.27
  36.2 2.0 gather_fusion.6
  51.3 4.3 collective-permute-start.2
  58.8 5.3 collective-permute-start.9
  64.1 3.1 collective-permute-start.8
  67.3 3.5 collective-permute-done.8
  70.8 2.8 collective-permute-start.10
  78.8 4.6 collective-permute-done.4
  86.6 7.2 collective-permute-done.6
  95.1 3.1 collective-permute-done.7
  102.4 560.0 %while.22 = (s32[]{:T(128)}, bf16[8,128,64]{1,2,0:T(8,128)(2,1)}, f32[8,1152,64]{1,2,0:T(8,128)}, f32[8,1152,64]{1,2,0:T(8,128)}, f32[8,512,64]{1,2,0:T(8,128)},...) while((s32[]{:T(128)}, bf16[8,128,64]{1,2,0:T(8,128)(2,1)}, ...), condition=%wide.region_7.8_spmd.clone, body=%wide.region_3.7_spmd.clone.sunk | while | flops 1255631232 | bytes 62306428 | solution.py:195
  662.4 75.1 %all-reduce.55 = (bf16[512,512]{0,1:T(8,128)(2,1)S(1)}, bf16[512,512]{0,1:T(8,128)(2,1)S(1)}) all-reduce(f32[512,512]{0,1:T(8,128)} %bitcast.686, f32[512,512]{0,1:T(8,128)} %bitcast.685), channel_id=1, replica_groups=mesh['seq'=16,'head'=2] {'seq'}, use_global_device_ids=true, to_apply=%region_8.9 | all-reduce | flops 524288 | bytes 3145728 | tf_op jit(solution)/shard_map/psum | solution.py:222
  740.9 3.2 fusion.345
  744.1 2.0 collective-permute-start.23
  755.5 11.2 %collective-permute-done.21 = f32[128,512]{0,1:T(8,128)S(1)} collective-permute-done((f32[128,512]{0,1:T(8,128)}, f32[128,512]{0,1:T(8,128)S(1)}, u32[]{:S(2)}, u32[]{:S(2)}) %collective-permute-start.21) | collective-permute-done | bytes 262176 | tf_op jit(solution)/shard_map/ppermute | solution.py:18
  768.1 4.6 collective-permute-start.31
  774.0 6.5 collective-permute-start.29
  785.2 3.9 collective-permute-start.28
  796.6 5.9 collective-permute-done.26
  802.5 2.6 collective-permute-done.25
  805.1 8.9 %collective-permute-done.24 = f32[128,512]{0,1:T(8,128)} collective-permute-done((f32[128,512]{0,1:T(8,128)S(1)}, f32[128,512]{0,1:T(8,128)}, u32[]{:S(2)}, u32[]{:S(2)}) %collective-permute-start.24) | collective-permute-done | bytes 262176 | tf_op jit(solution)/shard_map/ppermute | solution.py:18
  816.2 2.1 convert_element_type.385
  (2800 shorter events, 617.5 us)
Async XLA Ops:
  7.2 809.0 %reduce-scatter.2.cloned.1.call-start = ((), (), s32[]{:S(2)}) async-start(), calls=%async_computation.1 | async-start | bytes 1572864 | tf_op jit(solution)/shard_map/reduce_scatter | solution.py:230
  8.3 92.1 %collective-permute-start.15 = (bf16[128,512]{0,1:T(8,128)(2,1)S(1)}, bf16[128,512]{0,1:T(8,128)(2,1)}, u32[]{:S(2)}, u32[]{:S(2)}) collective-permute-start(bf16[128,512]{0,1:T(8,128)(2,1)S(1)} %copy.120), channel_id=1, source_target_pairs={{8,0},{10,2},{12,4},{14,6},{16,8},{18,10},{20,12},{22,14},{24,16},... | collective-permute-start | bytes 393224 | tf_op jit(solution)/shard_map/ppermute | solution.py:18
  9.6 89.8 %collective-permute-start.14 = (bf16[128,512]{0,1:T(8,128)(2,1)S(1)}, bf16[128,512]{0,1:T(8,128)(2,1)}, u32[]{:S(2)}, u32[]{:S(2)}) collective-permute-start(bf16[128,512]{0,1:T(8,128)(2,1)S(1)} %copy.120), channel_id=1, source_target_pairs={{6,0},{8,2},{10,4},{12,6},{14,8},{16,10},{18,12},{20,14},{22,16},{... | collective-permute-start | bytes 393224 | tf_op jit(solution)/shard_map/ppermute | solution.py:18
  10.9 87.4 %collective-permute-start.13 = (bf16[128,512]{0,1:T(8,128)(2,1)S(1)}, bf16[128,512]{0,1:T(8,128)(2,1)}, u32[]{:S(2)}, u32[]{:S(2)}) collective-permute-start(bf16[128,512]{0,1:T(8,128)(2,1)S(1)} %copy.120), channel_id=1, source_target_pairs={{4,0},{6,2},{8,4},{10,6},{12,8},{14,10},{16,12},{18,14},{20,16},{2... | collective-permute-start | bytes 393224 | tf_op jit(solution)/shard_map/ppermute | solution.py:18
  13.3 43.2 %collective-permute-start.1 = (bf16[128,512]{0,1:T(8,128)(2,1)S(1)}, bf16[128,512]{0,1:T(8,128)(2,1)}, u32[]{:S(2)}, u32[]{:S(2)}) collective-permute-start(bf16[128,512]{0,1:T(8,128)(2,1)S(1)} %copy.108), channel_id=1, source_target_pairs={{0,6},{2,8},{4,10},{6,12},{8,14},{10,16},{12,18},{14,20},{16,22},{... | collective-permute-start | bytes 393224 | tf_op jit(solution)/shard_map/ppermute | solution.py:18
  19.5 31.8 %collective-permute-start = (bf16[128,512]{0,1:T(8,128)(2,1)S(1)}, bf16[128,512]{0,1:T(8,128)(2,1)}, u32[]{:S(2)}, u32[]{:S(2)}) collective-permute-start(bf16[128,512]{0,1:T(8,128)(2,1)S(1)} %copy.108), channel_id=1, source_target_pairs={{0,8},{2,10},{4,12},{6,14},{8,16},{10,18},{12,20},{14,22},{16,24},... | collective-permute-start | bytes 393224 | tf_op jit(solution)/shard_map/ppermute | solution.py:18
  58.8 14.8 %collective-permute-start.9 = (bf16[128,512]{0,1:T(8,128)(2,1)S(1)}, bf16[128,512]{0,1:T(8,128)(2,1)S(1)}, u32[]{:S(2)}, u32[]{:S(2)}) collective-permute-start(bf16[128,512]{0,1:T(8,128)(2,1)S(1)} %copy.120), channel_id=1, source_target_pairs={{0,6},{2,8},{4,10},{6,12},{8,14},{10,16},{12,18},{14,20},{16,22},{... | collective-permute-start | bytes 393224 | tf_op jit(solution)/shard_map/ppermute | solution.py:18
  76.1 9.2 %collective-permute-start.5 = (bf16[128,512]{0,1:T(8,128)(2,1)S(1)}, bf16[128,512]{0,1:T(8,128)(2,1)S(1)}, u32[]{:S(2)}, u32[]{:S(2)}) collective-permute-start(bf16[128,512]{0,1:T(8,128)(2,1)S(1)} %copy.108), channel_id=1, source_target_pairs={{4,0},{6,2},{8,4},{10,6},{12,8},{14,10},{16,12},{18,14},{20,16},{2... | collective-permute-start | bytes 393224 | tf_op jit(solution)/shard_map/ppermute | solution.py:18
  83.4 10.4 %collective-permute-start.6 = (bf16[128,512]{0,1:T(8,128)(2,1)S(1)}, bf16[128,512]{0,1:T(8,128)(2,1)S(1)}, u32[]{:S(2)}, u32[]{:S(2)}) collective-permute-start(bf16[128,512]{0,1:T(8,128)(2,1)S(1)} %copy.108), channel_id=1, source_target_pairs={{6,0},{8,2},{10,4},{12,6},{14,8},{16,10},{18,12},{20,14},{22,16},{... | collective-permute-start | bytes 393224 | tf_op jit(solution)/shard_map/ppermute | solution.py:18
  85.3 13.0 %collective-permute-start.7 = (bf16[128,512]{0,1:T(8,128)(2,1)S(1)}, bf16[128,512]{0,1:T(8,128)(2,1)S(1)}, u32[]{:S(2)}, u32[]{:S(2)}) collective-permute-start(bf16[128,512]{0,1:T(8,128)(2,1)S(1)} %copy.108), channel_id=1, source_target_pairs={{8,0},{10,2},{12,4},{14,6},{16,8},{18,10},{20,12},{22,14},{24,16},... | collective-permute-start | bytes 393224 | tf_op jit(solution)/shard_map/ppermute | solution.py:18
  746.1 8.0 collective-permute-start.22
  747.4 19.4 %collective-permute-start.21 = (f32[128,512]{0,1:T(8,128)}, f32[128,512]{0,1:T(8,128)S(1)}, u32[]{:S(2)}, u32[]{:S(2)}) collective-permute-start(f32[128,512]{0,1:T(8,128)} %bitcast.698), channel_id=1, source_target_pairs={{0,4},{2,6},{4,8},{6,10},{8,12},{10,14},{12,16},{14,18},{16,20},{1... | collective-permute-start | bytes 786440 | tf_op jit(solution)/shard_map/ppermute | solution.py:18
  748.7 19.3 %collective-permute-start.20 = (f32[128,512]{0,1:T(8,128)}, f32[128,512]{0,1:T(8,128)S(1)}, u32[]{:S(2)}, u32[]{:S(2)}) collective-permute-start(f32[128,512]{0,1:T(8,128)} %bitcast.697), channel_id=1, source_target_pairs={{0,2},{2,4},{4,6},{6,8},{8,10},{10,12},{12,14},{14,16},{16,18},{18... | collective-permute-start | bytes 786440 | tf_op jit(solution)/shard_map/ppermute | solution.py:18
  750.0 22.6 %collective-permute-start.19 = (f32[128,512]{0,1:T(8,128)}, f32[128,512]{0,1:T(8,128)S(1)}, u32[]{:S(2)}, u32[]{:S(2)}) collective-permute-start(f32[128,512]{0,1:T(8,128)} %bitcast.696), channel_id=1, source_target_pairs={{2,0},{4,2},{6,4},{8,6},{10,8},{12,10},{14,12},{16,14},{18,16},{20... | collective-permute-start | bytes 786440 | tf_op jit(solution)/shard_map/ppermute | solution.py:18
  751.3 22.6 %collective-permute-start.18 = (f32[128,512]{0,1:T(8,128)}, f32[128,512]{0,1:T(8,128)S(1)}, u32[]{:S(2)}, u32[]{:S(2)}) collective-permute-start(f32[128,512]{0,1:T(8,128)} %bitcast.695), channel_id=1, source_target_pairs={{4,0},{6,2},{8,4},{10,6},{12,8},{14,10},{16,12},{18,14},{20,16},{2... | collective-permute-start | bytes 786440 | tf_op jit(solution)/shard_map/ppermute | solution.py:18
  754.1 31.1 %collective-permute-start.17 = (f32[128,512]{0,1:T(8,128)}, f32[128,512]{0,1:T(8,128)}, u32[]{:S(2)}, u32[]{:S(2)}) collective-permute-start(f32[128,512]{0,1:T(8,128)} %bitcast.28), channel_id=1, source_target_pairs={{6,0},{8,2},{10,4},{12,6},{14,8},{16,10},{18,12},{20,14},{22,16},{... | collective-permute-start | bytes 786440 | tf_op jit(solution)/shard_map/ppermute | solution.py:18
  766.8 22.4 %collective-permute-start.16 = (f32[128,512]{0,1:T(8,128)}, f32[128,512]{0,1:T(8,128)}, u32[]{:S(2)}, u32[]{:S(2)}) collective-permute-start(f32[128,512]{0,1:T(8,128)} %bitcast.27), channel_id=1, source_target_pairs={{8,0},{10,2},{12,4},{14,6},{16,8},{18,10},{20,12},{22,14},{24,16},... | collective-permute-start | bytes 786440 | tf_op jit(solution)/shard_map/ppermute | solution.py:18
  768.1 22.3 %collective-permute-start.31 = (f32[128,512]{0,1:T(8,128)}, f32[128,512]{0,1:T(8,128)S(1)}, u32[]{:S(2)}, u32[]{:S(2)}) collective-permute-start(f32[128,512]{0,1:T(8,128)} %bitcast.44), channel_id=1, source_target_pairs={{0,8},{2,10},{4,12},{6,14},{8,16},{10,18},{12,20},{14,22},{16,24},... | collective-permute-start | bytes 786440 | tf_op jit(solution)/shard_map/ppermute | solution.py:18
  772.7 19.1 %collective-permute-start.30 = (f32[128,512]{0,1:T(8,128)}, f32[128,512]{0,1:T(8,128)S(1)}, u32[]{:S(2)}, u32[]{:S(2)}) collective-permute-start(f32[128,512]{0,1:T(8,128)} %bitcast.43), channel_id=1, source_target_pairs={{0,6},{2,8},{4,10},{6,12},{8,14},{10,16},{12,18},{14,20},{16,22},{... | collective-permute-start | bytes 786440 | tf_op jit(solution)/shard_map/ppermute | solution.py:18
  774.0 19.0 %collective-permute-start.29 = (f32[128,512]{0,1:T(8,128)}, f32[128,512]{0,1:T(8,128)}, u32[]{:S(2)}, u32[]{:S(2)}) collective-permute-start(f32[128,512]{0,1:T(8,128)} %bitcast.42), channel_id=1, source_target_pairs={{0,4},{2,6},{4,8},{6,10},{8,12},{10,14},{12,16},{14,18},{16,20},{1... | collective-permute-start | bytes 786440 | tf_op jit(solution)/shard_map/ppermute | solution.py:18
  785.2 11.4 %collective-permute-start.28 = (f32[128,512]{0,1:T(8,128)}, f32[128,512]{0,1:T(8,128)}, u32[]{:S(2)}, u32[]{:S(2)}) collective-permute-start(f32[128,512]{0,1:T(8,128)} %bitcast.694), channel_id=1, source_target_pairs={{0,2},{2,4},{4,6},{6,8},{8,10},{10,12},{12,14},{14,16},{16,18},{18... | collective-permute-start | bytes 786440 | tf_op jit(solution)/shard_map/ppermute | solution.py:18
  790.4 12.0 %collective-permute-start.26 = (f32[128,512]{0,1:T(8,128)}, f32[128,512]{0,1:T(8,128)}, u32[]{:S(2)}, u32[]{:S(2)}) collective-permute-start(f32[128,512]{0,1:T(8,128)} %bitcast.692), channel_id=1, source_target_pairs={{4,0},{6,2},{8,4},{10,6},{12,8},{14,10},{16,12},{18,14},{20,16},{2... | collective-permute-start | bytes 786440 | tf_op jit(solution)/shard_map/ppermute | solution.py:18
  791.7 13.3 %collective-permute-start.25 = (f32[128,512]{0,1:T(8,128)}, f32[128,512]{0,1:T(8,128)}, u32[]{:S(2)}, u32[]{:S(2)}) collective-permute-start(f32[128,512]{0,1:T(8,128)} %bitcast.691), channel_id=1, source_target_pairs={{6,0},{8,2},{10,4},{12,6},{14,8},{16,10},{18,12},{20,14},{22,16},{... | collective-permute-start | bytes 786440 | tf_op jit(solution)/shard_map/ppermute | solution.py:18
  793.1 20.9 %collective-permute-start.24 = (f32[128,512]{0,1:T(8,128)S(1)}, f32[128,512]{0,1:T(8,128)}, u32[]{:S(2)}, u32[]{:S(2)}) collective-permute-start(f32[128,512]{0,1:T(8,128)S(1)} %bitcast.690), channel_id=1, source_target_pairs={{8,0},{10,2},{12,4},{14,6},{16,8},{18,10},{20,12},{22,14},{24,16},... | collective-permute-start | bytes 786440 | tf_op jit(solution)/shard_map/ppermute | solution.py:18
  (394 other events, 1742.2 us)
Sparse Core Ops, SparseCore 0:
  741.0 17.5 reduce-scatter.1
where the time goes:
time: 834 us; the launch traced here: 825 us
  matrix products  349 us (42%)
  local copies, waits for them, and re-layouts  233 us (28%)
  blocking collectives  75.1 us (9%)
  starting transfers between devices  72.5 us (9%)
  waiting for transfers between devices  48.8 us (6%)
  loops' own time  17 us (2%)
  between operations  15 us (2%)
  other arithmetic  14 us (2%)
    dot_general x428, matrix products, contract(): lax.dot_general(left, right, (((left_dim,), (right_dim,)), ((), ())), pre...  346 us
    psum x1, blocking collectives, body(): summed = lax.psum((join_heads(bucket_key), join_heads(bucket_query)), 'seq')  75.1 us
    ppermute x32, starting transfers between devices, shifted(): return lax.ppermute(block, axis, route)  72.5 us
    ppermute x32, waiting for transfers between devices, shifted(): return lax.ppermute(block, axis, route)  48.8 us
    reshape x144, local copies, waits for them, and re-layouts, skew_in(): return flat[rows - 1:rows - 1 + rows * line].reshape(rows, line)[:, :width]  48.1 us
    while x1216, local copies, waits for them, and re-layouts  48 us
    reshape x144, local copies, waits for them, and re-layouts, skew_out(): padded = jnp.pad(dense, ((0, 0), (0, rows - 1))).reshape(-1)  47.2 us
    another operation x1, loops' own time, body(): lax.map(every_pair, (query_heads, split_heads(key_window), split_heads(va...  17 us
  transfers between devices with their start and end apart: 33, of which 10 were waited for; matrix products, arithmetic and copies ran while one was open for 5% of the time, Pallas kernels for 0%

commit v1 on v0

--- a/solution.py
+++ b/solution.py
@@ -3,10 +3,15 @@
 import jax
 import jax.numpy as jnp
 from jax import lax
+from jax.experimental import pallas as pl
+from jax.experimental.pallas import tpu as pltpu
 from jax.sharding import PartitionSpec as P
 
 HD = 64
 SPAN = 4
+TILE = 128
+BF = jnp.bfloat16
+F32 = jnp.float32
 
 
 masked_score = -1e30
@@ -233,6 +238,350 @@
     return (query_out, key_grad, value_grad, rel_emb_grad, w_query_grad, w_key_grad)
 
 
+def nn(left, right):
+    return contract(left, right, 1, 0)
+
+
+def nt(left, right):
+    return contract(left, right, 1, 1)
+
+
+def grid_of(shape):
+    return (
+        lax.broadcasted_iota(jnp.int32, shape, 0),
+        lax.broadcasted_iota(jnp.int32, shape, 1),
+    )
+
+
+def pack_kernel(q_ref, g_ref, k_ref, v_ref, out_ref):
+    for head in range(out_ref.shape[0] // 2):
+        cols = slice(head * HD, (head + 1) * HD)
+        piece = jnp.concatenate(
+            [q_ref[:, cols], g_ref[:, cols], k_ref[:, cols], v_ref[:, cols]], 1
+        )
+        out_ref[2 * head] = piece
+        out_ref[2 * head + 1] = piece
+
+
+def head_kernel(
+    lens_ref, half_ref, all_ref, pos_ref, table_ref, rel_ref, out_ref,
+    onehot, pk, pq, acc, acc_pos, g_key, g_query, k_t, k_rev, s_q, st, dp, dtile, dq_nat, dq_pos,
+):
+    tiles = all_ref.shape[0]
+    halo = table_ref.shape[1] // 2 // TILE
+    span = 2 * halo + 1
+    scale = 1.0 / math.sqrt(3.0 * HD)
+    valid0 = (halo + 1) * TILE
+    valid = table_ref.shape[1]
+    buckets = pos_ref.shape[0]
+    half = half_ref[0]
+    row, col = grid_of((TILE, TILE))
+    swap = jnp.where(row + col == TILE - 1, 1.0, 0.0).astype(BF)
+    wrap = row + col >= TILE - 1
+    wrap_rev = col >= row
+    low = col < HD
+
+    for part in range(buckets // TILE):
+        ids = lax.broadcasted_iota(jnp.int32, (TILE, valid), 0) + part * TILE
+        onehot[pl.ds(part * TILE, TILE), :] = jnp.where(ids == table_ref[...], 1.0, 0.0).astype(BF)
+    pos_t = pos_ref[...].astype(F32).T.astype(BF)
+    expanded = nn(pos_t, onehot[...]).astype(BF)
+    pk[...] = jnp.zeros_like(pk)
+    pq[...] = jnp.zeros_like(pq)
+    pk[0:HD, valid0 : valid0 + valid] = expanded[:HD]
+    pq[0:HD, valid0 : valid0 + valid] = expanded[HD:]
+    acc[...] = jnp.zeros_like(acc)
+    acc_pos[...] = jnp.zeros_like(acc_pos)
+    g_key[...] = jnp.zeros_like(g_key)
+    g_query[...] = jnp.zeros_like(g_query)
+
+    def transpose_tile(tile, carry):
+        turned = all_ref[tile, :, 2 * HD : 4 * HD].astype(F32).T.astype(BF)
+        k_t[tile] = turned
+        k_rev[tile] = nn(turned[:HD], swap).astype(BF)
+        return carry
+
+    lax.fori_loop(0, tiles, transpose_tile, 0)
+
+    def block(b, carry):
+        own = 2 * b + half
+        first = jnp.clip(own - halo, 0, tiles - span)
+        delta = (own - first) * TILE
+        qd = all_ref[own, :, 0 : 2 * HD]
+        turned = qd.astype(F32).T
+        upper = row < HD
+        right = jnp.concatenate(
+            [jnp.where(upper, turned, 0.0), jnp.where(upper, 0.0, turned)], 1
+        ).astype(BF)
+        q_rev = nn(turned[:HD].astype(BF), swap).astype(BF)
+
+        position = own * TILE + lax.broadcasted_iota(jnp.int32, (1, TILE), 1)
+
+        def next_doc(d, state):
+            end, start, stop = state
+            end = end + lens_ref[d]
+            start = jnp.where(end <= position, end, start)
+            stop = jnp.where((end > position) & (stop < 0), end, stop)
+            return (end, start, stop)
+
+        _, start, stop = lax.fori_loop(
+            0,
+            lens_ref.shape[0],
+            next_doc,
+            (jnp.int32(0), jnp.zeros((1, TILE), jnp.int32), jnp.full((1, TILE), -1, jnp.int32)),
+        )
+        start = start - first * TILE
+        stop = stop - first * TILE
+
+        key_x = pl.multiple_of(halo * 2 * TILE - delta, TILE)
+        s_q[...] = nn(qd, pk[:, pl.ds(key_x, (span + 1) * TILE)])
+        best = jnp.full((8, TILE), masked_score, F32)
+        for t in range(span):
+            kv = all_ref[first + t, :, 2 * HD : 4 * HD]
+            both = nn(kv, right)
+            query_x = pl.multiple_of(2 * halo * TILE + delta - t * TILE, TILE)
+            s_k = nn(kv, pq[:, pl.ds(query_x, 2 * TILE)])
+            key_term = pltpu.roll(
+                jnp.where(wrap, s_k[:, :TILE], s_k[:, TILE:]), 1, 1, stride=1, stride_axis=0
+            )
+            query_term = pltpu.roll(
+                jnp.where(
+                    wrap,
+                    s_q[:, t * TILE : (t + 1) * TILE],
+                    s_q[:, (t + 1) * TILE : (t + 2) * TILE],
+                ),
+                1,
+                1,
+                stride=1,
+                stride_axis=0,
+            )
+            score = both[:, :TILE] + key_term + query_term.T
+            place = row + t * TILE
+            score = jnp.where((place >= start) & (place < stop), score, masked_score)
+            st[t] = score
+            dp[t] = both[:, TILE:]
+            best = jnp.maximum(best, jnp.max(score.reshape(TILE // 8, 8, TILE), 0))
+        top = jnp.max(best, 0, keepdims=True)
+        total = jnp.zeros((8, TILE), F32)
+        dot = jnp.zeros((8, TILE), F32)
+        for t in range(span):
+            expd = jnp.exp((st[t] - top) * scale)
+            st[t] = expd
+            total = total + jnp.sum(expd.reshape(TILE // 8, 8, TILE), 0)
+            dot = dot + jnp.sum((expd * dp[t]).reshape(TILE // 8, 8, TILE), 0)
+        inverse = 1.0 / jnp.sum(total, 0, keepdims=True)
+        row_dot = jnp.sum(dot, 0, keepdims=True) * inverse
+
+        lows = jnp.where(low, qd, jnp.zeros_like(qd))
+        pair = jnp.concatenate([lows, jnp.where(low, jnp.zeros_like(qd), qd)], 0)
+        dq_t = jnp.zeros((HD, TILE), F32)
+        before = jnp.zeros((TILE, TILE), F32)
+        for t in range(span):
+            prob = st[t] * inverse
+            dscore = (prob * (dp[t] - row_dot)).astype(BF)
+            query_x = pl.multiple_of(2 * halo * TILE + delta - t * TILE, TILE)
+            lhs = jnp.concatenate([dscore, prob.astype(BF)], 1)
+            acc[first + t] += nn(lhs, pair)
+            stacked = nn(jnp.concatenate([k_t[first + t][:HD], swap], 0), dscore)
+            dq_t = dq_t + stacked[:HD]
+            y = pltpu.roll(stacked[HD:], 0, 1, stride=1, stride_axis=0)
+            spread = jnp.concatenate(
+                [jnp.where(wrap_rev, y, 0.0), jnp.where(wrap_rev, 0.0, y)], 1
+            ).astype(BF)
+            acc_pos[first + t] += nt(spread, pq[0:HD, pl.ds(query_x, 2 * TILE)])
+            g_query[:, pl.ds(query_x, 2 * TILE)] += nn(k_rev[first + t], spread)
+            z = pltpu.roll(nt(swap, dscore), 0, 1, stride=1, stride_axis=0)
+            dtile[:, t * TILE : (t + 1) * TILE] = jnp.where(wrap_rev, z, before).astype(BF)
+            before = z
+        dtile[:, span * TILE :] = jnp.where(wrap_rev, 0.0, before).astype(BF)
+        spread_q = dtile[...]
+        window = pl.ds(key_x, (span + 1) * TILE)
+        g_key[:, window] += nn(q_rev, spread_q)
+        back = nt(spread_q, pk[0:HD, window])
+        high = back.astype(BF)
+        dq_pos[b] = jnp.concatenate([high, (back - high.astype(F32)).astype(BF)], 1)
+        dq_nat[b] = dq_t
+        return carry
+
+    lax.fori_loop(0, tiles // 2, block, 0)
+
+    parts = []
+    for g in (g_key, g_query):
+        band = g[:, valid0 : valid0 + valid]
+        high = band.astype(BF)
+        parts += [high, (band - high.astype(F32)).astype(BF)]
+    summed = nt(jnp.concatenate(parts, 0), onehot[...])
+    bucket_t = scale * jnp.concatenate(
+        [summed[:HD] + summed[HD : 2 * HD], summed[2 * HD : 3 * HD] + summed[3 * HD :]], 0
+    )
+    bucket_low = bucket_t.astype(BF)
+    weight_t = nn(bucket_low, rel_ref[...])
+    w_rows = rel_ref.shape[1] // tiles
+    b_rows = buckets // tiles
+    weight = weight_t.T.astype(BF)
+    bucket = bucket_t.T.astype(BF)
+    base_w = TILE + TILE // 2
+    base_b = base_w + w_rows
+    for tile in range(tiles):
+        out_ref[tile, base_w:base_b, :] = weight[tile * w_rows : (tile + 1) * w_rows]
+        out_ref[tile, base_b : base_b + b_rows, :] = bucket[tile * b_rows : (tile + 1) * b_rows]
+    factor = jnp.where(low, scale, 1.0)
+
+    def finish_keys(tile, carry):
+        back = acc_pos[tile]
+        high = back.astype(BF)
+        both = nn(swap, jnp.concatenate([high, (back - high.astype(F32)).astype(BF)], 1))
+        extra = both[:, :HD] + both[:, HD:]
+        extra = jnp.concatenate([extra, jnp.zeros_like(extra)], 1)
+        out_ref[tile, 0:TILE, :] = ((acc[tile] + extra) * factor).astype(BF)
+        return carry
+
+    lax.fori_loop(0, tiles, finish_keys, 0)
+
+    def finish_queries(b, carry):
+        both = nn(swap, dq_pos[b])
+        extra = both[:, :HD] + both[:, HD:]
+        grad = scale * (dq_nat[b].T + extra)
+        piece = jnp.concatenate([grad[: TILE // 2], grad[TILE // 2 :]], 1).astype(BF)
+        out_ref[2 * b, TILE:base_w, :] = piece
+        out_ref[2 * b + 1, TILE:base_w, :] = piece
+        return carry
+
+    lax.fori_loop(0, tiles // 2, finish_queries, 0)
+
+
+def unpack_kernel(
+    half_ref, got_ref, wk_ref, wq_ref, dq_ref, dk_ref, dv_ref, dwq_ref, dwk_ref, rel_ref,
+):
+    heads = got_ref.shape[0] // 2
+    w_rows = dwk_ref.shape[0]
+    base_w = TILE + TILE // 2
+    base_b = base_w + w_rows
+    half = half_ref[0]
+    keys_low, queries_low = [], []
+    for g in range(heads // 2):
+        cols = slice(2 * g * HD, 2 * (g + 1) * HD)
+        sums, weights, grads = [], [], []
+        for head in (2 * g, 2 * g + 1):
+            two = got_ref[2 * head, 0:TILE, :].astype(F32) + got_ref[2 * head + 1, 0:TILE, :].astype(F32)
+            sums.append(two.astype(BF))
+            rest = got_ref[2 * head, base_w:, :].astype(F32) + got_ref[2 * head + 1, base_w:, :].astype(F32)
+            weights.append(rest)
+            piece = got_ref[2 * head + half, TILE:base_w, :]
+            grads.append(jnp.concatenate([piece[:, :HD], piece[:, HD:]], 0))
+        dq_ref[:, cols] = jnp.concatenate(grads, 1)
+        dk_ref[:, cols] = jnp.concatenate([part[:, :HD] for part in sums], 1)
+        dv_ref[:, cols] = jnp.concatenate([part[:, HD:] for part in sums], 1)
+        dwk_ref[:, cols] = jnp.concatenate([part[:w_rows, :HD] for part in weights], 1)
+        dwq_ref[:, cols] = jnp.concatenate([part[:w_rows, HD:] for part in weights], 1)
+        keys_low += [part[w_rows:, :HD].astype(BF) for part in weights]
+        queries_low += [part[w_rows:, HD:].astype(BF) for part in weights]
+    rel = nt(jnp.concatenate(keys_low, 1), wk_ref[...]) + nt(
+        jnp.concatenate(queries_low, 1), wq_ref[...]
+    )
+    rel_ref[...] = rel.astype(BF)
+
+
+def whole_call(kernel, inputs, outputs, scratch=(), scalars=0, limit=48):
+    vmem = pl.BlockSpec(memory_space=pltpu.VMEM)
+    smem = pl.BlockSpec(memory_space=pltpu.SMEM)
+    return pl.pallas_call(
+        kernel,
+        out_shape=outputs,
+        in_specs=[smem] * scalars + [vmem] * (len(inputs) - scalars),
+        out_specs=jax.tree.map(lambda _: vmem, outputs),
+        scratch_shapes=list(scratch),
+        compiler_params=pltpu.CompilerParams(vmem_limit_bytes=limit << 20),
+    )(*inputs)
+
+
+def head_body(queries, keys, values, out_grad, rel_emb, w_query, w_key, doc_lengths, bucket_table):
+    tokens_dev, width = queries.shape
+    heads = width // HD
+    seq_count = lax.axis_size("seq")
+    seq_index = lax.axis_index("seq")
+    buckets, depth = rel_emb.shape
+    halo = bucket_table.shape[0] // 2 // TILE
+    span = 2 * halo + 1
+    mine = seq_index // 2
+    half = lax.rem(seq_index, 2).astype(jnp.int32).reshape(1)
+    shape = jax.ShapeDtypeStruct
+    packed = whole_call(
+        pack_kernel,
+        (queries, out_grad, keys, values),
+        shape((seq_count, tokens_dev, 4 * HD), BF),
+    )
+    arrived = lax.all_to_all(packed, "seq", 0, 0, tiled=True)
+    w_own = jnp.concatenate(
+        [
+            lax.dynamic_slice_in_dim(w_key, mine * HD, HD, 1),
+            lax.dynamic_slice_in_dim(w_query, mine * HD, HD, 1),
+        ],
+        1,
+    )
+    pos = nn(rel_emb, w_own).astype(BF)
+    table = jnp.flip(bucket_table).reshape(1, -1)
+    w_rows, b_rows = depth // seq_count, buckets // seq_count
+    rows = TILE + TILE // 2 + w_rows + b_rows
+    line = (2 * span - 1 + 1) * TILE
+    vm = pltpu.VMEM
+    results = whole_call(
+        head_kernel,
+        (doc_lengths, half, arrived, pos, table, rel_emb),
+        shape((seq_count, rows, 2 * HD), BF),
+        [
+            vm((buckets, table.shape[1]), BF),
+            vm((2 * HD, line), BF),
+            vm((2 * HD, line), BF),
+            vm((seq_count, TILE, 2 * HD), F32),
+            vm((seq_count, TILE, HD), F32),
+            vm((HD, line), F32),
+            vm((HD, line), F32),
+            vm((seq_count, 2 * HD, TILE), BF),
+            vm((seq_count, HD, TILE), BF),
+            vm((TILE, (span + 1) * TILE), F32),
+            vm((span, TILE, TILE), F32),
+            vm((span, TILE, TILE), F32),
+            vm((TILE, (span + 1) * TILE), BF),
+            vm((seq_count // 2, HD, TILE), F32),
+            vm((seq_count // 2, TILE, 2 * HD), BF),
+        ],
+        scalars=2,
+    )
+    returned = lax.all_to_all(results, "seq", 0, 0, tiled=True)
+    tokens = shape((tokens_dev, width), BF)
+    weights = shape((w_rows, width), F32)
+    query_grad, key_grad, value_grad, w_query_grad, w_key_grad, rel_rows = whole_call(
+        unpack_kernel,
+        (half, returned, w_key, w_query),
+        [tokens, tokens, tokens, weights, weights, shape((b_rows, depth), BF)],
+        scalars=1,
+    )
+    head_index = lax.axis_index("head")
+    kept = lax.dynamic_slice_in_dim(rel_rows, head_index * width, width, 1)
+    other = lax.dynamic_slice_in_dim(rel_rows, (1 - head_index) * width, width, 1)
+    other = lax.ppermute(other, "head", [(0, 1), (1, 0)])
+    rel_own = (kept.astype(F32) + other.astype(F32)).astype(BF)
+    rel_emb_grad = lax.all_gather(rel_own, "seq", axis=0, tiled=True).astype(F32)
+    return (query_grad, key_grad, value_grad, rel_emb_grad, w_query_grad, w_key_grad)
+
+
+def fits_heads(mesh, queries, rel_emb, bucket_table):
+    seq, head = mesh.shape["seq"], mesh.shape["head"]
+    heads = queries.shape[1] // HD // head
+    return (
+        head == 2
+        and seq == 2 * heads
+        and heads % 2 == 0
+        and queries.shape[0] == seq * TILE
+        and bucket_table.shape[0] % (2 * TILE) == 0
+        and seq >= bucket_table.shape[0] // TILE + 1
+        and rel_emb.shape[0] % (16 * seq) == 0
+        and rel_emb.shape[1] % (16 * seq) == 0
+        and rel_emb.shape[0] % TILE == 0
+    )
+
+
 def solution(mesh):
     in_specs = (
         P("seq", "head"),
@@ -253,4 +602,11 @@
         P("seq", "head"),
         P("seq", "head"),
     )
-    return jax.shard_map(body, mesh=mesh, in_specs=in_specs, out_specs=out_specs, check_vma=False)
+
+    def run(queries, keys, values, out_grad, rel_emb, w_query, w_key, doc_lengths, bucket_table):
+        chosen = head_body if fits_heads(mesh, queries, rel_emb, bucket_table) else body
+        return jax.shard_map(
+            chosen, mesh=mesh, in_specs=in_specs, out_specs=out_specs, check_vma=False
+        )(queries, keys, values, out_grad, rel_emb, w_query, w_key, doc_lengths, bucket_table)
+
+    return run

time: 834 us -> 140 us (0.17); the launches traced: 825 us -> 140 us
  matrix products: 349 us -> 0.51 us
  local copies, waits for them, and re-layouts: 233 us -> 4.88 us
  starting transfers between devices: 72.5 us -> 16 us
  blocking collectives: 75.1 us -> 24.6 us
  Pallas kernels: 0 us -> 43.4 us
  loops' own time: 17 us -> 0 us
  between operations: 15 us -> 0.73 us
  other arithmetic: 14 us -> 1.11 us
    dot_general x428 -> x1, matrix products: 346 us -> 0.51 us  [contract(): lax.dot_general(left, right, (((left_dim,), (right_dim,)), ((), ())), pre...]
    reshape x434 -> x0, local copies, waits for them, and re-layouts: 111 us -> none  [the longest x144 48.1 us: skew_in(): return flat[rows - 1:rows - 1 + rows * line].reshape(rows, line)[:, :width]]
    psum x1 -> x0, blocking collectives: 75.1 us -> none  [body(): summed = lax.psum((join_heads(bucket_key), join_heads(bucket_query)), 'seq')]
    ppermute x32 -> x1, starting transfers between devices: 72.5 us -> 1.5 us  [head_body(): other = lax.ppermute(other, 'head', [(0, 1), (1, 0)])]
    while x1216 -> x0, local copies, waits for them, and re-layouts: 48 us -> none
    all_to_all x0 -> x2, waiting for transfers between devices: none -> 46.3 us  [the longest x1 25.1 us: head_body(): returned = lax.all_to_all(results, 'seq', 0, 0, tiled=True)]
    ppermute x32 -> x1, waiting for transfers between devices: 48.8 us -> 2.57 us  [head_body(): other = lax.ppermute(other, 'head', [(0, 1), (1, 0)])]
    pallas_call x0 -> x3, Pallas kernels: none -> 43.4 us  [whole_call(): pl.pallas_call(kernel, out_shape=outputs, in_specs=[smem] * scalars + [vm...]
  transfers between devices with their start and end apart: 33 -> 3, of which waited for: 10 -> 3; matrix products, arithmetic and copies ran while one was open for 5% -> 1% of each run, Pallas kernels for 0% -> 0%
where the time goes in v1:
time: 140 us
  waiting for transfers between devices  48.8 us (35%)
  Pallas kernels  43.4 us (31%)
  blocking collectives  24.6 us (18%)
  starting transfers between devices  16 us (11%)
  local copies, waits for them, and re-layouts  4.88 us (3%)
    pallas_call x3, Pallas kernels, whole_call(): pl.pallas_call(kernel, out_shape=outputs, in_specs=[smem] * scalars + [vm...  43.4 us
    all_to_all x1, waiting for transfers between devices, head_body(): returned = lax.all_to_all(results, 'seq', 0, 0, tiled=True)  25.1 us
    all_gather x1, blocking collectives, head_body(): lax.all_gather(rel_own, 'seq', axis=0, tiled=True).astype(F32)  24.6 us
    all_to_all x1, waiting for transfers between devices, head_body(): arrived = lax.all_to_all(packed, 'seq', 0, 0, tiled=True)  21.1 us
    all_to_all x1, starting transfers between devices, head_body(): arrived = lax.all_to_all(packed, 'seq', 0, 0, tiled=True)  7.52 us
    all_to_all x1, starting transfers between devices, head_body(): returned = lax.all_to_all(results, 'seq', 0, 0, tiled=True)  6.99 us
    unnamed x18, local copies, waits for them, and re-layouts  3.63 us
  transfers between devices with their start and end apart: 3, of which 3 were waited for; matrix products, arithmetic and copies ran while one was open for 1% of the time, Pallas kernels for 0%

profile of v1, /device:TPU:0, one launch (start us, length us, event | category | flops | bytes accessed | tf_op | source)
XLA Modules:
  0.0 140.0 jit_solution(11685500143755053186)
XLA Ops:
  0.6 0.0 copy-start.3
  0.6 0.9 copy-done.3
  1.5 0.9 copy-done.4
  2.4 0.9 copy-done.5
  3.3 0.9 copy-done.6
  4.3 1.2 shard_map.136
  5.4 7.5 %all-to-all-start = ((bf16[16,128,256]{2,1,0:T(8,128)(2,1)}), bf16[16,128,256]{2,1,0:T(8,128)(2,1)S(1)}, u32[]{:S(2)}, u32[]{:S(2)}) async-start(bf16[16,128,256]{2,1,0:T(8,128)(2,1)} %shard_map.136), calls=%async_computation | async-start | bytes 2097152 | tf_op jit(solution)/shard_map/all_to_all | solution.py:514
  13.0 0.0 copy-done.8
  13.0 0.1 rev.4
  13.1 0.0 copy-done.1
  13.1 1.2 constant_dynamic-slice_fusion.1
  14.2 0.0 copy-done
  14.3 0.5 fusion.pos_ref
  14.8 21.1 %all-to-all-done.all_ref = bf16[16,128,256]{2,1,0:T(8,128)(2,1)S(1)} async-done(((bf16[16,128,256]{2,1,0:T(8,128)(2,1)}), bf16[16,128,256]{2,1,0:T(8,128)(2,1)S(1)}, u32[]{:S(2)}, u32[]{:S(2)}) %all-to-all-start) | async-done | bytes 1048608 | tf_op jit(solution)/shard_map/all_to_all | solution.py:514
  35.9 0.0 copy-done.7
  35.9 40.7 %shard_map.137 = bf16[16,288,128]{2,1,0:T(8,128)(2,1)} custom-call(s32[8]{0:T(128)S(1)} %copy-done.7, s32[1]{0:T(128)} %bitcast.half_ref, bf16[16,128,256]{2,1,0:T(8,128)(2,1)S(1)} %all-to-all-done.all_ref, bf16[512,128]{1,0:T(8,128)(2,1)S(1)} %fusion.pos_ref, s32[1,1024]{1,0:T(1,128)S(1)} %bitcast.5, bf16[512,1024]{1,0:T(8,128)(2,1)S(1)} %copy-done), custom_call_target="tpu_custom_call" | custom-call | tf_op jit(solution)/shard_map/pallas_call | solution.py:488
  76.6 7.0 %all-to-all-start.1 = ((bf16[16,288,128]{2,1,0:T(8,128)(2,1)}), bf16[16,288,128]{2,1,0:T(8,128)(2,1)S(1)}, u32[]{:S(2)}, u32[]{:S(2)}) async-start(bf16[16,288,128]{2,1,0:T(8,128)(2,1)} %shard_map.137), calls=%async_computation.1 | async-start | bytes 2359296 | tf_op jit(solution)/shard_map/all_to_all | solution.py:551
  83.6 25.1 %all-to-all-done.1.got_ref = bf16[16,288,128]{2,1,0:T(8,128)(2,1)S(1)} async-done(((bf16[16,288,128]{2,1,0:T(8,128)(2,1)}), bf16[16,288,128]{2,1,0:T(8,128)(2,1)S(1)}, u32[]{:S(2)}, u32[]{:S(2)}) %all-to-all-start.1) | async-done | bytes 1179680 | tf_op jit(solution)/shard_map/all_to_all | solution.py:551
  108.8 0.0 copy-done.2
  108.8 1.5 %shard_map.138 = (bf16[128,512]{1,0:T(8,128)(2,1)}, bf16[128,512]{1,0:T(8,128)(2,1)}, bf16[128,512]{1,0:T(8,128)(2,1)}, f32[64,512]{1,0:T(8,128)}, f32[64,512]{1,0:T(8,128)}, /*index=5*/bf16[32,1024]{1,0:T(8,128)(2,1)S(1)}) custom-call(s32[1]{0:T(128)} %bitcast.half_ref, bf16[16,288,128]{2,1,0:T(8,128)(2,1)S(1)} %all-to-all-done.1.got_ref, ...), custom_call_target="tpu_custom_call" | custom-call | tf_op jit(solution)/shard_map/pallas_call | solution.py:488
  110.2 1.5 %collective-permute-start = (bf16[32,512]{1,0:T(8,128)(2,1)S(1)}, bf16[32,512]{1,0:T(8,128)(2,1)S(1)}, u32[]{:S(2)}, u32[]{:S(2)}) collective-permute-start(bf16[32,512]{1,0:T(8,128)(2,1)S(1)} %constant_dynamic-slice_fusion), channel_id=1, source_target_pairs={{0,1},{1,0},{2,3},{3,2},{4,5},{5,4},{6,7},{7,6},{8,9},{9,8},{10,11... | collective-permute-start | bytes 98312 | tf_op jit(solution)/shard_map/ppermute | solution.py:563
  111.7 2.6 %collective-permute-done = bf16[32,512]{1,0:T(8,128)(2,1)S(1)} collective-permute-done((bf16[32,512]{1,0:T(8,128)(2,1)S(1)}, bf16[32,512]{1,0:T(8,128)(2,1)S(1)}, u32[]{:S(2)}, u32[]{:S(2)}) %collective-permute-start) | collective-permute-done | bytes 32800 | tf_op jit(solution)/shard_map/ppermute | solution.py:563
  114.3 24.6 %all_gather.3 = bf16[512,512]{1,0:T(8,128)(2,1)S(1)} all-gather(bf16[32,512]{1,0:T(8,128)(2,1)S(1)} %add_convert_fusion), channel_id=1, replica_groups=mesh['seq'=16,'head'=2] {'seq'}, dimensions={0}, use_global_device_ids=true | all-gather | bytes 557056 | tf_op jit(solution)/shard_map/all_gather | solution.py:565
  138.9 1.1 convert_element_type.22
  (10 shorter events, 0.0 us)
Async XLA Ops:
  0.6 0.9 copy-start.3
  1.5 0.9 copy-start.4
  2.4 0.9 copy-start.5
  3.3 0.9 copy-start.6
  5.4 7.6 %copy-start.8 = (s32[1024]{0:T(1024)S(1)}, s32[1024]{0:T(1024)}, u32[]{:S(2)}) copy-start(s32[1024]{0:T(1024)} %param.17) | copy-start | bytes 12292
  5.4 7.6 %copy-start.1 = (bf16[1024,512]{1,0:T(8,128)(2,1)S(1)}, bf16[1024,512]{1,0:T(8,128)(2,1)}, u32[]{:S(2)}) copy-start(bf16[1024,512]{1,0:T(8,128)(2,1)} %wq_ref.1) | copy-start | bytes 3145732
  5.4 8.8 %copy-start = (bf16[512,1024]{1,0:T(8,128)(2,1)S(1)}, bf16[512,1024]{1,0:T(8,128)(2,1)}, u32[]{:S(2)}) copy-start(bf16[512,1024]{1,0:T(8,128)(2,1)} %rel_ref.1) | copy-start | bytes 3145732
  5.4 30.5 %all-to-all-start = ((bf16[16,128,256]{2,1,0:T(8,128)(2,1)}), bf16[16,128,256]{2,1,0:T(8,128)(2,1)S(1)}, u32[]{:S(2)}, u32[]{:S(2)}) async-start(bf16[16,128,256]{2,1,0:T(8,128)(2,1)} %shard_map.136), calls=%async_computation | async-start | bytes 2097152 | tf_op jit(solution)/shard_map/all_to_all | solution.py:514
  13.1 22.8 %copy-start.7 = (s32[8]{0:T(128)S(1)}, s32[8]{0:T(128)}, u32[]{:S(2)}) copy-start(s32[8]{0:T(128)} %lens_ref.1) | copy-start | bytes 100
  76.6 32.1 %copy-start.2 = (bf16[1024,512]{1,0:T(8,128)(2,1)S(1)}, bf16[1024,512]{1,0:T(8,128)(2,1)}, u32[]{:S(2)}) copy-start(bf16[1024,512]{1,0:T(8,128)(2,1)} %wk_ref.1) | copy-start | bytes 3145732
  76.6 32.1 %all-to-all-start.1 = ((bf16[16,288,128]{2,1,0:T(8,128)(2,1)}), bf16[16,288,128]{2,1,0:T(8,128)(2,1)S(1)}, u32[]{:S(2)}, u32[]{:S(2)}) async-start(bf16[16,288,128]{2,1,0:T(8,128)(2,1)} %shard_map.137), calls=%async_computation.1 | async-start | bytes 2359296 | tf_op jit(solution)/shard_map/all_to_all | solution.py:551
  110.2 4.1 %collective-permute-start = (bf16[32,512]{1,0:T(8,128)(2,1)S(1)}, bf16[32,512]{1,0:T(8,128)(2,1)S(1)}, u32[]{:S(2)}, u32[]{:S(2)}) collective-permute-start(bf16[32,512]{1,0:T(8,128)(2,1)S(1)} %constant_dynamic-slice_fusion), channel_id=1, source_target_pairs={{0,1},{1,0},{2,3},{3,2},{4,5},{5,4},{6,7},{7,6},{8,9},{9,8},{10,11... | collective-permute-start | bytes 98312 | tf_op jit(solution)/shard_map/ppermute | solution.py:563

commit v2 on v1

--- a/solution.py
+++ b/solution.py
@@ -10,6 +10,7 @@
 HD = 64
 SPAN = 4
 TILE = 128
+SPANS = (3, 5, 7)
 BF = jnp.bfloat16
 F32 = jnp.float32
 
@@ -254,33 +255,16 @@
 
 
 def pack_kernel(q_ref, g_ref, k_ref, v_ref, out_ref):
-    for head in range(out_ref.shape[0] // 2):
+    for head in range(out_ref.shape[0]):
         cols = slice(head * HD, (head + 1) * HD)
-        piece = jnp.concatenate(
+        out_ref[head] = jnp.concatenate(
             [q_ref[:, cols], g_ref[:, cols], k_ref[:, cols], v_ref[:, cols]], 1
         )
-        out_ref[2 * head] = piece
-        out_ref[2 * head + 1] = piece
-
-
-def head_kernel(
-    lens_ref, half_ref, all_ref, pos_ref, table_ref, rel_ref, out_ref,
-    onehot, pk, pq, acc, acc_pos, g_key, g_query, k_t, k_rev, s_q, st, dp, dtile, dq_nat, dq_pos,
-):
-    tiles = all_ref.shape[0]
-    halo = table_ref.shape[1] // 2 // TILE
-    span = 2 * halo + 1
-    scale = 1.0 / math.sqrt(3.0 * HD)
-    valid0 = (halo + 1) * TILE
-    valid = table_ref.shape[1]
-    buckets = pos_ref.shape[0]
-    half = half_ref[0]
-    row, col = grid_of((TILE, TILE))
-    swap = jnp.where(row + col == TILE - 1, 1.0, 0.0).astype(BF)
-    wrap = row + col >= TILE - 1
-    wrap_rev = col >= row
-    low = col < HD
-
+
+
+def table_kernel(pos_ref, table_ref, onehot, pk, pq):
+    buckets, valid = onehot.shape
+    valid0 = valid // 2 + TILE
     for part in range(buckets // TILE):
         ids = lax.broadcasted_iota(jnp.int32, (TILE, valid), 0) + part * TILE
         onehot[pl.ds(part * TILE, TILE), :] = jnp.where(ids == table_ref[...], 1.0, 0.0).astype(BF)
@@ -290,24 +274,73 @@
     pq[...] = jnp.zeros_like(pq)
     pk[0:HD, valid0 : valid0 + valid] = expanded[:HD]
     pq[0:HD, valid0 : valid0 + valid] = expanded[HD:]
+
+
+def head_kernel(
+    lens_ref, half_ref, own_ref, other_ref, onehot, pk, pq,
+    send_ref, keep_ref, bucket_ref, query_ref,
+    kvs, acc, acc_pos, g_key, g_query, k_t, k_rev, s_q, st, dp, dtile, dq_nat, dq_pos,
+):
+    blocks = own_ref.shape[0]
+    tiles = 2 * blocks
+    buckets, valid = onehot.shape
+    halo = valid // 2 // TILE
+    longest = 2 * halo + 1
+    scale = 1.0 / math.sqrt(3.0 * HD)
+    valid0 = (halo + 1) * TILE
+    half = half_ref[0]
+    row, col = grid_of((TILE, TILE))
+    swap = jnp.where(row + col == TILE - 1, 1.0, 0.0).astype(BF)
+    wrap = row + col >= TILE - 1
+    wrap_rev = col >= row
+    low = col < HD
     acc[...] = jnp.zeros_like(acc)
     acc_pos[...] = jnp.zeros_like(acc_pos)
     g_key[...] = jnp.zeros_like(g_key)
     g_query[...] = jnp.zeros_like(g_query)
 
-    def transpose_tile(tile, carry):
-        turned = all_ref[tile, :, 2 * HD : 4 * HD].astype(F32).T.astype(BF)
-        k_t[tile] = turned
-        k_rev[tile] = nn(turned[:HD], swap).astype(BF)
+    def transpose_tile(b, carry):
+        for ref, tile in ((own_ref, 2 * b + half), (other_ref, 2 * b + 1 - half)):
+            kv = ref[b, :, 2 * HD : 4 * HD]
+            kvs[tile] = kv
+            turned = kv.astype(F32).T.astype(BF)
+            k_t[tile] = turned[:HD]
+            k_rev[tile] = nn(turned[:HD], swap).astype(BF)
         return carry
 
-    lax.fori_loop(0, tiles, transpose_tile, 0)
+    lax.fori_loop(0, blocks, transpose_tile, 0)
 
     def block(b, carry):
         own = 2 * b + half
-        first = jnp.clip(own - halo, 0, tiles - span)
+        token = own * TILE
+
+        def next_end(d, state):
+            end, start, stop = state
+            stop = jnp.where(end < token + TILE, end + lens_ref[d], stop)
+            end = end + lens_ref[d]
+            start = jnp.where(end <= token, end, start)
+            return (end, start, stop)
+
+        zero = jnp.int32(0)
+        _, reach_low, reach_high = lax.fori_loop(
+            0, lens_ref.shape[0], next_end, (zero, zero, zero)
+        )
+        lowest = reach_low // TILE
+        count = (reach_high + TILE - 1) // TILE - lowest
+        shorter = 0
+        for span in SPANS:
+            if span < longest:
+                pl.when((count > shorter) & (count <= span))(
+                    lambda span=span: work(b, own, lowest, span)
+                )
+                shorter = span
+        pl.when(count > shorter)(lambda: work(b, own, lowest, longest))
+        return carry
+
+    def work(b, own, lowest, span):
+        first = jnp.clip(lowest, 0, tiles - span)
         delta = (own - first) * TILE
-        qd = all_ref[own, :, 0 : 2 * HD]
+        qd = own_ref[b, :, 0 : 2 * HD]
         turned = qd.astype(F32).T
         upper = row < HD
         right = jnp.concatenate(
@@ -319,25 +352,23 @@
 
         def next_doc(d, state):
             end, start, stop = state
+            stop = jnp.where(end <= position, end + lens_ref[d], stop)
             end = end + lens_ref[d]
             start = jnp.where(end <= position, end, start)
-            stop = jnp.where((end > position) & (stop < 0), end, stop)
             return (end, start, stop)
 
+        nothing = jnp.zeros((1, TILE), jnp.int32)
         _, start, stop = lax.fori_loop(
-            0,
-            lens_ref.shape[0],
-            next_doc,
-            (jnp.int32(0), jnp.zeros((1, TILE), jnp.int32), jnp.full((1, TILE), -1, jnp.int32)),
+            0, lens_ref.shape[0], next_doc, (jnp.int32(0), nothing, nothing)
         )
         start = start - first * TILE
         stop = stop - first * TILE
 
         key_x = pl.multiple_of(halo * 2 * TILE - delta, TILE)
-        s_q[...] = nn(qd, pk[:, pl.ds(key_x, (span + 1) * TILE)])
+        s_q[:, 0 : (span + 1) * TILE] = nn(qd, pk[:, pl.ds(key_x, (span + 1) * TILE)])
         best = jnp.full((8, TILE), masked_score, F32)
         for t in range(span):
-            kv = all_ref[first + t, :, 2 * HD : 4 * HD]
+            kv = kvs[first + t]
             both = nn(kv, right)
             query_x = pl.multiple_of(2 * halo * TILE + delta - t * TILE, TILE)
             s_k = nn(kv, pq[:, pl.ds(query_x, 2 * TILE)])
@@ -382,7 +413,7 @@
             query_x = pl.multiple_of(2 * halo * TILE + delta - t * TILE, TILE)
             lhs = jnp.concatenate([dscore, prob.astype(BF)], 1)
             acc[first + t] += nn(lhs, pair)
-            stacked = nn(jnp.concatenate([k_t[first + t][:HD], swap], 0), dscore)
+            stacked = nn(jnp.concatenate([k_t[first + t], swap], 0), dscore)
             dq_t = dq_t + stacked[:HD]
             y = pltpu.roll(stacked[HD:], 0, 1, stride=1, stride_axis=0)
             spread = jnp.concatenate(
@@ -393,17 +424,16 @@
             z = pltpu.roll(nt(swap, dscore), 0, 1, stride=1, stride_axis=0)
             dtile[:, t * TILE : (t + 1) * TILE] = jnp.where(wrap_rev, z, before).astype(BF)
             before = z
-        dtile[:, span * TILE :] = jnp.where(wrap_rev, 0.0, before).astype(BF)
-        spread_q = dtile[...]
+        dtile[:, span * TILE : (span + 1) * TILE] = jnp.where(wrap_rev, 0.0, before).astype(BF)
+        spread_q = dtile[:, 0 : (span + 1) * TILE]
         window = pl.ds(key_x, (span + 1) * TILE)
         g_key[:, window] += nn(q_rev, spread_q)
         back = nt(spread_q, pk[0:HD, window])
         high = back.astype(BF)
         dq_pos[b] = jnp.concatenate([high, (back - high.astype(F32)).astype(BF)], 1)
         dq_nat[b] = dq_t
-        return carry
-
-    lax.fori_loop(0, tiles // 2, block, 0)
+
+    lax.fori_loop(0, blocks, block, 0)
 
     parts = []
     for g in (g_key, g_query):
@@ -414,68 +444,74 @@
     bucket_t = scale * jnp.concatenate(
         [summed[:HD] + summed[HD : 2 * HD], summed[2 * HD : 3 * HD] + summed[3 * HD :]], 0
     )
-    bucket_low = bucket_t.astype(BF)
-    weight_t = nn(bucket_low, rel_ref[...])
-    w_rows = rel_ref.shape[1] // tiles
-    b_rows = buckets // tiles
-    weight = weight_t.T.astype(BF)
     bucket = bucket_t.T.astype(BF)
-    base_w = TILE + TILE // 2
-    base_b = base_w + w_rows
-    for tile in range(tiles):
-        out_ref[tile, base_w:base_b, :] = weight[tile * w_rows : (tile + 1) * w_rows]
-        out_ref[tile, base_b : base_b + b_rows, :] = bucket[tile * b_rows : (tile + 1) * b_rows]
+    bucket_ref[...] = bucket
+    send_ref[blocks * TILE :, :] = bucket
     factor = jnp.where(low, scale, 1.0)
 
-    def finish_keys(tile, carry):
+    def gradients(tile):
         back = acc_pos[tile]
         high = back.astype(BF)
         both = nn(swap, jnp.concatenate([high, (back - high.astype(F32)).astype(BF)], 1))
         extra = both[:, :HD] + both[:, HD:]
         extra = jnp.concatenate([extra, jnp.zeros_like(extra)], 1)
-        out_ref[tile, 0:TILE, :] = ((acc[tile] + extra) * factor).astype(BF)
-        return carry
-
-    lax.fori_loop(0, tiles, finish_keys, 0)
-
-    def finish_queries(b, carry):
+        return (acc[tile] + extra) * factor
+
+    def finish(b, carry):
+        keep_ref[b] = gradients(2 * b + half)
+        send_ref[pl.ds(b * TILE, TILE), :] = gradients(2 * b + 1 - half).astype(BF)
         both = nn(swap, dq_pos[b])
         extra = both[:, :HD] + both[:, HD:]
         grad = scale * (dq_nat[b].T + extra)
-        piece = jnp.concatenate([grad[: TILE // 2], grad[TILE // 2 :]], 1).astype(BF)
-        out_ref[2 * b, TILE:base_w, :] = piece
-        out_ref[2 * b + 1, TILE:base_w, :] = piece
+        query_ref[b] = jnp.concatenate([grad[: TILE // 2], grad[TILE // 2 :]], 1).astype(BF)
         return carry
 
-    lax.fori_loop(0, tiles // 2, finish_queries, 0)
+    lax.fori_loop(0, blocks, finish, 0)
+
+
+def join_kernel(half_ref, keep_ref, bucket_ref, query_ref, came_ref, rel_ref, out_ref, weight, bucket):
+    blocks = keep_ref.shape[0]
+    tiles = 2 * blocks
+    half = half_ref[0]
+    w_rows = weight.shape[0] // tiles
+    b_rows = bucket.shape[0] // tiles
+    base_w = TILE + TILE // 2
+    base_b = base_w + w_rows
+    total = bucket_ref[...].astype(F32) + came_ref[blocks * TILE :, :].astype(F32)
+    bucket[...] = total
+    weight[...] = nn(total.T.astype(BF), rel_ref[...]).T
+    for b in range(blocks):
+        came = came_ref[b * TILE : (b + 1) * TILE, :].astype(F32)
+        tile = 2 * b + half
+        out_ref[b, 0:TILE, :] = (keep_ref[b] + came).astype(BF)
+        out_ref[b, TILE:base_w, :] = query_ref[b]
+        out_ref[b, base_w:base_b, :] = weight[pl.ds(tile * w_rows, w_rows), :].astype(BF)
+        out_ref[b, base_b:, :] = bucket[pl.ds(tile * b_rows, b_rows), :].astype(BF)
 
 
 def unpack_kernel(
-    half_ref, got_ref, wk_ref, wq_ref, dq_ref, dk_ref, dv_ref, dwq_ref, dwk_ref, rel_ref,
+    got_ref, wk_ref, wq_ref, dq_ref, dk_ref, dv_ref, dwq_ref, dwk_ref, rel_ref,
 ):
-    heads = got_ref.shape[0] // 2
     w_rows = dwk_ref.shape[0]
     base_w = TILE + TILE // 2
     base_b = base_w + w_rows
-    half = half_ref[0]
     keys_low, queries_low = [], []
-    for g in range(heads // 2):
+    for g in range(got_ref.shape[0] // 2):
         cols = slice(2 * g * HD, 2 * (g + 1) * HD)
-        sums, weights, grads = [], [], []
-        for head in (2 * g, 2 * g + 1):
-            two = got_ref[2 * head, 0:TILE, :].astype(F32) + got_ref[2 * head + 1, 0:TILE, :].astype(F32)
-            sums.append(two.astype(BF))
-            rest = got_ref[2 * head, base_w:, :].astype(F32) + got_ref[2 * head + 1, base_w:, :].astype(F32)
-            weights.append(rest)
-            piece = got_ref[2 * head + half, TILE:base_w, :]
-            grads.append(jnp.concatenate([piece[:, :HD], piece[:, HD:]], 0))
-        dq_ref[:, cols] = jnp.concatenate(grads, 1)
-        dk_ref[:, cols] = jnp.concatenate([part[:, :HD] for part in sums], 1)
-        dv_ref[:, cols] = jnp.concatenate([part[:, HD:] for part in sums], 1)
-        dwk_ref[:, cols] = jnp.concatenate([part[:w_rows, :HD] for part in weights], 1)
-        dwq_ref[:, cols] = jnp.concatenate([part[:w_rows, HD:] for part in weights], 1)
-        keys_low += [part[w_rows:, :HD].astype(BF) for part in weights]
-        queries_low += [part[w_rows:, HD:].astype(BF) for part in weights]
+        two = [got_ref[2 * g], got_ref[2 * g + 1]]
+        dq_ref[:, cols] = jnp.concatenate(
+            [
+                jnp.concatenate([one[TILE:base_w, :HD], one[TILE:base_w, HD:]], 0)
+                for one in two
+            ],
+            1,
+        )
+        dk_ref[:, cols] = jnp.concatenate([one[:TILE, :HD] for one in two], 1)
+        dv_ref[:, cols] = jnp.concatenate([one[:TILE, HD:] for one in two], 1)
+        dwk_ref[:, cols] = jnp.concatenate([one[base_w:base_b, :HD] for one in two], 1).astype(F32)
+        dwq_ref[:, cols] = jnp.concatenate([one[base_w:base_b, HD:] for one in two], 1).astype(F32)
+        keys_low += [one[base_b:, :HD] for one in two]
+        queries_low += [one[base_b:, HD:] for one in two]
     rel = nt(jnp.concatenate(keys_low, 1), wk_ref[...]) + nt(
         jnp.concatenate(queries_low, 1), wq_ref[...]
     )
@@ -495,6 +531,20 @@
     )(*inputs)
 
 
+def staged_call(kernel, inputs, outputs):
+    def spec(array):
+        return pl.BlockSpec(array.shape, lambda step: (0,) * len(array.shape))
+
+    return pl.pallas_call(
+        kernel,
+        grid=(1,),
+        out_shape=outputs,
+        in_specs=[spec(array) for array in inputs],
+        out_specs=jax.tree.map(spec, outputs),
+        compiler_params=pltpu.CompilerParams(vmem_limit_bytes=32 << 20),
+    )(*inputs)
+
+
 def head_body(queries, keys, values, out_grad, rel_emb, w_query, w_key, doc_lengths, bucket_table):
     tokens_dev, width = queries.shape
     heads = width // HD
@@ -505,13 +555,21 @@
     span = 2 * halo + 1
     mine = seq_index // 2
     half = lax.rem(seq_index, 2).astype(jnp.int32).reshape(1)
+    halves = [list(range(0, seq_count, 2)), list(range(1, seq_count, 2))]
+    partners = [(i, i ^ 1) for i in range(seq_count)]
     shape = jax.ShapeDtypeStruct
-    packed = whole_call(
+    vm = pltpu.VMEM
+
+    def spread(pieces):
+        return lax.all_to_all(pieces, "seq", 0, 0, axis_index_groups=halves, tiled=True)
+
+    packed = staged_call(
         pack_kernel,
         (queries, out_grad, keys, values),
-        shape((seq_count, tokens_dev, 4 * HD), BF),
-    )
-    arrived = lax.all_to_all(packed, "seq", 0, 0, tiled=True)
+        shape((heads, tokens_dev, 4 * HD), BF),
+    )
+    own = spread(packed)
+    other = lax.ppermute(own, "seq", partners)
     w_own = jnp.concatenate(
         [
             lax.dynamic_slice_in_dim(w_key, mine * HD, HD, 1),
@@ -523,46 +581,68 @@
     table = jnp.flip(bucket_table).reshape(1, -1)
     w_rows, b_rows = depth // seq_count, buckets // seq_count
     rows = TILE + TILE // 2 + w_rows + b_rows
-    line = (2 * span - 1 + 1) * TILE
-    vm = pltpu.VMEM
-    results = whole_call(
+    line = 2 * span * TILE
+    tables = whole_call(
+        table_kernel,
+        (pos, table),
+        [
+            shape((buckets, table.shape[1]), BF),
+            shape((2 * HD, line), BF),
+            shape((2 * HD, line), BF),
+        ],
+    )
+    sent, kept, bucket, query = whole_call(
         head_kernel,
-        (doc_lengths, half, arrived, pos, table, rel_emb),
-        shape((seq_count, rows, 2 * HD), BF),
+        (doc_lengths, half, own, other, *tables),
         [
-            vm((buckets, table.shape[1]), BF),
-            vm((2 * HD, line), BF),
-            vm((2 * HD, line), BF),
+            shape((heads * TILE + buckets, 2 * HD), BF),
+            shape((heads, TILE, 2 * HD), F32),
+            shape((buckets, 2 * HD), BF),
+            shape((heads, TILE // 2, 2 * HD), BF),
+        ],
+        [
+            vm((seq_count, TILE, 2 * HD), BF),
             vm((seq_count, TILE, 2 * HD), F32),
             vm((seq_count, TILE, HD), F32),
             vm((HD, line), F32),
             vm((HD, line), F32),
-            vm((seq_count, 2 * HD, TILE), BF),
+            vm((seq_count, HD, TILE), BF),
             vm((seq_count, HD, TILE), BF),
             vm((TILE, (span + 1) * TILE), F32),
             vm((span, TILE, TILE), F32),
             vm((span, TILE, TILE), F32),
             vm((TILE, (span + 1) * TILE), BF),
-            vm((seq_count // 2, HD, TILE), F32),
-            vm((seq_count // 2, TILE, 2 * HD), BF),
+            vm((heads, HD, TILE), F32),
+            vm((heads, TILE, 2 * HD), BF),
         ],
         scalars=2,
     )
-    returned = lax.all_to_all(results, "seq", 0, 0, tiled=True)
+    came = lax.ppermute(sent, "seq", partners)
+    joined = whole_call(
+        join_kernel,
+        (half, kept, bucket, query, came, rel_emb),
+        shape((heads, rows, 2 * HD), BF),
+        [vm((depth, 2 * HD), F32), vm((buckets, 2 * HD), F32)],
+        scalars=1,
+    )
+    returned = spread(joined)
     tokens = shape((tokens_dev, width), BF)
     weights = shape((w_rows, width), F32)
     query_grad, key_grad, value_grad, w_query_grad, w_key_grad, rel_rows = whole_call(
         unpack_kernel,
-        (half, returned, w_key, w_query),
+        (returned, w_key, w_query),
         [tokens, tokens, tokens, weights, weights, shape((b_rows, depth), BF)],
-        scalars=1,
     )
     head_index = lax.axis_index("head")
-    kept = lax.dynamic_slice_in_dim(rel_rows, head_index * width, width, 1)
-    other = lax.dynamic_slice_in_dim(rel_rows, (1 - head_index) * width, width, 1)
-    other = lax.ppermute(other, "head", [(0, 1), (1, 0)])
-    rel_own = (kept.astype(F32) + other.astype(F32)).astype(BF)
-    rel_emb_grad = lax.all_gather(rel_own, "seq", axis=0, tiled=True).astype(F32)
+    mine_rel = lax.dynamic_slice_in_dim(rel_rows, head_index * width, width, 1)
+    far_rel = lax.dynamic_slice_in_dim(rel_rows, (1 - head_index) * width, width, 1)
+    far_rel = lax.ppermute(far_rel, "head", [(0, 1), (1, 0)])
+    rel_own = (mine_rel.astype(F32) + far_rel.astype(F32)).astype(BF)
+    near = spread(jnp.broadcast_to(rel_own[None], (heads, b_rows, width)))
+    far = lax.ppermute(near, "seq", partners)
+    even = jnp.where(half[0] == 0, near, far)
+    odd = jnp.where(half[0] == 0, far, near)
+    rel_emb_grad = jnp.stack([even, odd], 1).reshape(buckets, width).astype(F32)
     return (query_grad, key_grad, value_grad, rel_emb_grad, w_query_grad, w_key_grad)
 
 

time: 140 us -> 101 us (0.72); the launches traced: 140 us -> 99 us
  waiting for transfers between devices: 48.8 us -> 21.9 us
  Pallas kernels: 43.4 us -> 29.2 us
  starting transfers between devices: 16 us -> 5.8 us
  blocking collectives: 24.6 us -> 33.4 us
  local copies, waits for them, and re-layouts: 4.88 us -> 6.3 us
    all_to_all x0 -> x2, blocking collectives: none -> 33.4 us  [spread(): lax.all_to_all(pieces, 'seq', 0, 0, axis_index_groups=halves, tiled=True)]
    all_to_all x2 -> x1, waiting for transfers between devices: 46.3 us -> 16.6 us  [spread(): lax.all_to_all(pieces, 'seq', 0, 0, axis_index_groups=halves, tiled=True)]
    all_gather x1 -> x0, blocking collectives: 24.6 us -> none  [head_body(): lax.all_gather(rel_own, 'seq', axis=0, tiled=True).astype(F32)]
    pallas_call x3 -> x4, Pallas kernels: 43.4 us -> 29 us  [whole_call(): pl.pallas_call(kernel, out_shape=outputs, in_specs=[smem] * scalars + [vm...]
    all_to_all x2 -> x1, starting transfers between devices: 14.5 us -> 3.74 us  [spread(): lax.all_to_all(pieces, 'seq', 0, 0, axis_index_groups=halves, tiled=True)]
    ppermute x1 -> x4, waiting for transfers between devices: 2.57 us -> 5.3 us  [the longest x1 2.42 us: head_body(): far_rel = lax.ppermute(far_rel, 'head', [(0, 1), (1, 0)])]
    unnamed x18, local copies, waits for them, and re-layouts: 3.63 us -> 5.05 us
  transfers between devices with their start and end apart: 3 -> 5, of which waited for: 3 -> 4; matrix products, arithmetic and copies ran while one was open for 1% -> 2% of each run, Pallas kernels for 0% -> 0%
where the time goes in v2:
time: 101 us; the launch traced here: 99 us
  blocking collectives  33.4 us (33%)
  Pallas kernels  29.2 us (29%)
  waiting for transfers between devices  21.9 us (22%)
  local copies, waits for them, and re-layouts  6.3 us (6%)
  starting transfers between devices  5.8 us (6%)
  other arithmetic  1.24 us (1%)
    all_to_all x2, blocking collectives, spread(): lax.all_to_all(pieces, 'seq', 0, 0, axis_index_groups=halves, tiled=True)  33.4 us
    pallas_call x4, Pallas kernels, whole_call(): pl.pallas_call(kernel, out_shape=outputs, in_specs=[smem] * scalars + [vm...  29 us
    all_to_all x1, waiting for transfers between devices, spread(): lax.all_to_all(pieces, 'seq', 0, 0, axis_index_groups=halves, tiled=True)  16.6 us
    unnamed x18, local copies, waits for them, and re-layouts  5.05 us
    all_to_all x1, starting transfers between devices, spread(): lax.all_to_all(pieces, 'seq', 0, 0, axis_index_groups=halves, tiled=True)  3.74 us
    ppermute x1, waiting for transfers between devices, head_body(): far_rel = lax.ppermute(far_rel, 'head', [(0, 1), (1, 0)])  2.42 us
  transfers between devices with their start and end apart: 5, of which 4 were waited for; matrix products, arithmetic and copies ran while one was open for 2% of the time, Pallas kernels for 0%

profile of v2, /device:TPU:0, one launch (start us, length us, event | category | flops | bytes accessed | tf_op | source)
XLA Modules:
  0.0 99.0 jit_solution(5254651473054350696)
XLA Ops:
  0.7 1.0 copy-done.3
  1.6 0.9 copy-done.4
  2.5 0.9 copy-done.5
  3.4 0.9 copy-done.6
  4.3 0.2 shard_map.136
  4.6 21.7 %all_to_all.15.own_ref = bf16[8,128,256]{2,1,0:T(8,128)(2,1)S(1)} all-to-all(bf16[8,128,256]{2,1,0:T(8,128)(2,1)S(1)} %shard_map.136), channel_id=1, replica_groups={{0,4,8,12,16,20,24,28},{2,6,10,14,18,22,26,30},{1,5,9,13,17,21,25,29},{..., dimensions={0} | all-to-all | bytes 1048576 | tf_op jit(solution)/shard_map/all_to_all | solution.py:564
  26.3 0.7 copy-done.8
  27.0 0.1 rev.4
  27.1 1.2 %constant_dynamic-slice_fusion.1 = (bf16[1024,64]{1,0:T(8,128)(2,1)S(1)}, bf16[1024,64]{1,0:T(8,128)(2,1)S(1)}) fusion(bf16[1024,512]{1,0:T(8,128)(2,1)S(1)} %copy-done.1, s32[]{:T(128)S(6)} %select_n.28, bf16[1024,512]{1,0:T(8,128)(2,1)} %wk_ref.1), kind=kLoop, calls=%fused_computation.11 | loop fusion | bytes 524292 | tf_op jit(solution)/shard_map/dynamic_slice | solution.py:576
  28.3 0.5 fusion.pos_ref
  28.8 0.5 shard_map.137
  29.3 0.6 copy-done.7
  29.9 25.7 %shard_map.138 = (bf16[1536,128]{1,0:T(8,128)(2,1)S(1)}, f32[8,128,128]{2,1,0:T(8,128)S(1)}, bf16[512,128]{1,0:T(8,128)(2,1)S(1)}, bf16[8,64,128]{2,1,0:T(8,128)(2,1)S(1)}) custom-call(s32[8]{0:T(128)S(1)} %copy-done.7, s32[1]{0:T(128)} %bitcast.half_ref, bf16[8,128,256]{2,1,0:T(8,128)(2,1)S(1)} %all_to_all.15.own_ref, ...), custom_call_target="tpu_custom_call" | custom-call | tf_op jit(solution)/shard_map/pallas_call | solution.py:524
  55.6 0.6 collective-permute-start.1
  56.2 1.3 %collective-permute-done.1.came_ref = bf16[1536,128]{1,0:T(8,128)(2,1)S(1)} collective-permute-done((bf16[1536,128]{1,0:T(8,128)(2,1)S(1)}, bf16[1536,128]{1,0:T(8,128)(2,1)S(1)}, u32[]{:S(2)}, u32[]{:S(2)}) %collective-permute-start.1) | collective-permute-done | bytes 393248 | tf_op jit(solution)/shard_map/ppermute | solution.py:620
  57.5 1.3 %shard_map.139 = bf16[8,288,128]{2,1,0:T(8,128)(2,1)} custom-call(s32[1]{0:T(128)} %bitcast.half_ref, f32[8,128,128]{2,1,0:T(8,128)S(1)} %get-tuple-element.22.keep_ref, bf16[512,128]{1,0:T(8,128)(2,1)S(1)} %get-tuple-element.23.bucket_ref, bf16[8,64,128]{2,1,0:T(8,128)(2,1)S(1)} %get-tuple-element.24.query_ref, ...), custom_call_target="tpu_custom_call" | custom-call | tf_op jit(solution)/shard_map/pallas_call | solution.py:524
  58.8 3.7 %all-to-all-start.1 = ((bf16[8,288,128]{2,1,0:T(8,128)(2,1)}), bf16[8,288,128]{2,1,0:T(8,128)(2,1)S(1)}, u32[]{:S(2)}, u32[]{:S(2)}) async-start(bf16[8,288,128]{2,1,0:T(8,128)(2,1)} %shard_map.139), calls=%async_computation.1 | async-start | bytes 1179648 | tf_op jit(solution)/shard_map/all_to_all | solution.py:564
  62.6 16.6 %all-to-all-done.1.got_ref = bf16[8,288,128]{2,1,0:T(8,128)(2,1)S(1)} async-done(((bf16[8,288,128]{2,1,0:T(8,128)(2,1)}), bf16[8,288,128]{2,1,0:T(8,128)(2,1)S(1)}, u32[]{:S(2)}, u32[]{:S(2)}) %all-to-all-start.1) | async-done | bytes 589856 | tf_op jit(solution)/shard_map/all_to_all | solution.py:564
  79.2 1.5 %shard_map.140 = (bf16[128,512]{1,0:T(8,128)(2,1)}, bf16[128,512]{1,0:T(8,128)(2,1)}, bf16[128,512]{1,0:T(8,128)(2,1)}, f32[64,512]{1,0:T(8,128)}, f32[64,512]{1,0:T(8,128)}, /*index=5*/bf16[32,1024]{1,0:T(8,128)(2,1)S(1)}) custom-call(bf16[8,288,128]{2,1,0:T(8,128)(2,1)S(1)} %all-to-all-done.1.got_ref, bf16[1024,512]{1,0:T(8,128)(2,1)S(1)} %copy-done.2, ...), custom_call_target="tpu_custom_call" | custom-call | tf_op jit(solution)/shard_map/pallas_call | solution.py:524
  80.6 1.5 %collective-permute-start.2 = (bf16[32,512]{1,0:T(8,128)(2,1)S(1)}, bf16[32,512]{1,0:T(8,128)(2,1)S(1)}, u32[]{:S(2)}, u32[]{:S(2)}) collective-permute-start(bf16[32,512]{1,0:T(8,128)(2,1)S(1)} %constant_dynamic-slice_fusion), channel_id=1, source_target_pairs={{0,1},{1,0},{2,3},{3,2},{4,5},{5,4},{6,7},{7,6},{8,9},{9,8},{10,11... | collective-permute-start | bytes 98312 | tf_op jit(solution)/shard_map/ppermute | solution.py:639
  82.1 2.4 %collective-permute-done.2 = bf16[32,512]{1,0:T(8,128)(2,1)S(1)} collective-permute-done((bf16[32,512]{1,0:T(8,128)(2,1)S(1)}, bf16[32,512]{1,0:T(8,128)(2,1)S(1)}, u32[]{:S(2)}, u32[]{:S(2)}) %collective-permute-start.2) | collective-permute-done | bytes 32800 | tf_op jit(solution)/shard_map/ppermute | solution.py:639
  84.6 11.6 %all_to_all.16 = bf16[8,32,512]{2,1,0:T(8,128)(2,1)S(1)} all-to-all(bf16[8,32,512]{2,1,0:T(8,128)(2,1)S(1)} %broadcast_in_dim.2), channel_id=1, replica_groups={{0,4,8,12,16,20,24,28},{2,6,10,14,18,22,26,30},{1,5,9,13,17,21,25,29},{..., dimensions={0} | all-to-all | bytes 524288 | tf_op jit(solution)/shard_map/all_to_all | solution.py:564
  96.2 1.5 %collective-permute-done.3 = bf16[8,32,512]{2,1,0:T(8,128)(2,1)S(1)} collective-permute-done((bf16[8,32,512]{2,1,0:T(8,128)(2,1)S(1)}, bf16[8,32,512]{2,1,0:T(8,128)(2,1)S(1)}, u32[]{:S(2)}, u32[]{:S(2)}) %collective-permute-start.3) | collective-permute-done | bytes 262176 | tf_op jit(solution)/shard_map/ppermute | solution.py:642
  97.9 1.1 %bitcast_convert_fusion = f32[512,512]{1,0:T(8,128)} fusion(bf16[8,2,32,512]{3,2,1,0:T(8,128)(2,1)S(1)} %pad_maximum_fusion), kind=kLoop, calls=%fused_computation.3 | loop fusion | flops 262144 | bytes 1572864 | tf_op jit(solution)/shard_map/convert_element_type | solution.py:645
  (20 shorter events, 0.2 us)
Async XLA Ops:
  0.6 26.5 %copy-start.1 = (bf16[1024,512]{1,0:T(8,128)(2,1)S(1)}, bf16[1024,512]{1,0:T(8,128)(2,1)}, u32[]{:S(2)}) copy-start(bf16[1024,512]{1,0:T(8,128)(2,1)} %wq_ref.1) | copy-start | bytes 3145732
  0.6 1.0 %copy-start.3 = (bf16[128,512]{1,0:T(8,128)(2,1)S(1)}, bf16[128,512]{1,0:T(8,128)(2,1)}, u32[]{:S(2)}) copy-start(bf16[128,512]{1,0:T(8,128)(2,1)} %q_ref.1) | copy-start | bytes 393220
  1.6 0.9 copy-start.4
  2.5 0.9 copy-start.5
  3.4 0.9 copy-start.6
  4.6 23.7 %copy-start = (bf16[512,1024]{1,0:T(8,128)(2,1)S(1)}, bf16[512,1024]{1,0:T(8,128)(2,1)}, u32[]{:S(2)}) copy-start(bf16[512,1024]{1,0:T(8,128)(2,1)} %rel_ref.1) | copy-start | bytes 3145732
  26.3 2.9 %collective-permute-start = (bf16[8,128,256]{2,1,0:T(8,128)(2,1)S(1)}, bf16[8,128,256]{2,1,0:T(8,128)(2,1)S(1)}, u32[]{:S(2)}, u32[]{:S(2)}) collective-permute-start(bf16[8,128,256]{2,1,0:T(8,128)(2,1)S(1)} %all_to_all.15.own_ref), channel_id=1, source_target_pairs={{0,2},{2,0},{4,6},{6,4},{8,10},{10,8},{12,14},{14,12},{16,18},{18,... | collective-permute-start | bytes 1572872 | tf_op jit(solution)/shard_map/ppermute | solution.py:572
  26.3 0.7 copy-start.8
  29.3 0.7 copy-start.7
  55.6 1.9 %collective-permute-start.1 = (bf16[1536,128]{1,0:T(8,128)(2,1)S(1)}, bf16[1536,128]{1,0:T(8,128)(2,1)S(1)}, u32[]{:S(2)}, u32[]{:S(2)}) collective-permute-start(bf16[1536,128]{1,0:T(8,128)(2,1)S(1)} %get-tuple-element.25), channel_id=1, source_target_pairs={{0,2},{2,0},{4,6},{6,4},{8,10},{10,8},{12,14},{14,12},{16,18},{18,... | collective-permute-start | bytes 1179656 | tf_op jit(solution)/shard_map/ppermute | solution.py:620
  58.8 20.3 %copy-start.2 = (bf16[1024,512]{1,0:T(8,128)(2,1)S(1)}, bf16[1024,512]{1,0:T(8,128)(2,1)}, u32[]{:S(2)}) copy-start(bf16[1024,512]{1,0:T(8,128)(2,1)} %wk_ref.1) | copy-start | bytes 3145732
  58.8 20.3 %all-to-all-start.1 = ((bf16[8,288,128]{2,1,0:T(8,128)(2,1)}), bf16[8,288,128]{2,1,0:T(8,128)(2,1)S(1)}, u32[]{:S(2)}, u32[]{:S(2)}) async-start(bf16[8,288,128]{2,1,0:T(8,128)(2,1)} %shard_map.139), calls=%async_computation.1 | async-start | bytes 1179648 | tf_op jit(solution)/shard_map/all_to_all | solution.py:564
  80.6 3.9 %collective-permute-start.2 = (bf16[32,512]{1,0:T(8,128)(2,1)S(1)}, bf16[32,512]{1,0:T(8,128)(2,1)S(1)}, u32[]{:S(2)}, u32[]{:S(2)}) collective-permute-start(bf16[32,512]{1,0:T(8,128)(2,1)S(1)} %constant_dynamic-slice_fusion), channel_id=1, source_target_pairs={{0,1},{1,0},{2,3},{3,2},{4,5},{5,4},{6,7},{7,6},{8,9},{9,8},{10,11... | collective-permute-start | bytes 98312 | tf_op jit(solution)/shard_map/ppermute | solution.py:639
  96.2 1.5 %collective-permute-start.3 = (bf16[8,32,512]{2,1,0:T(8,128)(2,1)S(1)}, bf16[8,32,512]{2,1,0:T(8,128)(2,1)S(1)}, u32[]{:S(2)}, u32[]{:S(2)}) collective-permute-start(bf16[8,32,512]{2,1,0:T(8,128)(2,1)S(1)} %all_to_all.16), channel_id=1, source_target_pairs={{0,2},{2,0},{4,6},{6,4},{8,10},{10,8},{12,14},{14,12},{16,18},{18,... | collective-permute-start | bytes 786440 | tf_op jit(solution)/shard_map/ppermute | solution.py:642

commit v3 on v2

--- a/solution.py
+++ b/solution.py
@@ -10,7 +10,7 @@
 HD = 64
 SPAN = 4
 TILE = 128
-SPANS = (3, 5, 7)
+SPANS = (2, 3, 4, 5, 6, 7)
 BF = jnp.bfloat16
 F32 = jnp.float32
 
@@ -254,15 +254,26 @@
     )
 
 
-def pack_kernel(q_ref, g_ref, k_ref, v_ref, out_ref):
+def pack_kernel(q_ref, g_ref, k_ref, v_ref, out_ref, held, pieces, came, left):
+    loads = [
+        pltpu.make_async_copy(ref, held.at[i], came.at[i])
+        for i, ref in enumerate((q_ref, g_ref, k_ref, v_ref))
+    ]
+    for load in loads:
+        load.start()
+    for load in loads:
+        load.wait()
+    stores = []
     for head in range(out_ref.shape[0]):
         cols = slice(head * HD, (head + 1) * HD)
-        out_ref[head] = jnp.concatenate(
-            [q_ref[:, cols], g_ref[:, cols], k_ref[:, cols], v_ref[:, cols]], 1
-        )
-
-
-def table_kernel(pos_ref, table_ref, onehot, pk, pq):
+        pieces[head] = jnp.concatenate([held[i, :, cols] for i in range(4)], 1)
+        stores.append(pltpu.make_async_copy(pieces.at[head], out_ref.at[head], left.at[head]))
+        stores[-1].start()
+    for store in stores:
+        store.wait()
+
+
+def table_kernel(pos_ref, table_ref, onehot, pk, pq, both):
     buckets, valid = onehot.shape
     valid0 = valid // 2 + TILE
     for part in range(buckets // TILE):
@@ -274,12 +285,14 @@
     pq[...] = jnp.zeros_like(pq)
     pk[0:HD, valid0 : valid0 + valid] = expanded[:HD]
     pq[0:HD, valid0 : valid0 + valid] = expanded[HD:]
+    both[...] = jnp.zeros_like(both)
+    both[valid0 : valid0 + valid, :] = expanded.astype(F32).T.astype(BF)
 
 
 def head_kernel(
-    lens_ref, half_ref, own_ref, other_ref, onehot, pk, pq,
+    lens_ref, half_ref, own_ref, other_ref, onehot, pk, pq, rows_ref,
     send_ref, keep_ref, bucket_ref, query_ref,
-    kvs, acc, acc_pos, g_key, g_query, k_t, k_rev, s_q, st, dp, dtile, dq_nat, dq_pos,
+    kvs, acc, acc_pos, g_key, g_query, k_t, k_rev, s_q, st, dp, dtile, pairs, dq_nat, dq_pos,
 ):
     blocks = own_ref.shape[0]
     tiles = 2 * blocks
@@ -367,9 +380,11 @@
         key_x = pl.multiple_of(halo * 2 * TILE - delta, TILE)
         s_q[:, 0 : (span + 1) * TILE] = nn(qd, pk[:, pl.ds(key_x, (span + 1) * TILE)])
         best = jnp.full((8, TILE), masked_score, F32)
+        window_kv = kvs[pl.ds(first, span)].reshape(span * TILE, 2 * HD)
+        contents = nn(window_kv, right)
         for t in range(span):
-            kv = kvs[first + t]
-            both = nn(kv, right)
+            kv = window_kv[t * TILE : (t + 1) * TILE]
+            both = contents[t * TILE : (t + 1) * TILE]
             query_x = pl.multiple_of(2 * halo * TILE + delta - t * TILE, TILE)
             s_k = nn(kv, pq[:, pl.ds(query_x, 2 * TILE)])
             key_term = pltpu.roll(
@@ -407,28 +422,41 @@
         pair = jnp.concatenate([lows, jnp.where(low, jnp.zeros_like(qd), qd)], 0)
         dq_t = jnp.zeros((HD, TILE), F32)
         before = jnp.zeros((TILE, TILE), F32)
+        ahead_part = None
         for t in range(span):
             prob = st[t] * inverse
             dscore = (prob * (dp[t] - row_dot)).astype(BF)
-            query_x = pl.multiple_of(2 * halo * TILE + delta - t * TILE, TILE)
-            lhs = jnp.concatenate([dscore, prob.astype(BF)], 1)
-            acc[first + t] += nn(lhs, pair)
+            pairs[t] = jnp.concatenate([dscore, prob.astype(BF)], 1)
             stacked = nn(jnp.concatenate([k_t[first + t], swap], 0), dscore)
             dq_t = dq_t + stacked[:HD]
+            query_x = pl.multiple_of(2 * halo * TILE + delta - t * TILE, TILE)
             y = pltpu.roll(stacked[HD:], 0, 1, stride=1, stride_axis=0)
-            spread = jnp.concatenate(
-                [jnp.where(wrap_rev, y, 0.0), jnp.where(wrap_rev, 0.0, y)], 1
-            ).astype(BF)
-            acc_pos[first + t] += nt(spread, pq[0:HD, pl.ds(query_x, 2 * TILE)])
-            g_query[:, pl.ds(query_x, 2 * TILE)] += nn(k_rev[first + t], spread)
+            near = jnp.where(wrap_rev, y, 0.0).astype(BF)
+            far = jnp.where(wrap_rev, 0.0, y).astype(BF)
+            back = nn(jnp.concatenate([near, far], 1), rows_ref[pl.ds(query_x, 2 * TILE), :])
+            acc_pos[first + t] += back[:, HD:]
+            turned_keys = k_rev[first + t]
+            chunk = pl.ds(query_x + TILE, TILE)
+            if ahead_part is None:
+                g_query[:, chunk] += nn(turned_keys, far)
+            else:
+                g_query[:, chunk] += nn(
+                    jnp.concatenate([ahead_part[0], turned_keys], 1),
+                    jnp.concatenate([ahead_part[1], far], 0),
+                )
+            ahead_part = (turned_keys, near)
             z = pltpu.roll(nt(swap, dscore), 0, 1, stride=1, stride_axis=0)
             dtile[:, t * TILE : (t + 1) * TILE] = jnp.where(wrap_rev, z, before).astype(BF)
             before = z
+        g_query[:, pl.ds(query_x, TILE)] += nn(*ahead_part)
+        acc[pl.ds(first, span)] += nn(
+            pairs[0:span].reshape(span * TILE, 2 * TILE), pair
+        ).reshape(span, TILE, 2 * HD)
         dtile[:, span * TILE : (span + 1) * TILE] = jnp.where(wrap_rev, 0.0, before).astype(BF)
         spread_q = dtile[:, 0 : (span + 1) * TILE]
         window = pl.ds(key_x, (span + 1) * TILE)
         g_key[:, window] += nn(q_rev, spread_q)
-        back = nt(spread_q, pk[0:HD, window])
+        back = nn(spread_q, rows_ref[window, :])[:, :HD]
         high = back.astype(BF)
         dq_pos[b] = jnp.concatenate([high, (back - high.astype(F32)).astype(BF)], 1)
         dq_nat[b] = dq_t
@@ -469,33 +497,46 @@
     lax.fori_loop(0, blocks, finish, 0)
 
 
-def join_kernel(half_ref, keep_ref, bucket_ref, query_ref, came_ref, rel_ref, out_ref, weight, bucket):
+def join_kernel(
+    half_ref, keep_ref, bucket_ref, query_ref, came_ref, rel_ref, out_ref, rows_ref,
+    weight, bucket, pieces, low_rows, sems,
+):
     blocks = keep_ref.shape[0]
     tiles = 2 * blocks
     half = half_ref[0]
     w_rows = weight.shape[0] // tiles
     b_rows = bucket.shape[0] // tiles
     base_w = TILE + TILE // 2
-    base_b = base_w + w_rows
     total = bucket_ref[...].astype(F32) + came_ref[blocks * TILE :, :].astype(F32)
     bucket[...] = total
+    for b in range(blocks):
+        tile = 2 * b + half
+        low_rows[b] = bucket[pl.ds(tile * b_rows, b_rows), :].astype(BF)
+    first = pltpu.make_async_copy(low_rows, rows_ref, sems.at[0])
+    first.start()
     weight[...] = nn(total.T.astype(BF), rel_ref[...]).T
     for b in range(blocks):
         came = came_ref[b * TILE : (b + 1) * TILE, :].astype(F32)
         tile = 2 * b + half
-        out_ref[b, 0:TILE, :] = (keep_ref[b] + came).astype(BF)
-        out_ref[b, TILE:base_w, :] = query_ref[b]
-        out_ref[b, base_w:base_b, :] = weight[pl.ds(tile * w_rows, w_rows), :].astype(BF)
-        out_ref[b, base_b:, :] = bucket[pl.ds(tile * b_rows, b_rows), :].astype(BF)
-
-
-def unpack_kernel(
-    got_ref, wk_ref, wq_ref, dq_ref, dk_ref, dv_ref, dwq_ref, dwk_ref, rel_ref,
-):
-    w_rows = dwk_ref.shape[0]
+        pieces[b, 0:TILE, :] = (keep_ref[b] + came).astype(BF)
+        pieces[b, TILE:base_w, :] = query_ref[b]
+        pieces[b, base_w:, :] = weight[pl.ds(tile * w_rows, w_rows), :].astype(BF)
+    second = pltpu.make_async_copy(pieces, out_ref, sems.at[1])
+    second.start()
+    first.wait()
+    second.wait()
+
+
+def rel_kernel(got_ref, wk_ref, wq_ref, rel_ref):
+    heads = range(got_ref.shape[0])
+    rel = nt(jnp.concatenate([got_ref[h, :, :HD] for h in heads], 1), wk_ref[...]) + nt(
+        jnp.concatenate([got_ref[h, :, HD:] for h in heads], 1), wq_ref[...]
+    )
+    rel_ref[...] = rel.astype(BF)
+
+
+def unpack_kernel(got_ref, dq_ref, dk_ref, dv_ref, dwq_ref, dwk_ref):
     base_w = TILE + TILE // 2
-    base_b = base_w + w_rows
-    keys_low, queries_low = [], []
     for g in range(got_ref.shape[0] // 2):
         cols = slice(2 * g * HD, 2 * (g + 1) * HD)
         two = [got_ref[2 * g], got_ref[2 * g + 1]]
@@ -508,40 +549,23 @@
         )
         dk_ref[:, cols] = jnp.concatenate([one[:TILE, :HD] for one in two], 1)
         dv_ref[:, cols] = jnp.concatenate([one[:TILE, HD:] for one in two], 1)
-        dwk_ref[:, cols] = jnp.concatenate([one[base_w:base_b, :HD] for one in two], 1).astype(F32)
-        dwq_ref[:, cols] = jnp.concatenate([one[base_w:base_b, HD:] for one in two], 1).astype(F32)
-        keys_low += [one[base_b:, :HD] for one in two]
-        queries_low += [one[base_b:, HD:] for one in two]
-    rel = nt(jnp.concatenate(keys_low, 1), wk_ref[...]) + nt(
-        jnp.concatenate(queries_low, 1), wq_ref[...]
-    )
-    rel_ref[...] = rel.astype(BF)
-
-
-def whole_call(kernel, inputs, outputs, scratch=(), scalars=0, limit=48):
-    vmem = pl.BlockSpec(memory_space=pltpu.VMEM)
-    smem = pl.BlockSpec(memory_space=pltpu.SMEM)
+        dwk_ref[:, cols] = jnp.concatenate([one[base_w:, :HD] for one in two], 1).astype(F32)
+        dwq_ref[:, cols] = jnp.concatenate([one[base_w:, HD:] for one in two], 1).astype(F32)
+
+
+VMEM = pl.BlockSpec(memory_space=pltpu.VMEM)
+SMEM = pl.BlockSpec(memory_space=pltpu.SMEM)
+HBM = pl.BlockSpec(memory_space=pltpu.HBM)
+
+
+def whole_call(kernel, inputs, outputs, scratch=(), scalars=0, source=VMEM, target=VMEM, limit=48):
     return pl.pallas_call(
         kernel,
         out_shape=outputs,
-        in_specs=[smem] * scalars + [vmem] * (len(inputs) - scalars),
-        out_specs=jax.tree.map(lambda _: vmem, outputs),
+        in_specs=[SMEM] * scalars + [source] * (len(inputs) - scalars),
+        out_specs=jax.tree.map(lambda _: target, outputs),
         scratch_shapes=list(scratch),
         compiler_params=pltpu.CompilerParams(vmem_limit_bytes=limit << 20),
-    )(*inputs)
-
-
-def staged_call(kernel, inputs, outputs):
-    def spec(array):
-        return pl.BlockSpec(array.shape, lambda step: (0,) * len(array.shape))
-
-    return pl.pallas_call(
-        kernel,
-        grid=(1,),
-        out_shape=outputs,
-        in_specs=[spec(array) for array in inputs],
-        out_specs=jax.tree.map(spec, outputs),
-        compiler_params=pltpu.CompilerParams(vmem_limit_bytes=32 << 20),
     )(*inputs)
 
 
@@ -563,10 +587,19 @@
     def spread(pieces):
         return lax.all_to_all(pieces, "seq", 0, 0, axis_index_groups=halves, tiled=True)
 
-    packed = staged_call(
+    packed = whole_call(
         pack_kernel,
         (queries, out_grad, keys, values),
         shape((heads, tokens_dev, 4 * HD), BF),
+        [
+            vm((4, tokens_dev, width), BF),
+            vm((heads, tokens_dev, 4 * HD), BF),
+            pltpu.SemaphoreType.DMA((4,)),
+            pltpu.SemaphoreType.DMA((heads,)),
+        ],
+        source=HBM,
+        target=HBM,
+        limit=64,
     )
     own = spread(packed)
     other = lax.ppermute(own, "seq", partners)
@@ -580,7 +613,7 @@
     pos = nn(rel_emb, w_own).astype(BF)
     table = jnp.flip(bucket_table).reshape(1, -1)
     w_rows, b_rows = depth // seq_count, buckets // seq_count
-    rows = TILE + TILE // 2 + w_rows + b_rows
+    rows = TILE + TILE // 2 + w_rows
     line = 2 * span * TILE
     tables = whole_call(
         table_kernel,
@@ -589,6 +622,7 @@
             shape((buckets, table.shape[1]), BF),
             shape((2 * HD, line), BF),
             shape((2 * HD, line), BF),
+            shape((line, 2 * HD), BF),
         ],
     )
     sent, kept, bucket, query = whole_call(
@@ -612,27 +646,34 @@
             vm((span, TILE, TILE), F32),
             vm((span, TILE, TILE), F32),
             vm((TILE, (span + 1) * TILE), BF),
+            vm((span, TILE, 2 * TILE), BF),
             vm((heads, HD, TILE), F32),
             vm((heads, TILE, 2 * HD), BF),
         ],
         scalars=2,
     )
     came = lax.ppermute(sent, "seq", partners)
-    joined = whole_call(
+    joined, bucket_rows = whole_call(
         join_kernel,
         (half, kept, bucket, query, came, rel_emb),
-        shape((heads, rows, 2 * HD), BF),
-        [vm((depth, 2 * HD), F32), vm((buckets, 2 * HD), F32)],
+        [shape((heads, rows, 2 * HD), BF), shape((heads, b_rows, 2 * HD), BF)],
+        [
+            vm((depth, 2 * HD), F32),
+            vm((buckets, 2 * HD), F32),
+            vm((heads, rows, 2 * HD), BF),
+            vm((heads, b_rows, 2 * HD), BF),
+            pltpu.SemaphoreType.DMA((2,)),
+        ],
         scalars=1,
+        target=HBM,
+        limit=64,
+    )
+    rel_rows = whole_call(
+        rel_kernel, (spread(bucket_rows), w_key, w_query), shape((b_rows, depth), BF)
     )
     returned = spread(joined)
     tokens = shape((tokens_dev, width), BF)
     weights = shape((w_rows, width), F32)
-    query_grad, key_grad, value_grad, w_query_grad, w_key_grad, rel_rows = whole_call(
-        unpack_kernel,
-        (returned, w_key, w_query),
-        [tokens, tokens, tokens, weights, weights, shape((b_rows, depth), BF)],
-    )
     head_index = lax.axis_index("head")
     mine_rel = lax.dynamic_slice_in_dim(rel_rows, head_index * width, width, 1)
     far_rel = lax.dynamic_slice_in_dim(rel_rows, (1 - head_index) * width, width, 1)
@@ -643,6 +684,9 @@
     even = jnp.where(half[0] == 0, near, far)
     odd = jnp.where(half[0] == 0, far, near)
     rel_emb_grad = jnp.stack([even, odd], 1).reshape(buckets, width).astype(F32)
+    query_grad, key_grad, value_grad, w_query_grad, w_key_grad = whole_call(
+        unpack_kernel, (returned,), [tokens, tokens, tokens, weights, weights]
+    )
     return (query_grad, key_grad, value_grad, rel_emb_grad, w_query_grad, w_key_grad)
 
 

time: 101 us -> 108 us (1.069)
  Pallas kernels: 29.2 us -> 33.7 us
  starting transfers between devices: 5.8 us -> 8.72 us
  local copies, waits for them, and re-layouts: 6.3 us -> 8.01 us
    pallas_call x5 -> x6, Pallas kernels: 29.2 us -> 33.7 us  [whole_call(): pl.pallas_call(kernel, out_shape=outputs, in_specs=[SMEM] * scalars + [so...]
    all_to_all x1 -> x2, starting transfers between devices: 3.74 us -> 7.09 us  [spread(): lax.all_to_all(pieces, 'seq', 0, 0, axis_index_groups=halves, tiled=True)]
    unnamed x18, local copies, waits for them, and re-layouts: 5.05 us -> 6.65 us
    all_to_all x1 -> x2, waiting for transfers between devices: 16.6 us -> 15.3 us  [spread(): lax.all_to_all(pieces, 'seq', 0, 0, axis_index_groups=halves, tiled=True)]
  transfers between devices with their start and end apart: 5 -> 6, of which waited for: 4 -> 5; matrix products, arithmetic and copies ran while one was open for 2% -> 3% of each run, Pallas kernels for 0% -> 1%
where the time goes in v3:
time: 108 us; the launch traced here: 107 us
  Pallas kernels  33.7 us (31%)
  blocking collectives  32.6 us (30%)
  waiting for transfers between devices  21 us (19%)
  starting transfers between devices  8.72 us (8%)
  local copies, waits for them, and re-layouts  8.01 us (7%)
  other arithmetic  1.24 us (1%)
    pallas_call x6, Pallas kernels, whole_call(): pl.pallas_call(kernel, out_shape=outputs, in_specs=[SMEM] * scalars + [so...  33.7 us
    all_to_all x2, blocking collectives, spread(): lax.all_to_all(pieces, 'seq', 0, 0, axis_index_groups=halves, tiled=True)  32.6 us
    all_to_all x2, waiting for transfers between devices, spread(): lax.all_to_all(pieces, 'seq', 0, 0, axis_index_groups=halves, tiled=True)  15.3 us
    all_to_all x2, starting transfers between devices, spread(): lax.all_to_all(pieces, 'seq', 0, 0, axis_index_groups=halves, tiled=True)  7.09 us
    unnamed x18, local copies, waits for them, and re-layouts  6.65 us
    ppermute x1, waiting for transfers between devices, head_body(): far_rel = lax.ppermute(far_rel, 'head', [(0, 1), (1, 0)])  2.43 us
  transfers between devices with their start and end apart: 6, of which 5 were waited for; matrix products, arithmetic and copies ran while one was open for 3% of the time, Pallas kernels for 1%

profile of v3, /device:TPU:0, one launch (start us, length us, event | category | flops | bytes accessed | tf_op | source)
XLA Modules:
  0.0 106.6 jit_solution(3587551465674342586)
XLA Ops:
  0.6 2.1 %shard_map.136 = bf16[8,128,256]{2,1,0:T(8,128)(2,1)} custom-call(bf16[128,512]{1,0:T(8,128)(2,1)} %q_ref.1, bf16[128,512]{1,0:T(8,128)(2,1)} %g_ref.1, bf16[128,512]{1,0:T(8,128)(2,1)} %k_ref.1, bf16[128,512]{1,0:T(8,128)(2,1)} %v_ref.1), custom_call_target="tpu_custom_call" | custom-call | tf_op jit(solution)/shard_map/pallas_call | solution.py:562
  2.7 22.0 %all_to_all.20.own_ref = bf16[8,128,256]{2,1,0:T(8,128)(2,1)S(1)} all-to-all(bf16[8,128,256]{2,1,0:T(8,128)(2,1)} %shard_map.136), channel_id=1, replica_groups={{0,4,8,12,16,20,24,28},{2,6,10,14,18,22,26,30},{1,5,9,13,17,21,25,29},{..., dimensions={0} | all-to-all | bytes 1048576 | tf_op jit(solution)/shard_map/all_to_all | solution.py:588
  24.7 0.7 copy-done.8
  25.4 1.2 %constant_dynamic-slice_fusion.1 = (bf16[1024,64]{1,0:T(8,128)(2,1)S(1)}, bf16[1024,64]{1,0:T(8,128)(2,1)S(1)}) fusion(bf16[1024,512]{1,0:T(8,128)(2,1)} %wq_ref.1, s32[]{:T(128)S(6)} %select_n.28, bf16[1024,512]{1,0:T(8,128)(2,1)} %wk_ref.1), kind=kLoop, calls=%fused_computation.11 | loop fusion | bytes 524292 | tf_op jit(solution)/shard_map/dynamic_slice | solution.py:609
  28.4 26.4 %shard_map.138 = (bf16[1536,128]{1,0:T(8,128)(2,1)S(1)}, f32[8,128,128]{2,1,0:T(8,128)S(1)}, bf16[512,128]{1,0:T(8,128)(2,1)S(1)}, bf16[8,64,128]{2,1,0:T(8,128)(2,1)S(1)}) custom-call(s32[8]{0:T(128)S(1)} %copy-done.5, s32[1]{0:T(128)} %bitcast.half_ref, bf16[8,128,256]{2,1,0:T(8,128)(2,1)S(1)} %all_to_all.20.own_ref, ...), custom_call_target="tpu_custom_call" | custom-call | tf_op jit(solution)/shard_map/pallas_call | solution.py:562
  54.8 0.8 copy-done.2
  55.6 0.7 copy-done.3
  56.3 0.7 copy-done.4
  56.9 1.7 %collective-permute-done.1.came_ref = bf16[1536,128]{1,0:T(8,128)(2,1)S(1)} collective-permute-done((bf16[1536,128]{1,0:T(8,128)(2,1)S(1)}, bf16[1536,128]{1,0:T(8,128)(2,1)S(1)}, u32[]{:S(2)}, u32[]{:S(2)}) %collective-permute-start.1) | collective-permute-done | bytes 393248 | tf_op jit(solution)/shard_map/ppermute | solution.py:655
  58.6 0.8 copy-done.7
  59.4 2.9 %shard_map.139 = (bf16[8,256,128]{2,1,0:T(8,128)(2,1)}, bf16[8,32,128]{2,1,0:T(8,128)(2,1)}) custom-call(s32[1]{0:T(128)} %bitcast.half_ref, f32[8,128,128]{2,1,0:T(8,128)} %copy-done.2, bf16[512,128]{1,0:T(8,128)(2,1)} %copy-done.3, bf16[8,64,128]{2,1,0:T(8,128)(2,1)} %copy-done.4, bf16[1536,128]{1,0:T(8,128)(2,1)} %copy-done.7, bf16[512,1024]{1,0:T(8,128)(2,1)} %rel_ref.1), custom_call_target="tpu_custom_call" | custom-call | tf_op jit(solution)/shard_map/pallas_call | solution.py:562
  62.3 3.6 %all-to-all-start.2 = ((bf16[8,32,128]{2,1,0:T(8,128)(2,1)}), bf16[8,32,128]{2,1,0:T(8,128)(2,1)S(1)}, u32[]{:S(2)}, u32[]{:S(2)}) async-start(bf16[8,32,128]{2,1,0:T(8,128)(2,1)} %get-tuple-element.33), calls=%async_computation.2 | async-start | bytes 131072 | tf_op jit(solution)/shard_map/all_to_all | solution.py:588
  65.9 6.9 %all-to-all-done.2.got_ref = bf16[8,32,128]{2,1,0:T(8,128)(2,1)S(1)} async-done(((bf16[8,32,128]{2,1,0:T(8,128)(2,1)}), bf16[8,32,128]{2,1,0:T(8,128)(2,1)S(1)}, u32[]{:S(2)}, u32[]{:S(2)}) %all-to-all-start.2) | async-done | bytes 65568 | tf_op jit(solution)/shard_map/all_to_all | solution.py:588
  72.8 1.2 %copy-done = bf16[1024,512]{1,0:T(8,128)(2,1)S(1)} copy-done((bf16[1024,512]{1,0:T(8,128)(2,1)S(1)}, bf16[1024,512]{1,0:T(8,128)(2,1)}, u32[]{:S(2)}) %copy-start) | copy-done | bytes 1048600
  74.1 1.2 %copy-done.1 = bf16[1024,512]{1,0:T(8,128)(2,1)S(1)} copy-done((bf16[1024,512]{1,0:T(8,128)(2,1)S(1)}, bf16[1024,512]{1,0:T(8,128)(2,1)}, u32[]{:S(2)}) %copy-start.1) | copy-done | bytes 1048600
  75.3 0.7 shard_map.141
  76.0 1.6 %collective-permute-start.2 = (bf16[32,512]{1,0:T(8,128)(2,1)S(1)}, bf16[32,512]{1,0:T(8,128)(2,1)S(1)}, u32[]{:S(2)}, u32[]{:S(2)}) collective-permute-start(bf16[32,512]{1,0:T(8,128)(2,1)S(1)} %constant_dynamic-slice_fusion), channel_id=1, source_target_pairs={{0,1},{1,0},{2,3},{3,2},{4,5},{5,4},{6,7},{7,6},{8,9},{9,8},{10,11... | collective-permute-start | bytes 98312 | tf_op jit(solution)/shard_map/ppermute | solution.py:680
  77.6 2.4 %collective-permute-done.2 = bf16[32,512]{1,0:T(8,128)(2,1)S(1)} collective-permute-done((bf16[32,512]{1,0:T(8,128)(2,1)S(1)}, bf16[32,512]{1,0:T(8,128)(2,1)S(1)}, u32[]{:S(2)}, u32[]{:S(2)}) %collective-permute-start.2) | collective-permute-done | bytes 32800 | tf_op jit(solution)/shard_map/ppermute | solution.py:680
  80.0 10.6 %all_to_all.21 = bf16[8,32,512]{2,1,0:T(8,128)(2,1)S(1)} all-to-all(bf16[8,32,512]{2,1,0:T(8,128)(2,1)S(1)} %broadcast_in_dim.2), channel_id=1, replica_groups={{0,4,8,12,16,20,24,28},{2,6,10,14,18,22,26,30},{1,5,9,13,17,21,25,29},{..., dimensions={0} | all-to-all | bytes 524288 | tf_op jit(solution)/shard_map/all_to_all | solution.py:588
  90.7 3.5 %all-to-all-start.1 = ((bf16[8,256,128]{2,1,0:T(8,128)(2,1)}), bf16[8,256,128]{2,1,0:T(8,128)(2,1)S(1)}, u32[]{:S(2)}, u32[]{:S(2)}) async-start(bf16[8,256,128]{2,1,0:T(8,128)(2,1)} %get-tuple-element.29), calls=%async_computation.1 | async-start | bytes 1048576 | tf_op jit(solution)/shard_map/all_to_all | solution.py:588
  94.3 1.5 %collective-permute-done.3 = bf16[8,32,512]{2,1,0:T(8,128)(2,1)S(1)} collective-permute-done((bf16[8,32,512]{2,1,0:T(8,128)(2,1)S(1)}, bf16[8,32,512]{2,1,0:T(8,128)(2,1)S(1)}, u32[]{:S(2)}, u32[]{:S(2)}) %collective-permute-start.3) | collective-permute-done | bytes 262176 | tf_op jit(solution)/shard_map/ppermute | solution.py:683
  95.9 1.1 %bitcast_convert_fusion = f32[512,512]{1,0:T(8,128)} fusion(bf16[8,2,32,512]{3,2,1,0:T(8,128)(2,1)S(1)} %pad_maximum_fusion), kind=kLoop, calls=%fused_computation.3 | loop fusion | flops 262144 | bytes 1572864 | tf_op jit(solution)/shard_map/convert_element_type | solution.py:686
  97.0 8.4 %all-to-all-done.1.got_ref = bf16[8,256,128]{2,1,0:T(8,128)(2,1)S(1)} async-done(((bf16[8,256,128]{2,1,0:T(8,128)(2,1)}), bf16[8,256,128]{2,1,0:T(8,128)(2,1)S(1)}, u32[]{:S(2)}, u32[]{:S(2)}) %all-to-all-start.1) | async-done | bytes 524320 | tf_op jit(solution)/shard_map/all_to_all | solution.py:588
  105.4 1.1 %shard_map.140 = (bf16[128,512]{1,0:T(8,128)(2,1)}, bf16[128,512]{1,0:T(8,128)(2,1)}, bf16[128,512]{1,0:T(8,128)(2,1)}, f32[64,512]{1,0:T(8,128)}, f32[64,512]{1,0:T(8,128)}) custom-call(bf16[8,256,128]{2,1,0:T(8,128)(2,1)S(1)} %all-to-all-done.1.got_ref), custom_call_target="tpu_custom_call" | custom-call | tf_op jit(solution)/shard_map/pallas_call | solution.py:562
  (23 shorter events, 2.0 us)
Async XLA Ops:
  2.7 24.0 %copy-start.6 = (bf16[512,1024]{1,0:T(8,128)(2,1)S(1)}, bf16[512,1024]{1,0:T(8,128)(2,1)}, u32[]{:S(2)}) copy-start(bf16[512,1024]{1,0:T(8,128)(2,1)} %rel_ref.1) | copy-start | bytes 3145732
  24.7 3.1 %collective-permute-start = (bf16[8,128,256]{2,1,0:T(8,128)(2,1)S(1)}, bf16[8,128,256]{2,1,0:T(8,128)(2,1)S(1)}, u32[]{:S(2)}, u32[]{:S(2)}) collective-permute-start(bf16[8,128,256]{2,1,0:T(8,128)(2,1)S(1)} %all_to_all.20.own_ref), channel_id=1, source_target_pairs={{0,2},{2,0},{4,6},{6,4},{8,10},{10,8},{12,14},{14,12},{16,18},{18,... | collective-permute-start | bytes 1572872 | tf_op jit(solution)/shard_map/ppermute | solution.py:605
  24.7 0.7 copy-start.8
  27.8 0.7 copy-start.5
  54.8 0.8 copy-start.2
  55.6 0.7 copy-start.3
  56.3 0.7 copy-start.4
  56.9 1.7 %collective-permute-start.1 = (bf16[1536,128]{1,0:T(8,128)(2,1)S(1)}, bf16[1536,128]{1,0:T(8,128)(2,1)S(1)}, u32[]{:S(2)}, u32[]{:S(2)}) collective-permute-start(bf16[1536,128]{1,0:T(8,128)(2,1)S(1)} %get-tuple-element.28), channel_id=1, source_target_pairs={{0,2},{2,0},{4,6},{6,4},{8,10},{10,8},{12,14},{14,12},{16,18},{18,... | collective-permute-start | bytes 1179656 | tf_op jit(solution)/shard_map/ppermute | solution.py:655
  58.6 0.8 copy-start.7
  62.3 10.5 %all-to-all-start.2 = ((bf16[8,32,128]{2,1,0:T(8,128)(2,1)}), bf16[8,32,128]{2,1,0:T(8,128)(2,1)S(1)}, u32[]{:S(2)}, u32[]{:S(2)}) async-start(bf16[8,32,128]{2,1,0:T(8,128)(2,1)} %get-tuple-element.33), calls=%async_computation.2 | async-start | bytes 131072 | tf_op jit(solution)/shard_map/all_to_all | solution.py:588
  72.8 1.2 %copy-start = (bf16[1024,512]{1,0:T(8,128)(2,1)S(1)}, bf16[1024,512]{1,0:T(8,128)(2,1)}, u32[]{:S(2)}) copy-start(bf16[1024,512]{1,0:T(8,128)(2,1)} %wq_ref.1) | copy-start | bytes 3145732
  74.1 1.2 %copy-start.1 = (bf16[1024,512]{1,0:T(8,128)(2,1)S(1)}, bf16[1024,512]{1,0:T(8,128)(2,1)}, u32[]{:S(2)}) copy-start(bf16[1024,512]{1,0:T(8,128)(2,1)} %wk_ref.1) | copy-start | bytes 3145732
  76.0 4.0 %collective-permute-start.2 = (bf16[32,512]{1,0:T(8,128)(2,1)S(1)}, bf16[32,512]{1,0:T(8,128)(2,1)S(1)}, u32[]{:S(2)}, u32[]{:S(2)}) collective-permute-start(bf16[32,512]{1,0:T(8,128)(2,1)S(1)} %constant_dynamic-slice_fusion), channel_id=1, source_target_pairs={{0,1},{1,0},{2,3},{3,2},{4,5},{5,4},{6,7},{7,6},{8,9},{9,8},{10,11... | collective-permute-start | bytes 98312 | tf_op jit(solution)/shard_map/ppermute | solution.py:680
  90.7 14.8 %all-to-all-start.1 = ((bf16[8,256,128]{2,1,0:T(8,128)(2,1)}), bf16[8,256,128]{2,1,0:T(8,128)(2,1)S(1)}, u32[]{:S(2)}, u32[]{:S(2)}) async-start(bf16[8,256,128]{2,1,0:T(8,128)(2,1)} %get-tuple-element.29), calls=%async_computation.1 | async-start | bytes 1048576 | tf_op jit(solution)/shard_map/all_to_all | solution.py:588
  94.2 1.6 %collective-permute-start.3 = (bf16[8,32,512]{2,1,0:T(8,128)(2,1)S(1)}, bf16[8,32,512]{2,1,0:T(8,128)(2,1)S(1)}, u32[]{:S(2)}, u32[]{:S(2)}) collective-permute-start(bf16[8,32,512]{2,1,0:T(8,128)(2,1)S(1)} %all_to_all.21), channel_id=1, source_target_pairs={{0,2},{2,0},{4,6},{6,4},{8,10},{10,8},{12,14},{14,12},{16,18},{18,... | collective-permute-start | bytes 786440 | tf_op jit(solution)/shard_map/ppermute | solution.py:683

commit v4 on v3

--- a/solution.py
+++ b/solution.py
@@ -302,6 +302,7 @@
     scale = 1.0 / math.sqrt(3.0 * HD)
     valid0 = (halo + 1) * TILE
     half = half_ref[0]
+    docs = lens_ref.shape[0]
     row, col = grid_of((TILE, TILE))
     swap = jnp.where(row + col == TILE - 1, 1.0, 0.0).astype(BF)
     wrap = row + col >= TILE - 1
@@ -321,7 +322,7 @@
             k_rev[tile] = nn(turned[:HD], swap).astype(BF)
         return carry
 
-    lax.fori_loop(0, blocks, transpose_tile, 0)
+    lax.fori_loop(0, blocks, transpose_tile, 0, unroll=True)
 
     def block(b, carry):
         own = 2 * b + half
@@ -336,7 +337,7 @@
 
         zero = jnp.int32(0)
         _, reach_low, reach_high = lax.fori_loop(
-            0, lens_ref.shape[0], next_end, (zero, zero, zero)
+            0, docs, next_end, (zero, zero, zero), unroll=docs <= 16
         )
         lowest = reach_low // TILE
         count = (reach_high + TILE - 1) // TILE - lowest
@@ -372,7 +373,7 @@
 
         nothing = jnp.zeros((1, TILE), jnp.int32)
         _, start, stop = lax.fori_loop(
-            0, lens_ref.shape[0], next_doc, (jnp.int32(0), nothing, nothing)
+            0, docs, next_doc, (jnp.int32(0), nothing, nothing), unroll=docs <= 16
         )
         start = start - first * TILE
         stop = stop - first * TILE
@@ -494,49 +495,41 @@
         query_ref[b] = jnp.concatenate([grad[: TILE // 2], grad[TILE // 2 :]], 1).astype(BF)
         return carry
 
-    lax.fori_loop(0, blocks, finish, 0)
-
-
-def join_kernel(
-    half_ref, keep_ref, bucket_ref, query_ref, came_ref, rel_ref, out_ref, rows_ref,
-    weight, bucket, pieces, low_rows, sems,
-):
+    lax.fori_loop(0, blocks, finish, 0, unroll=True)
+
+
+def join_kernel(half_ref, keep_ref, bucket_ref, query_ref, came_ref, rel_ref, out_ref, weight, bucket):
     blocks = keep_ref.shape[0]
     tiles = 2 * blocks
     half = half_ref[0]
     w_rows = weight.shape[0] // tiles
     b_rows = bucket.shape[0] // tiles
     base_w = TILE + TILE // 2
+    base_b = base_w + w_rows
     total = bucket_ref[...].astype(F32) + came_ref[blocks * TILE :, :].astype(F32)
     bucket[...] = total
-    for b in range(blocks):
-        tile = 2 * b + half
-        low_rows[b] = bucket[pl.ds(tile * b_rows, b_rows), :].astype(BF)
-    first = pltpu.make_async_copy(low_rows, rows_ref, sems.at[0])
-    first.start()
     weight[...] = nn(total.T.astype(BF), rel_ref[...]).T
     for b in range(blocks):
         came = came_ref[b * TILE : (b + 1) * TILE, :].astype(F32)
         tile = 2 * b + half
-        pieces[b, 0:TILE, :] = (keep_ref[b] + came).astype(BF)
-        pieces[b, TILE:base_w, :] = query_ref[b]
-        pieces[b, base_w:, :] = weight[pl.ds(tile * w_rows, w_rows), :].astype(BF)
-    second = pltpu.make_async_copy(pieces, out_ref, sems.at[1])
-    second.start()
-    first.wait()
-    second.wait()
+        out_ref[b, 0:TILE, :] = (keep_ref[b] + came).astype(BF)
+        out_ref[b, TILE:base_w, :] = query_ref[b]
+        out_ref[b, base_w:base_b, :] = weight[pl.ds(tile * w_rows, w_rows), :].astype(BF)
+        out_ref[b, base_b:, :] = bucket[pl.ds(tile * b_rows, b_rows), :].astype(BF)
 
 
 def rel_kernel(got_ref, wk_ref, wq_ref, rel_ref):
     heads = range(got_ref.shape[0])
-    rel = nt(jnp.concatenate([got_ref[h, :, :HD] for h in heads], 1), wk_ref[...]) + nt(
-        jnp.concatenate([got_ref[h, :, HD:] for h in heads], 1), wq_ref[...]
+    base_b = got_ref.shape[1] - rel_ref.shape[0]
+    rel = nt(jnp.concatenate([got_ref[h, base_b:, :HD] for h in heads], 1), wk_ref[...]) + nt(
+        jnp.concatenate([got_ref[h, base_b:, HD:] for h in heads], 1), wq_ref[...]
     )
     rel_ref[...] = rel.astype(BF)
 
 
 def unpack_kernel(got_ref, dq_ref, dk_ref, dv_ref, dwq_ref, dwk_ref):
     base_w = TILE + TILE // 2
+    base_b = base_w + dwk_ref.shape[0]
     for g in range(got_ref.shape[0] // 2):
         cols = slice(2 * g * HD, 2 * (g + 1) * HD)
         two = [got_ref[2 * g], got_ref[2 * g + 1]]
@@ -549,8 +542,8 @@
         )
         dk_ref[:, cols] = jnp.concatenate([one[:TILE, :HD] for one in two], 1)
         dv_ref[:, cols] = jnp.concatenate([one[:TILE, HD:] for one in two], 1)
-        dwk_ref[:, cols] = jnp.concatenate([one[base_w:, :HD] for one in two], 1).astype(F32)
-        dwq_ref[:, cols] = jnp.concatenate([one[base_w:, HD:] for one in two], 1).astype(F32)
+        dwk_ref[:, cols] = jnp.concatenate([one[base_w:base_b, :HD] for one in two], 1).astype(F32)
+        dwq_ref[:, cols] = jnp.concatenate([one[base_w:base_b, HD:] for one in two], 1).astype(F32)
 
 
 VMEM = pl.BlockSpec(memory_space=pltpu.VMEM)
@@ -613,7 +606,7 @@
     pos = nn(rel_emb, w_own).astype(BF)
     table = jnp.flip(bucket_table).reshape(1, -1)
     w_rows, b_rows = depth // seq_count, buckets // seq_count
-    rows = TILE + TILE // 2 + w_rows
+    rows = TILE + TILE // 2 + w_rows + b_rows
     line = 2 * span * TILE
     tables = whole_call(
         table_kernel,
@@ -653,25 +646,17 @@
         scalars=2,
     )
     came = lax.ppermute(sent, "seq", partners)
-    joined, bucket_rows = whole_call(
+    joined = whole_call(
         join_kernel,
         (half, kept, bucket, query, came, rel_emb),
-        [shape((heads, rows, 2 * HD), BF), shape((heads, b_rows, 2 * HD), BF)],
-        [
-            vm((depth, 2 * HD), F32),
-            vm((buckets, 2 * HD), F32),
-            vm((heads, rows, 2 * HD), BF),
-            vm((heads, b_rows, 2 * HD), BF),
-            pltpu.SemaphoreType.DMA((2,)),
-        ],
+        shape((heads, rows, 2 * HD), BF),
+        [vm((depth, 2 * HD), F32), vm((buckets, 2 * HD), F32)],
         scalars=1,
-        target=HBM,
-        limit=64,
-    )
+    )
+    returned = spread(joined)
     rel_rows = whole_call(
-        rel_kernel, (spread(bucket_rows), w_key, w_query), shape((b_rows, depth), BF)
-    )
-    returned = spread(joined)
+        rel_kernel, (returned, w_key, w_query), shape((b_rows, depth), BF)
+    )
     tokens = shape((tokens_dev, width), BF)
     weights = shape((w_rows, width), F32)
     head_index = lax.axis_index("head")

time: 108 us -> 92.8 us (0.86)
  Pallas kernels: 33.7 us -> 25.4 us
  local copies, waits for them, and re-layouts: 8.01 us -> 2.71 us
  starting transfers between devices: 8.72 us -> 7.22 us
    pallas_call x6, Pallas kernels: 33.7 us -> 25.4 us  [whole_call(): pl.pallas_call(kernel, out_shape=outputs, in_specs=[SMEM] * scalars + [so...]
    unnamed x18 -> x10, local copies, waits for them, and re-layouts: 6.65 us -> 1.35 us
    all_to_all x2 -> x1, starting transfers between devices: 7.09 us -> 3.72 us  [spread(): lax.all_to_all(pieces, 'seq', 0, 0, axis_index_groups=halves, tiled=True)]
    ppermute x1, starting transfers between devices: 0.01 us -> 1.96 us  [head_body(): came = lax.ppermute(sent, 'seq', partners)]
    all_to_all x2 -> x1, waiting for transfers between devices: 15.3 us -> 16.6 us  [spread(): lax.all_to_all(pieces, 'seq', 0, 0, axis_index_groups=halves, tiled=True)]
    ppermute x1, waiting for transfers between devices: 1.52 us -> 0.41 us  [head_body(): far = lax.ppermute(near, 'seq', partners)]
  transfers between devices with their start and end apart: 6 -> 5, of which waited for: 5 -> 4; matrix products, arithmetic and copies ran while one was open for 3% -> 2% of each run, Pallas kernels for 1% -> 2%
where the time goes in v4:
time: 92.8 us; the launch traced here: 92.2 us
  blocking collectives  33.6 us (36%)
  Pallas kernels  25.4 us (27%)
  waiting for transfers between devices  20.8 us (22%)
  starting transfers between devices  7.22 us (8%)
  local copies, waits for them, and re-layouts  2.71 us (3%)
  other arithmetic  1.24 us (1%)
    all_to_all x2, blocking collectives, spread(): lax.all_to_all(pieces, 'seq', 0, 0, axis_index_groups=halves, tiled=True)  33.6 us
    pallas_call x6, Pallas kernels, whole_call(): pl.pallas_call(kernel, out_shape=outputs, in_specs=[SMEM] * scalars + [so...  25.4 us
    all_to_all x1, waiting for transfers between devices, spread(): lax.all_to_all(pieces, 'seq', 0, 0, axis_index_groups=halves, tiled=True)  16.6 us
    all_to_all x1, starting transfers between devices, spread(): lax.all_to_all(pieces, 'seq', 0, 0, axis_index_groups=halves, tiled=True)  3.72 us
    ppermute x1, waiting for transfers between devices, head_body(): far_rel = lax.ppermute(far_rel, 'head', [(0, 1), (1, 0)])  2.44 us
    ppermute x1, starting transfers between devices, head_body(): came = lax.ppermute(sent, 'seq', partners)  1.96 us
  transfers between devices with their start and end apart: 5, of which 4 were waited for; matrix products, arithmetic and copies ran while one was open for 2% of the time, Pallas kernels for 2%

profile of v4, /device:TPU:0, one launch (start us, length us, event | category | flops | bytes accessed | tf_op | source)
XLA Modules:
  0.0 92.2 jit_solution(18020713842578761179)
XLA Ops:
  0.6 2.1 %shard_map.136 = bf16[8,128,256]{2,1,0:T(8,128)(2,1)} custom-call(bf16[128,512]{1,0:T(8,128)(2,1)} %q_ref.1, bf16[128,512]{1,0:T(8,128)(2,1)} %g_ref.1, bf16[128,512]{1,0:T(8,128)(2,1)} %k_ref.1, bf16[128,512]{1,0:T(8,128)(2,1)} %v_ref.1), custom_call_target="tpu_custom_call" | custom-call | tf_op jit(solution)/shard_map/pallas_call | solution.py:555
  2.7 0.0 copy-start
  2.7 22.0 %all_to_all.15.own_ref = bf16[8,128,256]{2,1,0:T(8,128)(2,1)S(1)} all-to-all(bf16[8,128,256]{2,1,0:T(8,128)(2,1)} %shard_map.136), channel_id=1, replica_groups={{0,4,8,12,16,20,24,28},{2,6,10,14,18,22,26,30},{1,5,9,13,17,21,25,29},{..., dimensions={0} | all-to-all | bytes 1048576 | tf_op jit(solution)/shard_map/all_to_all | solution.py:581
  24.7 0.7 copy-done.4
  25.4 0.1 rev.4
  25.4 1.2 %constant_dynamic-slice_fusion.1 = (bf16[1024,64]{1,0:T(8,128)(2,1)S(1)}, bf16[1024,64]{1,0:T(8,128)(2,1)S(1)}) fusion(bf16[1024,512]{1,0:T(8,128)(2,1)} %wq_ref.1, s32[]{:T(128)S(6)} %select_n.28, bf16[1024,512]{1,0:T(8,128)(2,1)} %wk_ref.1), kind=kLoop, calls=%fused_computation.11 | loop fusion | bytes 524292 | tf_op jit(solution)/shard_map/dynamic_slice | solution.py:602
  26.7 0.5 fusion.pos_ref
  27.2 0.5 shard_map.137
  27.8 0.0 copy-start.3
  27.8 0.6 copy-done.3
  28.4 19.7 %shard_map.138 = (bf16[1536,128]{1,0:T(8,128)(2,1)S(1)}, f32[8,128,128]{2,1,0:T(8,128)S(1)}, bf16[512,128]{1,0:T(8,128)(2,1)S(1)}, bf16[8,64,128]{2,1,0:T(8,128)(2,1)S(1)}) custom-call(s32[8]{0:T(128)S(1)} %copy-done.3, s32[1]{0:T(128)} %bitcast.half_ref, bf16[8,128,256]{2,1,0:T(8,128)(2,1)S(1)} %all_to_all.15.own_ref, ...), custom_call_target="tpu_custom_call" | custom-call | tf_op jit(solution)/shard_map/pallas_call | solution.py:555
  48.1 2.0 %collective-permute-start.1 = (bf16[1536,128]{1,0:T(8,128)(2,1)S(1)}, bf16[1536,128]{1,0:T(8,128)(2,1)S(1)}, u32[]{:S(2)}, u32[]{:S(2)}) collective-permute-start(bf16[1536,128]{1,0:T(8,128)(2,1)S(1)} %get-tuple-element.26), channel_id=1, source_target_pairs={{0,2},{2,0},{4,6},{6,4},{8,10},{10,8},{12,14},{14,12},{16,18},{18,... | collective-permute-start | bytes 1179656 | tf_op jit(solution)/shard_map/ppermute | solution.py:648
  50.1 1.3 %collective-permute-done.1.came_ref = bf16[1536,128]{1,0:T(8,128)(2,1)S(1)} collective-permute-done((bf16[1536,128]{1,0:T(8,128)(2,1)S(1)}, bf16[1536,128]{1,0:T(8,128)(2,1)S(1)}, u32[]{:S(2)}, u32[]{:S(2)}) %collective-permute-start.1) | collective-permute-done | bytes 393248 | tf_op jit(solution)/shard_map/ppermute | solution.py:648
  51.4 1.3 %shard_map.139 = bf16[8,288,128]{2,1,0:T(8,128)(2,1)} custom-call(s32[1]{0:T(128)} %bitcast.half_ref, f32[8,128,128]{2,1,0:T(8,128)S(1)} %get-tuple-element.23.keep_ref, bf16[512,128]{1,0:T(8,128)(2,1)S(1)} %get-tuple-element.24.bucket_ref, bf16[8,64,128]{2,1,0:T(8,128)(2,1)S(1)} %get-tuple-element.25.query_ref, ...), custom_call_target="tpu_custom_call" | custom-call | tf_op jit(solution)/shard_map/pallas_call | solution.py:555
  52.7 3.7 %all-to-all-start.1 = ((bf16[8,288,128]{2,1,0:T(8,128)(2,1)}), bf16[8,288,128]{2,1,0:T(8,128)(2,1)S(1)}, u32[]{:S(2)}, u32[]{:S(2)}) async-start(bf16[8,288,128]{2,1,0:T(8,128)(2,1)} %shard_map.139), calls=%async_computation.1 | async-start | bytes 1179648 | tf_op jit(solution)/shard_map/all_to_all | solution.py:581
  56.5 16.6 %all-to-all-done.1.got_ref = bf16[8,288,128]{2,1,0:T(8,128)(2,1)S(1)} async-done(((bf16[8,288,128]{2,1,0:T(8,128)(2,1)}), bf16[8,288,128]{2,1,0:T(8,128)(2,1)S(1)}, u32[]{:S(2)}, u32[]{:S(2)}) %all-to-all-start.1) | async-done | bytes 589856 | tf_op jit(solution)/shard_map/all_to_all | solution.py:581
  73.1 0.7 shard_map.141
  73.8 1.5 %collective-permute-start.2 = (bf16[32,512]{1,0:T(8,128)(2,1)S(1)}, bf16[32,512]{1,0:T(8,128)(2,1)S(1)}, u32[]{:S(2)}, u32[]{:S(2)}) collective-permute-start(bf16[32,512]{1,0:T(8,128)(2,1)S(1)} %constant_dynamic-slice_fusion), channel_id=1, source_target_pairs={{0,1},{1,0},{2,3},{3,2},{4,5},{5,4},{6,7},{7,6},{8,9},{9,8},{10,11... | collective-permute-start | bytes 98312 | tf_op jit(solution)/shard_map/ppermute | solution.py:665
  75.3 2.4 %collective-permute-done.2 = bf16[32,512]{1,0:T(8,128)(2,1)S(1)} collective-permute-done((bf16[32,512]{1,0:T(8,128)(2,1)S(1)}, bf16[32,512]{1,0:T(8,128)(2,1)S(1)}, u32[]{:S(2)}, u32[]{:S(2)}) %collective-permute-start.2) | collective-permute-done | bytes 32800 | tf_op jit(solution)/shard_map/ppermute | solution.py:665
  77.8 11.6 %all_to_all.16 = bf16[8,32,512]{2,1,0:T(8,128)(2,1)S(1)} all-to-all(bf16[8,32,512]{2,1,0:T(8,128)(2,1)S(1)} %broadcast_in_dim.2), channel_id=1, replica_groups={{0,4,8,12,16,20,24,28},{2,6,10,14,18,22,26,30},{1,5,9,13,17,21,25,29},{..., dimensions={0} | all-to-all | bytes 524288 | tf_op jit(solution)/shard_map/all_to_all | solution.py:581
  89.5 1.1 %shard_map.140 = (bf16[128,512]{1,0:T(8,128)(2,1)}, bf16[128,512]{1,0:T(8,128)(2,1)}, bf16[128,512]{1,0:T(8,128)(2,1)}, f32[64,512]{1,0:T(8,128)}, f32[64,512]{1,0:T(8,128)}) custom-call(bf16[8,288,128]{2,1,0:T(8,128)(2,1)S(1)} %all-to-all-done.1.got_ref), custom_call_target="tpu_custom_call" | custom-call | tf_op jit(solution)/shard_map/pallas_call | solution.py:555
  90.6 0.4 collective-permute-done.3
  91.0 0.1 pad_maximum_fusion
  91.1 1.1 %bitcast_convert_fusion = f32[512,512]{1,0:T(8,128)} fusion(bf16[8,2,32,512]{3,2,1,0:T(8,128)(2,1)S(1)} %pad_maximum_fusion), kind=kLoop, calls=%fused_computation.3 | loop fusion | flops 262144 | bytes 1572864 | tf_op jit(solution)/shard_map/convert_element_type | solution.py:671
  (13 shorter events, 0.1 us)
Async XLA Ops:
  2.7 24.0 %copy-start = (bf16[512,1024]{1,0:T(8,128)(2,1)S(1)}, bf16[512,1024]{1,0:T(8,128)(2,1)}, u32[]{:S(2)}) copy-start(bf16[512,1024]{1,0:T(8,128)(2,1)} %rel_ref.1) | copy-start | bytes 3145732
  24.7 3.1 %collective-permute-start = (bf16[8,128,256]{2,1,0:T(8,128)(2,1)S(1)}, bf16[8,128,256]{2,1,0:T(8,128)(2,1)S(1)}, u32[]{:S(2)}, u32[]{:S(2)}) collective-permute-start(bf16[8,128,256]{2,1,0:T(8,128)(2,1)S(1)} %all_to_all.15.own_ref), channel_id=1, source_target_pairs={{0,2},{2,0},{4,6},{6,4},{8,10},{10,8},{12,14},{14,12},{16,18},{18,... | collective-permute-start | bytes 1572872 | tf_op jit(solution)/shard_map/ppermute | solution.py:598
  24.7 0.7 copy-start.4
  27.8 0.7 copy-start.3
  48.1 3.3 %collective-permute-start.1 = (bf16[1536,128]{1,0:T(8,128)(2,1)S(1)}, bf16[1536,128]{1,0:T(8,128)(2,1)S(1)}, u32[]{:S(2)}, u32[]{:S(2)}) collective-permute-start(bf16[1536,128]{1,0:T(8,128)(2,1)S(1)} %get-tuple-element.26), channel_id=1, source_target_pairs={{0,2},{2,0},{4,6},{6,4},{8,10},{10,8},{12,14},{14,12},{16,18},{18,... | collective-permute-start | bytes 1179656 | tf_op jit(solution)/shard_map/ppermute | solution.py:648
  51.4 21.6 %copy-start.2 = (bf16[1024,512]{1,0:T(8,128)(2,1)S(1)}, bf16[1024,512]{1,0:T(8,128)(2,1)}, u32[]{:S(2)}) copy-start(bf16[1024,512]{1,0:T(8,128)(2,1)} %wk_ref.1) | copy-start | bytes 3145732
  52.7 20.3 %copy-start.1 = (bf16[1024,512]{1,0:T(8,128)(2,1)S(1)}, bf16[1024,512]{1,0:T(8,128)(2,1)}, u32[]{:S(2)}) copy-start(bf16[1024,512]{1,0:T(8,128)(2,1)} %wq_ref.1) | copy-start | bytes 3145732
  52.7 20.3 %all-to-all-start.1 = ((bf16[8,288,128]{2,1,0:T(8,128)(2,1)}), bf16[8,288,128]{2,1,0:T(8,128)(2,1)S(1)}, u32[]{:S(2)}, u32[]{:S(2)}) async-start(bf16[8,288,128]{2,1,0:T(8,128)(2,1)} %shard_map.139), calls=%async_computation.1 | async-start | bytes 1179648 | tf_op jit(solution)/shard_map/all_to_all | solution.py:581
  73.8 4.0 %collective-permute-start.2 = (bf16[32,512]{1,0:T(8,128)(2,1)S(1)}, bf16[32,512]{1,0:T(8,128)(2,1)S(1)}, u32[]{:S(2)}, u32[]{:S(2)}) collective-permute-start(bf16[32,512]{1,0:T(8,128)(2,1)S(1)} %constant_dynamic-slice_fusion), channel_id=1, source_target_pairs={{0,1},{1,0},{2,3},{3,2},{4,5},{5,4},{6,7},{7,6},{8,9},{9,8},{10,11... | collective-permute-start | bytes 98312 | tf_op jit(solution)/shard_map/ppermute | solution.py:665
  89.5 1.5 %collective-permute-start.3 = (bf16[8,32,512]{2,1,0:T(8,128)(2,1)S(1)}, bf16[8,32,512]{2,1,0:T(8,128)(2,1)S(1)}, u32[]{:S(2)}, u32[]{:S(2)}) collective-permute-start(bf16[8,32,512]{2,1,0:T(8,128)(2,1)S(1)} %all_to_all.16), channel_id=1, source_target_pairs={{0,2},{2,0},{4,6},{6,4},{8,10},{10,8},{12,14},{14,12},{16,18},{18,... | collective-permute-start | bytes 786440 | tf_op jit(solution)/shard_map/ppermute | solution.py:668

commit v5 on v4

--- a/solution.py
+++ b/solution.py
@@ -289,8 +289,12 @@
     both[valid0 : valid0 + valid, :] = expanded.astype(F32).T.astype(BF)
 
 
+def cut_kernel(own_ref, onehot, pk, pq, rows_ref, out_ref):
+    out_ref[...] = own_ref[:, :, 2 * HD :]
+
+
 def head_kernel(
-    lens_ref, half_ref, own_ref, other_ref, onehot, pk, pq, rows_ref,
+    scalars_ref, own_ref, other_ref, onehot, pk, pq, rows_ref,
     send_ref, keep_ref, bucket_ref, query_ref,
     kvs, acc, acc_pos, g_key, g_query, k_t, k_rev, s_q, st, dp, dtile, pairs, dq_nat, dq_pos,
 ):
@@ -301,12 +305,12 @@
     longest = 2 * halo + 1
     scale = 1.0 / math.sqrt(3.0 * HD)
     valid0 = (halo + 1) * TILE
-    half = half_ref[0]
-    docs = lens_ref.shape[0]
+    docs = scalars_ref.shape[0] - 1
+    half = scalars_ref[docs]
     row, col = grid_of((TILE, TILE))
     swap = jnp.where(row + col == TILE - 1, 1.0, 0.0).astype(BF)
     wrap = row + col >= TILE - 1
-    wrap_rev = col >= row
+    keep = jnp.where(col >= row, 1.0, 0.0).astype(BF)
     low = col < HD
     acc[...] = jnp.zeros_like(acc)
     acc_pos[...] = jnp.zeros_like(acc_pos)
@@ -314,8 +318,10 @@
     g_query[...] = jnp.zeros_like(g_query)
 
     def transpose_tile(b, carry):
-        for ref, tile in ((own_ref, 2 * b + half), (other_ref, 2 * b + 1 - half)):
-            kv = ref[b, :, 2 * HD : 4 * HD]
+        for kv, tile in (
+            (own_ref[b, :, 2 * HD : 4 * HD], 2 * b + half),
+            (other_ref[b], 2 * b + 1 - half),
+        ):
             kvs[tile] = kv
             turned = kv.astype(F32).T.astype(BF)
             k_t[tile] = turned[:HD]
@@ -330,8 +336,8 @@
 
         def next_end(d, state):
             end, start, stop = state
-            stop = jnp.where(end < token + TILE, end + lens_ref[d], stop)
-            end = end + lens_ref[d]
+            stop = jnp.where(end < token + TILE, end + scalars_ref[d], stop)
+            end = end + scalars_ref[d]
             start = jnp.where(end <= token, end, start)
             return (end, start, stop)
 
@@ -366,8 +372,8 @@
 
         def next_doc(d, state):
             end, start, stop = state
-            stop = jnp.where(end <= position, end + lens_ref[d], stop)
-            end = end + lens_ref[d]
+            stop = jnp.where(end <= position, end + scalars_ref[d], stop)
+            end = end + scalars_ref[d]
             start = jnp.where(end <= position, end, start)
             return (end, start, stop)
 
@@ -403,8 +409,8 @@
                 stride_axis=0,
             )
             score = both[:, :TILE] + key_term + query_term.T
-            place = row + t * TILE
-            score = jnp.where((place >= start) & (place < stop), score, masked_score)
+            inside = (row >= start - t * TILE) & (row < stop - t * TILE)
+            score = jnp.where(inside, score, masked_score)
             st[t] = score
             dp[t] = both[:, TILE:]
             best = jnp.maximum(best, jnp.max(score.reshape(TILE // 8, 8, TILE), 0))
@@ -412,7 +418,7 @@
         total = jnp.zeros((8, TILE), F32)
         dot = jnp.zeros((8, TILE), F32)
         for t in range(span):
-            expd = jnp.exp((st[t] - top) * scale)
+            expd = jnp.exp2((st[t] - top) * (scale * math.log2(math.e)))
             st[t] = expd
             total = total + jnp.sum(expd.reshape(TILE // 8, 8, TILE), 0)
             dot = dot + jnp.sum((expd * dp[t]).reshape(TILE // 8, 8, TILE), 0)
@@ -422,7 +428,7 @@
         lows = jnp.where(low, qd, jnp.zeros_like(qd))
         pair = jnp.concatenate([lows, jnp.where(low, jnp.zeros_like(qd), qd)], 0)
         dq_t = jnp.zeros((HD, TILE), F32)
-        before = jnp.zeros((TILE, TILE), F32)
+        before = jnp.zeros((TILE, TILE), BF)
         ahead_part = None
         for t in range(span):
             prob = st[t] * inverse
@@ -432,8 +438,9 @@
             dq_t = dq_t + stacked[:HD]
             query_x = pl.multiple_of(2 * halo * TILE + delta - t * TILE, TILE)
             y = pltpu.roll(stacked[HD:], 0, 1, stride=1, stride_axis=0)
-            near = jnp.where(wrap_rev, y, 0.0).astype(BF)
-            far = jnp.where(wrap_rev, 0.0, y).astype(BF)
+            y = y.astype(BF)
+            near = y * keep
+            far = y - near
             back = nn(jnp.concatenate([near, far], 1), rows_ref[pl.ds(query_x, 2 * TILE), :])
             acc_pos[first + t] += back[:, HD:]
             turned_keys = k_rev[first + t]
@@ -447,13 +454,15 @@
                 )
             ahead_part = (turned_keys, near)
             z = pltpu.roll(nt(swap, dscore), 0, 1, stride=1, stride_axis=0)
-            dtile[:, t * TILE : (t + 1) * TILE] = jnp.where(wrap_rev, z, before).astype(BF)
-            before = z
+            z = z.astype(BF)
+            here = z * keep
+            dtile[:, t * TILE : (t + 1) * TILE] = here + before
+            before = z - here
         g_query[:, pl.ds(query_x, TILE)] += nn(*ahead_part)
         acc[pl.ds(first, span)] += nn(
             pairs[0:span].reshape(span * TILE, 2 * TILE), pair
         ).reshape(span, TILE, 2 * HD)
-        dtile[:, span * TILE : (span + 1) * TILE] = jnp.where(wrap_rev, 0.0, before).astype(BF)
+        dtile[:, span * TILE : (span + 1) * TILE] = before
         spread_q = dtile[:, 0 : (span + 1) * TILE]
         window = pl.ds(key_x, (span + 1) * TILE)
         g_key[:, window] += nn(q_rev, spread_q)
@@ -518,6 +527,15 @@
         out_ref[b, base_b:, :] = bucket[pl.ds(tile * b_rows, b_rows), :].astype(BF)
 
 
+def weave_kernel(half_ref, near_ref, far_ref, out_ref):
+    shards, rows, _ = near_ref.shape
+    half = half_ref[0]
+    for shard in range(shards):
+        for ref, place in ((near_ref, half), (far_ref, 1 - half)):
+            start = pl.multiple_of((2 * shard + place) * rows, rows)
+            out_ref[pl.ds(start, rows), :] = ref[shard].astype(F32)
+
+
 def rel_kernel(got_ref, wk_ref, wq_ref, rel_ref):
     heads = range(got_ref.shape[0])
     base_b = got_ref.shape[1] - rel_ref.shape[0]
@@ -595,7 +613,6 @@
         limit=64,
     )
     own = spread(packed)
-    other = lax.ppermute(own, "seq", partners)
     w_own = jnp.concatenate(
         [
             lax.dynamic_slice_in_dim(w_key, mine * HD, HD, 1),
@@ -618,9 +635,14 @@
             shape((line, 2 * HD), BF),
         ],
     )
+    other = lax.ppermute(
+        whole_call(cut_kernel, (own, *tables), shape((heads, tokens_dev, 2 * HD), BF)),
+        "seq",
+        partners,
+    )
     sent, kept, bucket, query = whole_call(
         head_kernel,
-        (doc_lengths, half, own, other, *tables),
+        (jnp.concatenate([doc_lengths, half]), own, other, *tables),
         [
             shape((heads * TILE + buckets, 2 * HD), BF),
             shape((heads, TILE, 2 * HD), F32),
@@ -643,7 +665,7 @@
             vm((heads, HD, TILE), F32),
             vm((heads, TILE, 2 * HD), BF),
         ],
-        scalars=2,
+        scalars=1,
     )
     came = lax.ppermute(sent, "seq", partners)
     joined = whole_call(
@@ -666,9 +688,9 @@
     rel_own = (mine_rel.astype(F32) + far_rel.astype(F32)).astype(BF)
     near = spread(jnp.broadcast_to(rel_own[None], (heads, b_rows, width)))
     far = lax.ppermute(near, "seq", partners)
-    even = jnp.where(half[0] == 0, near, far)
-    odd = jnp.where(half[0] == 0, far, near)
-    rel_emb_grad = jnp.stack([even, odd], 1).reshape(buckets, width).astype(F32)
+    rel_emb_grad = whole_call(
+        weave_kernel, (half, near, far), shape((buckets, width), F32), scalars=1
+    )
     query_grad, key_grad, value_grad, w_query_grad, w_key_grad = whole_call(
         unpack_kernel, (returned,), [tokens, tokens, tokens, weights, weights]
     )

time: 92.8 us -> 91.8 us (0.989)
  blocking collectives: 33.6 us -> 11.6 us
  waiting for transfers between devices: 20.8 us -> 31.5 us
  starting transfers between devices: 7.22 us -> 12.9 us
  local copies, waits for them, and re-layouts: 2.71 us -> 6.38 us
  Pallas kernels: 25.4 us -> 27.2 us
  other arithmetic: 1.24 us -> 0.09 us
    all_to_all x2 -> x1, blocking collectives: 33.6 us -> 11.6 us  [spread(): lax.all_to_all(pieces, 'seq', 0, 0, axis_index_groups=halves, tiled=True)]
    all_to_all x1 -> x2, waiting for transfers between devices: 16.6 us -> 26 us  [spread(): lax.all_to_all(pieces, 'seq', 0, 0, axis_index_groups=halves, tiled=True)]
    all_to_all x1 -> x2, starting transfers between devices: 3.72 us -> 11.2 us  [spread(): lax.all_to_all(pieces, 'seq', 0, 0, axis_index_groups=halves, tiled=True)]
    unnamed x10 -> x18, local copies, waits for them, and re-layouts: 1.35 us -> 5.03 us
    ppermute x1, starting transfers between devices: 1.96 us -> 0.07 us  [head_body(): came = lax.ppermute(sent, 'seq', partners)]
    pallas_call x6 -> x8, Pallas kernels: 25.4 us -> 27.2 us  [whole_call(): pl.pallas_call(kernel, out_shape=outputs, in_specs=[SMEM] * scalars + [so...]
    convert_element_type x1 -> x0, other arithmetic: 1.14 us -> none  [head_body(): rel_emb_grad = jnp.stack([even, odd], 1).reshape(buckets, width).astype(F32)]
  transfers between devices with their start and end apart: 5 -> 6, of which waited for: 4 -> 6; matrix products, arithmetic and copies ran while one was open for 2% -> 2% of each run, Pallas kernels for 2% -> 2%
where the time goes in v5:
time: 91.8 us; the launch traced here: 90.9 us
  waiting for transfers between devices  31.5 us (34%)
  Pallas kernels  27.2 us (30%)
  starting transfers between devices  12.9 us (14%)
  blocking collectives  11.6 us (13%)
  local copies, waits for them, and re-layouts  6.38 us (7%)
    pallas_call x8, Pallas kernels, whole_call(): pl.pallas_call(kernel, out_shape=outputs, in_specs=[SMEM] * scalars + [so...  27.2 us
    all_to_all x2, waiting for transfers between devices, spread(): lax.all_to_all(pieces, 'seq', 0, 0, axis_index_groups=halves, tiled=True)  26 us
    all_to_all x1, blocking collectives, spread(): lax.all_to_all(pieces, 'seq', 0, 0, axis_index_groups=halves, tiled=True)  11.6 us
    all_to_all x2, starting transfers between devices, spread(): lax.all_to_all(pieces, 'seq', 0, 0, axis_index_groups=halves, tiled=True)  11.2 us
    unnamed x18, local copies, waits for them, and re-layouts  5.03 us
    ppermute x1, waiting for transfers between devices, head_body(): far_rel = lax.ppermute(far_rel, 'head', [(0, 1), (1, 0)])  2.42 us
  transfers between devices with their start and end apart: 6, of which 6 were waited for; matrix products, arithmetic and copies ran while one was open for 2% of the time, Pallas kernels for 2%

profile of v5, /device:TPU:0, one launch (start us, length us, event | category | flops | bytes accessed | tf_op | source)
XLA Modules:
  0.0 90.9 jit_solution(14400546704437113123)
XLA Ops:
  0.6 2.1 %shard_map.136 = bf16[8,128,256]{2,1,0:T(8,128)(2,1)} custom-call(bf16[128,512]{1,0:T(8,128)(2,1)} %q_ref.1, bf16[128,512]{1,0:T(8,128)(2,1)} %g_ref.1, bf16[128,512]{1,0:T(8,128)(2,1)} %k_ref.1, bf16[128,512]{1,0:T(8,128)(2,1)} %v_ref.1), custom_call_target="tpu_custom_call" | custom-call | tf_op jit(solution)/shard_map/pallas_call | solution.py:573
  2.7 7.4 %all-to-all-start = ((bf16[8,128,256]{2,1,0:T(8,128)(2,1)}), bf16[8,128,256]{2,1,0:T(8,128)(2,1)S(1)}, u32[]{:S(2)}, u32[]{:S(2)}) async-start(bf16[8,128,256]{2,1,0:T(8,128)(2,1)} %shard_map.136), calls=%async_computation | async-start | bytes 1048576 | tf_op jit(solution)/shard_map/all_to_all | solution.py:599
  10.2 0.7 copy-done.7
  10.9 1.2 %constant_dynamic-slice_fusion.1 = (bf16[1024,64]{1,0:T(8,128)(2,1)S(1)}, bf16[1024,64]{1,0:T(8,128)(2,1)S(1)}) fusion(bf16[1024,512]{1,0:T(8,128)(2,1)} %wq_ref.1, s32[]{:T(128)S(6)} %select_n.16, bf16[1024,512]{1,0:T(8,128)(2,1)} %wk_ref.1), kind=kLoop, calls=%fused_computation.7 | loop fusion | bytes 524292 | tf_op jit(solution)/shard_map/dynamic_slice | solution.py:619
  12.2 0.5 fusion.pos_ref
  12.7 0.5 shard_map.137
  13.3 0.8 copy-done.1
  14.1 0.8 copy-done.3
  14.9 9.7 %all-to-all-done.own_ref = bf16[8,128,256]{2,1,0:T(8,128)(2,1)S(1)} async-done(((bf16[8,128,256]{2,1,0:T(8,128)(2,1)}), bf16[8,128,256]{2,1,0:T(8,128)(2,1)S(1)}, u32[]{:S(2)}, u32[]{:S(2)}) %all-to-all-start) | async-done | bytes 524320 | tf_op jit(solution)/shard_map/all_to_all | solution.py:599
  24.7 1.1 %copy-done.2 = bf16[128,2304]{1,0:T(8,128)(2,1)S(1)} copy-done((bf16[128,2304]{1,0:T(8,128)(2,1)S(1)}, bf16[128,2304]{1,0:T(8,128)(2,1)}, u32[]{:S(2)}) %copy-start.2) | copy-done | bytes 589848
  25.7 1.1 %copy-done.4 = bf16[2304,128]{1,0:T(8,128)(2,1)S(1)} copy-done((bf16[2304,128]{1,0:T(8,128)(2,1)S(1)}, bf16[2304,128]{1,0:T(8,128)(2,1)}, u32[]{:S(2)}) %copy-start.4) | copy-done | bytes 589848
  26.9 0.6 copy-done.8
  27.6 0.9 collective-permute-done.other_ref
  28.5 20.3 %shard_map.139 = (bf16[1536,128]{1,0:T(8,128)(2,1)S(1)}, f32[8,128,128]{2,1,0:T(8,128)S(1)}, bf16[512,128]{1,0:T(8,128)(2,1)S(1)}, bf16[8,64,128]{2,1,0:T(8,128)(2,1)S(1)}) custom-call(s32[9]{0:T(128)S(1)} %pad_add_fusion.scalars_ref, bf16[8,128,256]{2,1,0:T(8,128)(2,1)S(1)} %all-to-all-done.own_ref, ...), custom_call_target="tpu_custom_call" | custom-call | tf_op jit(solution)/shard_map/pallas_call | solution.py:573
  48.9 1.7 %collective-permute-done.1.came_ref = bf16[1536,128]{1,0:T(8,128)(2,1)S(1)} collective-permute-done((bf16[1536,128]{1,0:T(8,128)(2,1)S(1)}, bf16[1536,128]{1,0:T(8,128)(2,1)S(1)}, u32[]{:S(2)}, u32[]{:S(2)}) %collective-permute-start.1) | collective-permute-done | bytes 393248 | tf_op jit(solution)/shard_map/ppermute | solution.py:670
  50.6 1.3 %shard_map.140 = bf16[8,288,128]{2,1,0:T(8,128)(2,1)} custom-call(s32[1]{0:T(128)} %bitcast.half_ref, f32[8,128,128]{2,1,0:T(8,128)S(1)} %get-tuple-element.23.keep_ref, bf16[512,128]{1,0:T(8,128)(2,1)S(1)} %get-tuple-element.24.bucket_ref, bf16[8,64,128]{2,1,0:T(8,128)(2,1)S(1)} %get-tuple-element.25.query_ref, ...), custom_call_target="tpu_custom_call" | custom-call | tf_op jit(solution)/shard_map/pallas_call | solution.py:573
  51.9 3.8 %all-to-all-start.1 = ((bf16[8,288,128]{2,1,0:T(8,128)(2,1)}), bf16[8,288,128]{2,1,0:T(8,128)(2,1)S(1)}, u32[]{:S(2)}, u32[]{:S(2)}) async-start(bf16[8,288,128]{2,1,0:T(8,128)(2,1)} %shard_map.140), calls=%async_computation.1 | async-start | bytes 1179648 | tf_op jit(solution)/shard_map/all_to_all | solution.py:599
  55.7 16.3 %all-to-all-done.1.got_ref = bf16[8,288,128]{2,1,0:T(8,128)(2,1)S(1)} async-done(((bf16[8,288,128]{2,1,0:T(8,128)(2,1)}), bf16[8,288,128]{2,1,0:T(8,128)(2,1)S(1)}, u32[]{:S(2)}, u32[]{:S(2)}) %all-to-all-start.1) | async-done | bytes 589856 | tf_op jit(solution)/shard_map/all_to_all | solution.py:599
  72.0 0.7 shard_map.142
  72.7 1.6 %collective-permute-start.2 = (bf16[32,512]{1,0:T(8,128)(2,1)S(1)}, bf16[32,512]{1,0:T(8,128)(2,1)S(1)}, u32[]{:S(2)}, u32[]{:S(2)}) collective-permute-start(bf16[32,512]{1,0:T(8,128)(2,1)S(1)} %constant_dynamic-slice_fusion), channel_id=1, source_target_pairs={{0,1},{1,0},{2,3},{3,2},{4,5},{5,4},{6,7},{7,6},{8,9},{9,8},{10,11... | collective-permute-start | bytes 98312 | tf_op jit(solution)/shard_map/ppermute | solution.py:687
  74.3 2.4 %collective-permute-done.2 = bf16[32,512]{1,0:T(8,128)(2,1)S(1)} collective-permute-done((bf16[32,512]{1,0:T(8,128)(2,1)S(1)}, bf16[32,512]{1,0:T(8,128)(2,1)S(1)}, u32[]{:S(2)}, u32[]{:S(2)}) %collective-permute-start.2) | collective-permute-done | bytes 32800 | tf_op jit(solution)/shard_map/ppermute | solution.py:687
  76.7 11.6 %all_to_all.15.near_ref = bf16[8,32,512]{2,1,0:T(8,128)(2,1)S(1)} all-to-all(bf16[8,32,512]{2,1,0:T(8,128)(2,1)S(1)} %broadcast_in_dim.2), channel_id=1, replica_groups={{0,4,8,12,16,20,24,28},{2,6,10,14,18,22,26,30},{1,5,9,13,17,21,25,29},{..., dimensions={0} | all-to-all | bytes 524288 | tf_op jit(solution)/shard_map/all_to_all | solution.py:599
  88.4 1.1 %shard_map.141 = (bf16[128,512]{1,0:T(8,128)(2,1)}, bf16[128,512]{1,0:T(8,128)(2,1)}, bf16[128,512]{1,0:T(8,128)(2,1)}, f32[64,512]{1,0:T(8,128)}, f32[64,512]{1,0:T(8,128)}) custom-call(bf16[8,288,128]{2,1,0:T(8,128)(2,1)S(1)} %all-to-all-done.1.got_ref), custom_call_target="tpu_custom_call" | custom-call | tf_op jit(solution)/shard_map/pallas_call | solution.py:573
  89.9 1.0 %shard_map.143 = f32[512,512]{1,0:T(8,128)} custom-call(s32[1]{0:T(128)} %bitcast.half_ref, bf16[8,32,512]{2,1,0:T(8,128)(2,1)S(1)} %all_to_all.15.near_ref, bf16[8,32,512]{2,1,0:T(8,128)(2,1)S(1)} %collective-permute-done.3.far_ref), custom_call_target="tpu_custom_call" | custom-call | tf_op jit(solution)/shard_map/pallas_call | solution.py:573
  (22 shorter events, 0.8 us)
Async XLA Ops:
  2.7 9.5 %copy-start = (bf16[512,1024]{1,0:T(8,128)(2,1)S(1)}, bf16[512,1024]{1,0:T(8,128)(2,1)}, u32[]{:S(2)}) copy-start(bf16[512,1024]{1,0:T(8,128)(2,1)} %rel_ref.1) | copy-start | bytes 3145732
  2.7 21.9 %all-to-all-start = ((bf16[8,128,256]{2,1,0:T(8,128)(2,1)}), bf16[8,128,256]{2,1,0:T(8,128)(2,1)S(1)}, u32[]{:S(2)}, u32[]{:S(2)}) async-start(bf16[8,128,256]{2,1,0:T(8,128)(2,1)} %shard_map.136), calls=%async_computation | async-start | bytes 1048576 | tf_op jit(solution)/shard_map/all_to_all | solution.py:599
  10.2 0.7 copy-start.7
  13.3 0.8 copy-start.1
  14.1 0.8 copy-start.3
  24.7 1.1 %copy-start.2 = (bf16[128,2304]{1,0:T(8,128)(2,1)S(1)}, bf16[128,2304]{1,0:T(8,128)(2,1)}, u32[]{:S(2)}) copy-start(bf16[128,2304]{1,0:T(8,128)(2,1)} %copy-done.1) | copy-start | bytes 1769476
  25.7 1.1 %copy-start.4 = (bf16[2304,128]{1,0:T(8,128)(2,1)S(1)}, bf16[2304,128]{1,0:T(8,128)(2,1)}, u32[]{:S(2)}) copy-start(bf16[2304,128]{1,0:T(8,128)(2,1)} %copy-done.3) | copy-start | bytes 1769476
  26.8 0.7 copy-start.8
  26.8 1.6 %collective-permute-start = (bf16[8,128,128]{2,1,0:T(8,128)(2,1)S(1)}, bf16[8,128,128]{2,1,0:T(8,128)(2,1)S(1)}, u32[]{:S(2)}, u32[]{:S(2)}) collective-permute-start(bf16[8,128,128]{2,1,0:T(8,128)(2,1)S(1)} %shard_map.138), channel_id=1, source_target_pairs={{0,2},{2,0},{4,6},{6,4},{8,10},{10,8},{12,14},{14,12},{16,18},{18,... | collective-permute-start | bytes 786440 | tf_op jit(solution)/shard_map/ppermute | solution.py:638
  48.8 1.8 %collective-permute-start.1 = (bf16[1536,128]{1,0:T(8,128)(2,1)S(1)}, bf16[1536,128]{1,0:T(8,128)(2,1)S(1)}, u32[]{:S(2)}, u32[]{:S(2)}) collective-permute-start(bf16[1536,128]{1,0:T(8,128)(2,1)S(1)} %get-tuple-element.26), channel_id=1, source_target_pairs={{0,2},{2,0},{4,6},{6,4},{8,10},{10,8},{12,14},{14,12},{16,18},{18,... | collective-permute-start | bytes 1179656 | tf_op jit(solution)/shard_map/ppermute | solution.py:670
  50.6 21.4 %copy-start.6 = (bf16[1024,512]{1,0:T(8,128)(2,1)S(1)}, bf16[1024,512]{1,0:T(8,128)(2,1)}, u32[]{:S(2)}) copy-start(bf16[1024,512]{1,0:T(8,128)(2,1)} %wk_ref.1) | copy-start | bytes 3145732
  51.9 20.1 %copy-start.5 = (bf16[1024,512]{1,0:T(8,128)(2,1)S(1)}, bf16[1024,512]{1,0:T(8,128)(2,1)}, u32[]{:S(2)}) copy-start(bf16[1024,512]{1,0:T(8,128)(2,1)} %wq_ref.1) | copy-start | bytes 3145732
  51.9 20.1 %all-to-all-start.1 = ((bf16[8,288,128]{2,1,0:T(8,128)(2,1)}), bf16[8,288,128]{2,1,0:T(8,128)(2,1)S(1)}, u32[]{:S(2)}, u32[]{:S(2)}) async-start(bf16[8,288,128]{2,1,0:T(8,128)(2,1)} %shard_map.140), calls=%async_computation.1 | async-start | bytes 1179648 | tf_op jit(solution)/shard_map/all_to_all | solution.py:599
  72.7 4.0 %collective-permute-start.2 = (bf16[32,512]{1,0:T(8,128)(2,1)S(1)}, bf16[32,512]{1,0:T(8,128)(2,1)S(1)}, u32[]{:S(2)}, u32[]{:S(2)}) collective-permute-start(bf16[32,512]{1,0:T(8,128)(2,1)S(1)} %constant_dynamic-slice_fusion), channel_id=1, source_target_pairs={{0,1},{1,0},{2,3},{3,2},{4,5},{5,4},{6,7},{7,6},{8,9},{9,8},{10,11... | collective-permute-start | bytes 98312 | tf_op jit(solution)/shard_map/ppermute | solution.py:687
  88.4 1.5 %collective-permute-start.3 = (bf16[8,32,512]{2,1,0:T(8,128)(2,1)S(1)}, bf16[8,32,512]{2,1,0:T(8,128)(2,1)S(1)}, u32[]{:S(2)}, u32[]{:S(2)}) collective-permute-start(bf16[8,32,512]{2,1,0:T(8,128)(2,1)S(1)} %all_to_all.15.near_ref), channel_id=1, source_target_pairs={{0,2},{2,0},{4,6},{6,4},{8,10},{10,8},{12,14},{14,12},{16,18},{18,... | collective-permute-start | bytes 786440 | tf_op jit(solution)/shard_map/ppermute | solution.py:690

commit v6 on v5

--- a/solution.py
+++ b/solution.py
@@ -273,30 +273,23 @@
         store.wait()
 
 
-def table_kernel(pos_ref, table_ref, onehot, pk, pq, both):
+def table_kernel(scalars_ref, pos_ref, table_ref, onehot, expanded):
     buckets, valid = onehot.shape
-    valid0 = valid // 2 + TILE
     for part in range(buckets // TILE):
         ids = lax.broadcasted_iota(jnp.int32, (TILE, valid), 0) + part * TILE
         onehot[pl.ds(part * TILE, TILE), :] = jnp.where(ids == table_ref[...], 1.0, 0.0).astype(BF)
     pos_t = pos_ref[...].astype(F32).T.astype(BF)
-    expanded = nn(pos_t, onehot[...]).astype(BF)
-    pk[...] = jnp.zeros_like(pk)
-    pq[...] = jnp.zeros_like(pq)
-    pk[0:HD, valid0 : valid0 + valid] = expanded[:HD]
-    pq[0:HD, valid0 : valid0 + valid] = expanded[HD:]
-    both[...] = jnp.zeros_like(both)
-    both[valid0 : valid0 + valid, :] = expanded.astype(F32).T.astype(BF)
-
-
-def cut_kernel(own_ref, onehot, pk, pq, rows_ref, out_ref):
+    expanded[...] = nn(pos_t, onehot[...]).astype(BF)
+
+
+def cut_kernel(own_ref, expanded, out_ref):
     out_ref[...] = own_ref[:, :, 2 * HD :]
 
 
 def head_kernel(
-    scalars_ref, own_ref, other_ref, onehot, pk, pq, rows_ref,
+    scalars_ref, own_ref, other_ref, onehot, expanded,
     send_ref, keep_ref, bucket_ref, query_ref,
-    kvs, acc, acc_pos, g_key, g_query, k_t, k_rev, s_q, st, dp, dtile, pairs, dq_nat, dq_pos,
+    pk, pq, rows_ref, kvs, acc, acc_pos, g_key, g_query, k_t, k_rev, s_q, st, dp, dtile, pairs, dq_nat, dq_pos,
 ):
     blocks = own_ref.shape[0]
     tiles = 2 * blocks
@@ -312,6 +305,11 @@
     wrap = row + col >= TILE - 1
     keep = jnp.where(col >= row, 1.0, 0.0).astype(BF)
     low = col < HD
+    for table in (pk, pq, rows_ref):
+        table[...] = jnp.zeros_like(table)
+    pk[0:HD, valid0 : valid0 + valid] = expanded[:HD]
+    pq[0:HD, valid0 : valid0 + valid] = expanded[HD:]
+    rows_ref[valid0 : valid0 + valid, :] = expanded[...].astype(F32).T.astype(BF)
     acc[...] = jnp.zeros_like(acc)
     acc_pos[...] = jnp.zeros_like(acc_pos)
     g_key[...] = jnp.zeros_like(g_key)
@@ -625,24 +623,21 @@
     w_rows, b_rows = depth // seq_count, buckets // seq_count
     rows = TILE + TILE // 2 + w_rows + b_rows
     line = 2 * span * TILE
-    tables = whole_call(
+    scalars = jnp.concatenate([doc_lengths, half])
+    onehot, expanded = whole_call(
         table_kernel,
-        (pos, table),
-        [
-            shape((buckets, table.shape[1]), BF),
-            shape((2 * HD, line), BF),
-            shape((2 * HD, line), BF),
-            shape((line, 2 * HD), BF),
-        ],
+        (scalars, pos, table),
+        [shape((buckets, table.shape[1]), BF), shape((2 * HD, table.shape[1]), BF)],
+        scalars=1,
     )
     other = lax.ppermute(
-        whole_call(cut_kernel, (own, *tables), shape((heads, tokens_dev, 2 * HD), BF)),
+        whole_call(cut_kernel, (own, expanded), shape((heads, tokens_dev, 2 * HD), BF)),
         "seq",
         partners,
     )
     sent, kept, bucket, query = whole_call(
         head_kernel,
-        (jnp.concatenate([doc_lengths, half]), own, other, *tables),
+        (scalars, own, other, onehot, expanded),
         [
             shape((heads * TILE + buckets, 2 * HD), BF),
             shape((heads, TILE, 2 * HD), F32),
@@ -650,6 +645,9 @@
             shape((heads, TILE // 2, 2 * HD), BF),
         ],
         [
+            vm((2 * HD, line), BF),
+            vm((2 * HD, line), BF),
+            vm((line, 2 * HD), BF),
             vm((seq_count, TILE, 2 * HD), BF),
             vm((seq_count, TILE, 2 * HD), F32),
             vm((seq_count, TILE, HD), F32),

time: 91.8 us -> 90.2 us (0.983)
  local copies, waits for them, and re-layouts: 6.38 us -> 2.7 us
  starting transfers between devices: 12.9 us -> 14.3 us
  waiting for transfers between devices: 31.5 us -> 32.5 us
    unnamed x18 -> x10, local copies, waits for them, and re-layouts: 5.03 us -> 1.35 us
    ppermute x1, starting transfers between devices: 0.07 us -> 1.5 us  [head_body(): came = lax.ppermute(sent, 'seq', partners)]
where the time goes in v6:
time: 90.2 us; the launch traced here: 89.6 us
  waiting for transfers between devices  32.5 us (36%)
  Pallas kernels  27.1 us (30%)
  starting transfers between devices  14.3 us (16%)
  blocking collectives  11.6 us (13%)
  local copies, waits for them, and re-layouts  2.7 us (3%)
    pallas_call x8, Pallas kernels, whole_call(): pl.pallas_call(kernel, out_shape=outputs, in_specs=[SMEM] * scalars + [so...  27.1 us
    all_to_all x2, waiting for transfers between devices, spread(): lax.all_to_all(pieces, 'seq', 0, 0, axis_index_groups=halves, tiled=True)  26.8 us
    all_to_all x1, blocking collectives, spread(): lax.all_to_all(pieces, 'seq', 0, 0, axis_index_groups=halves, tiled=True)  11.6 us
    all_to_all x2, starting transfers between devices, spread(): lax.all_to_all(pieces, 'seq', 0, 0, axis_index_groups=halves, tiled=True)  11.2 us
    ppermute x1, waiting for transfers between devices, head_body(): far_rel = lax.ppermute(far_rel, 'head', [(0, 1), (1, 0)])  2.43 us
  transfers between devices with their start and end apart: 6, of which 6 were waited for; matrix products, arithmetic and copies ran while one was open for 2% of the time, Pallas kernels for 2%

profile of v6, /device:TPU:0, one launch (start us, length us, event | category | flops | bytes accessed | tf_op | source)
XLA Modules:
  0.0 89.6 jit_solution(5620590960016843600)
XLA Ops:
  0.6 2.1 %shard_map.136 = bf16[8,128,256]{2,1,0:T(8,128)(2,1)} custom-call(bf16[128,512]{1,0:T(8,128)(2,1)} %q_ref.1, bf16[128,512]{1,0:T(8,128)(2,1)} %g_ref.1, bf16[128,512]{1,0:T(8,128)(2,1)} %k_ref.1, bf16[128,512]{1,0:T(8,128)(2,1)} %v_ref.1), custom_call_target="tpu_custom_call" | custom-call | tf_op jit(solution)/shard_map/pallas_call | solution.py:571
  2.7 7.4 %all-to-all-start = ((bf16[8,128,256]{2,1,0:T(8,128)(2,1)}), bf16[8,128,256]{2,1,0:T(8,128)(2,1)S(1)}, u32[]{:S(2)}, u32[]{:S(2)}) async-start(bf16[8,128,256]{2,1,0:T(8,128)(2,1)} %shard_map.136), calls=%async_computation | async-start | bytes 1048576 | tf_op jit(solution)/shard_map/all_to_all | solution.py:597
  10.1 0.7 copy-done.3
  10.8 0.1 rev.4
  10.9 0.7 copy-done.4
  11.6 0.1 pad_add_fusion.scalars_ref
  11.6 1.2 %constant_dynamic-slice_fusion.1 = (bf16[1024,64]{1,0:T(8,128)(2,1)S(1)}, bf16[1024,64]{1,0:T(8,128)(2,1)S(1)}) fusion(bf16[1024,512]{1,0:T(8,128)(2,1)} %wq_ref.1, s32[]{:T(128)S(6)} %select_n.16, bf16[1024,512]{1,0:T(8,128)(2,1)} %wk_ref.1), kind=kLoop, calls=%fused_computation.7 | loop fusion | bytes 524292 | tf_op jit(solution)/shard_map/dynamic_slice | solution.py:617
  12.9 0.5 fusion.pos_ref
  13.4 0.9 %shard_map.137 = (bf16[512,1024]{1,0:T(8,128)(2,1)S(1)}, bf16[128,1024]{1,0:T(8,128)(2,1)S(1)}) custom-call(s32[9]{0:T(128)S(1)} %pad_add_fusion.scalars_ref, bf16[512,128]{1,0:T(8,128)(2,1)S(1)} %fusion.pos_ref, s32[1,1024]{1,0:T(1,128)S(1)} %bitcast.5), custom_call_target="tpu_custom_call" | custom-call | tf_op jit(solution)/shard_map/pallas_call | solution.py:571
  14.4 10.3 %all-to-all-done.own_ref = bf16[8,128,256]{2,1,0:T(8,128)(2,1)S(1)} async-done(((bf16[8,128,256]{2,1,0:T(8,128)(2,1)}), bf16[8,128,256]{2,1,0:T(8,128)(2,1)S(1)}, u32[]{:S(2)}, u32[]{:S(2)}) %all-to-all-start) | async-done | bytes 524320 | tf_op jit(solution)/shard_map/all_to_all | solution.py:597
  24.8 1.5 %collective-permute-done.other_ref = bf16[8,128,128]{2,1,0:T(8,128)(2,1)S(1)} collective-permute-done((bf16[8,128,128]{2,1,0:T(8,128)(2,1)S(1)}, bf16[8,128,128]{2,1,0:T(8,128)(2,1)S(1)}, u32[]{:S(2)}, u32[]{:S(2)}) %collective-permute-start) | collective-permute-done | bytes 262176 | tf_op jit(solution)/shard_map/ppermute | solution.py:633
  26.3 19.9 %shard_map.139 = (bf16[1536,128]{1,0:T(8,128)(2,1)S(1)}, f32[8,128,128]{2,1,0:T(8,128)S(1)}, bf16[512,128]{1,0:T(8,128)(2,1)S(1)}, bf16[8,64,128]{2,1,0:T(8,128)(2,1)S(1)}) custom-call(s32[9]{0:T(128)S(1)} %pad_add_fusion.scalars_ref, bf16[8,128,256]{2,1,0:T(8,128)(2,1)S(1)} %all-to-all-done.own_ref, ...), custom_call_target="tpu_custom_call" | custom-call | tf_op jit(solution)/shard_map/pallas_call | solution.py:571
  46.2 1.5 %collective-permute-start.1 = (bf16[1536,128]{1,0:T(8,128)(2,1)S(1)}, bf16[1536,128]{1,0:T(8,128)(2,1)S(1)}, u32[]{:S(2)}, u32[]{:S(2)}) collective-permute-start(bf16[1536,128]{1,0:T(8,128)(2,1)S(1)} %get-tuple-element.22), channel_id=1, source_target_pairs={{0,2},{2,0},{4,6},{6,4},{8,10},{10,8},{12,14},{14,12},{16,18},{18,... | collective-permute-start | bytes 1179656 | tf_op jit(solution)/shard_map/ppermute | solution.py:668
  47.7 1.3 %collective-permute-done.1.came_ref = bf16[1536,128]{1,0:T(8,128)(2,1)S(1)} collective-permute-done((bf16[1536,128]{1,0:T(8,128)(2,1)S(1)}, bf16[1536,128]{1,0:T(8,128)(2,1)S(1)}, u32[]{:S(2)}, u32[]{:S(2)}) %collective-permute-start.1) | collective-permute-done | bytes 393248 | tf_op jit(solution)/shard_map/ppermute | solution.py:668
  49.1 1.3 %shard_map.140 = bf16[8,288,128]{2,1,0:T(8,128)(2,1)} custom-call(s32[1]{0:T(128)} %bitcast.half_ref, f32[8,128,128]{2,1,0:T(8,128)S(1)} %get-tuple-element.19.keep_ref, bf16[512,128]{1,0:T(8,128)(2,1)S(1)} %get-tuple-element.20.bucket_ref, bf16[8,64,128]{2,1,0:T(8,128)(2,1)S(1)} %get-tuple-element.21.query_ref, ...), custom_call_target="tpu_custom_call" | custom-call | tf_op jit(solution)/shard_map/pallas_call | solution.py:571
  50.4 3.8 %all-to-all-start.1 = ((bf16[8,288,128]{2,1,0:T(8,128)(2,1)}), bf16[8,288,128]{2,1,0:T(8,128)(2,1)S(1)}, u32[]{:S(2)}, u32[]{:S(2)}) async-start(bf16[8,288,128]{2,1,0:T(8,128)(2,1)} %shard_map.140), calls=%async_computation.1 | async-start | bytes 1179648 | tf_op jit(solution)/shard_map/all_to_all | solution.py:597
  54.1 16.5 %all-to-all-done.1.got_ref = bf16[8,288,128]{2,1,0:T(8,128)(2,1)S(1)} async-done(((bf16[8,288,128]{2,1,0:T(8,128)(2,1)}), bf16[8,288,128]{2,1,0:T(8,128)(2,1)S(1)}, u32[]{:S(2)}, u32[]{:S(2)}) %all-to-all-start.1) | async-done | bytes 589856 | tf_op jit(solution)/shard_map/all_to_all | solution.py:597
  70.7 0.7 shard_map.142
  71.4 1.6 %collective-permute-start.2 = (bf16[32,512]{1,0:T(8,128)(2,1)S(1)}, bf16[32,512]{1,0:T(8,128)(2,1)S(1)}, u32[]{:S(2)}, u32[]{:S(2)}) collective-permute-start(bf16[32,512]{1,0:T(8,128)(2,1)S(1)} %constant_dynamic-slice_fusion), channel_id=1, source_target_pairs={{0,1},{1,0},{2,3},{3,2},{4,5},{5,4},{6,7},{7,6},{8,9},{9,8},{10,11... | collective-permute-start | bytes 98312 | tf_op jit(solution)/shard_map/ppermute | solution.py:685
  73.0 2.4 %collective-permute-done.2 = bf16[32,512]{1,0:T(8,128)(2,1)S(1)} collective-permute-done((bf16[32,512]{1,0:T(8,128)(2,1)S(1)}, bf16[32,512]{1,0:T(8,128)(2,1)S(1)}, u32[]{:S(2)}, u32[]{:S(2)}) %collective-permute-start.2) | collective-permute-done | bytes 32800 | tf_op jit(solution)/shard_map/ppermute | solution.py:685
  75.4 11.6 %all_to_all.15.near_ref = bf16[8,32,512]{2,1,0:T(8,128)(2,1)S(1)} all-to-all(bf16[8,32,512]{2,1,0:T(8,128)(2,1)S(1)} %broadcast_in_dim.2), channel_id=1, replica_groups={{0,4,8,12,16,20,24,28},{2,6,10,14,18,22,26,30},{1,5,9,13,17,21,25,29},{..., dimensions={0} | all-to-all | bytes 524288 | tf_op jit(solution)/shard_map/all_to_all | solution.py:597
  87.1 1.1 %shard_map.141 = (bf16[128,512]{1,0:T(8,128)(2,1)}, bf16[128,512]{1,0:T(8,128)(2,1)}, bf16[128,512]{1,0:T(8,128)(2,1)}, f32[64,512]{1,0:T(8,128)}, f32[64,512]{1,0:T(8,128)}) custom-call(bf16[8,288,128]{2,1,0:T(8,128)(2,1)S(1)} %all-to-all-done.1.got_ref), custom_call_target="tpu_custom_call" | custom-call | tf_op jit(solution)/shard_map/pallas_call | solution.py:571
  88.2 0.4 collective-permute-done.3.far_ref
  88.6 1.0 %shard_map.143 = f32[512,512]{1,0:T(8,128)} custom-call(s32[1]{0:T(128)} %bitcast.half_ref, bf16[8,32,512]{2,1,0:T(8,128)(2,1)S(1)} %all_to_all.15.near_ref, bf16[8,32,512]{2,1,0:T(8,128)(2,1)S(1)} %collective-permute-done.3.far_ref), custom_call_target="tpu_custom_call" | custom-call | tf_op jit(solution)/shard_map/pallas_call | solution.py:571
  (14 shorter events, 0.2 us)
Async XLA Ops:
  2.7 10.2 %copy-start = (bf16[512,1024]{1,0:T(8,128)(2,1)S(1)}, bf16[512,1024]{1,0:T(8,128)(2,1)}, u32[]{:S(2)}) copy-start(bf16[512,1024]{1,0:T(8,128)(2,1)} %rel_ref.1) | copy-start | bytes 3145732
  2.7 21.9 %all-to-all-start = ((bf16[8,128,256]{2,1,0:T(8,128)(2,1)}), bf16[8,128,256]{2,1,0:T(8,128)(2,1)S(1)}, u32[]{:S(2)}, u32[]{:S(2)}) async-start(bf16[8,128,256]{2,1,0:T(8,128)(2,1)} %shard_map.136), calls=%async_computation | async-start | bytes 1048576 | tf_op jit(solution)/shard_map/all_to_all | solution.py:597
  10.1 0.7 copy-start.3
  10.9 0.7 copy-start.4
  24.7 1.6 %collective-permute-start = (bf16[8,128,128]{2,1,0:T(8,128)(2,1)S(1)}, bf16[8,128,128]{2,1,0:T(8,128)(2,1)S(1)}, u32[]{:S(2)}, u32[]{:S(2)}) collective-permute-start(bf16[8,128,128]{2,1,0:T(8,128)(2,1)S(1)} %shard_map.138), channel_id=1, source_target_pairs={{0,2},{2,0},{4,6},{6,4},{8,10},{10,8},{12,14},{14,12},{16,18},{18,... | collective-permute-start | bytes 786440 | tf_op jit(solution)/shard_map/ppermute | solution.py:633
  46.2 2.8 %collective-permute-start.1 = (bf16[1536,128]{1,0:T(8,128)(2,1)S(1)}, bf16[1536,128]{1,0:T(8,128)(2,1)S(1)}, u32[]{:S(2)}, u32[]{:S(2)}) collective-permute-start(bf16[1536,128]{1,0:T(8,128)(2,1)S(1)} %get-tuple-element.22), channel_id=1, source_target_pairs={{0,2},{2,0},{4,6},{6,4},{8,10},{10,8},{12,14},{14,12},{16,18},{18,... | collective-permute-start | bytes 1179656 | tf_op jit(solution)/shard_map/ppermute | solution.py:668
  49.1 21.6 %copy-start.2 = (bf16[1024,512]{1,0:T(8,128)(2,1)S(1)}, bf16[1024,512]{1,0:T(8,128)(2,1)}, u32[]{:S(2)}) copy-start(bf16[1024,512]{1,0:T(8,128)(2,1)} %wk_ref.1) | copy-start | bytes 3145732
  50.4 20.3 %copy-start.1 = (bf16[1024,512]{1,0:T(8,128)(2,1)S(1)}, bf16[1024,512]{1,0:T(8,128)(2,1)}, u32[]{:S(2)}) copy-start(bf16[1024,512]{1,0:T(8,128)(2,1)} %wq_ref.1) | copy-start | bytes 3145732
  50.4 20.3 %all-to-all-start.1 = ((bf16[8,288,128]{2,1,0:T(8,128)(2,1)}), bf16[8,288,128]{2,1,0:T(8,128)(2,1)S(1)}, u32[]{:S(2)}, u32[]{:S(2)}) async-start(bf16[8,288,128]{2,1,0:T(8,128)(2,1)} %shard_map.140), calls=%async_computation.1 | async-start | bytes 1179648 | tf_op jit(solution)/shard_map/all_to_all | solution.py:597
  71.4 4.0 %collective-permute-start.2 = (bf16[32,512]{1,0:T(8,128)(2,1)S(1)}, bf16[32,512]{1,0:T(8,128)(2,1)S(1)}, u32[]{:S(2)}, u32[]{:S(2)}) collective-permute-start(bf16[32,512]{1,0:T(8,128)(2,1)S(1)} %constant_dynamic-slice_fusion), channel_id=1, source_target_pairs={{0,1},{1,0},{2,3},{3,2},{4,5},{5,4},{6,7},{7,6},{8,9},{9,8},{10,11... | collective-permute-start | bytes 98312 | tf_op jit(solution)/shard_map/ppermute | solution.py:685
  87.1 1.5 %collective-permute-start.3 = (bf16[8,32,512]{2,1,0:T(8,128)(2,1)S(1)}, bf16[8,32,512]{2,1,0:T(8,128)(2,1)S(1)}, u32[]{:S(2)}, u32[]{:S(2)}) collective-permute-start(bf16[8,32,512]{2,1,0:T(8,128)(2,1)S(1)} %all_to_all.15.near_ref), channel_id=1, source_target_pairs={{0,2},{2,0},{4,6},{6,4},{8,10},{10,8},{12,14},{14,12},{16,18},{18,... | collective-permute-start | bytes 786440 | tf_op jit(solution)/shard_map/ppermute | solution.py:688

commit v7 on v6

--- a/solution.py
+++ b/solution.py
@@ -289,7 +289,7 @@
 def head_kernel(
     scalars_ref, own_ref, other_ref, onehot, expanded,
     send_ref, keep_ref, bucket_ref, query_ref,
-    pk, pq, rows_ref, kvs, acc, acc_pos, g_key, g_query, k_t, k_rev, s_q, st, dp, dtile, pairs, dq_nat, dq_pos,
+    pk, pq, kvs, acc, acc_pos, g_key, g_query, k_t, k_rev, s_q, st, dp, dtile, pairs, dq_nat, dq_pos,
 ):
     blocks = own_ref.shape[0]
     tiles = 2 * blocks
@@ -305,11 +305,9 @@
     wrap = row + col >= TILE - 1
     keep = jnp.where(col >= row, 1.0, 0.0).astype(BF)
     low = col < HD
-    for table in (pk, pq, rows_ref):
+    for table, part in ((pk, expanded[:HD]), (pq, expanded[HD:])):
         table[...] = jnp.zeros_like(table)
-    pk[0:HD, valid0 : valid0 + valid] = expanded[:HD]
-    pq[0:HD, valid0 : valid0 + valid] = expanded[HD:]
-    rows_ref[valid0 : valid0 + valid, :] = expanded[...].astype(F32).T.astype(BF)
+        table[:, valid0 : valid0 + valid] = part
     acc[...] = jnp.zeros_like(acc)
     acc_pos[...] = jnp.zeros_like(acc_pos)
     g_key[...] = jnp.zeros_like(g_key)
@@ -383,7 +381,7 @@
         stop = stop - first * TILE
 
         key_x = pl.multiple_of(halo * 2 * TILE - delta, TILE)
-        s_q[:, 0 : (span + 1) * TILE] = nn(qd, pk[:, pl.ds(key_x, (span + 1) * TILE)])
+        s_q[:, 0 : (span + 1) * TILE] = nn(qd[:, :HD], pk[:, pl.ds(key_x, (span + 1) * TILE)])
         best = jnp.full((8, TILE), masked_score, F32)
         window_kv = kvs[pl.ds(first, span)].reshape(span * TILE, 2 * HD)
         contents = nn(window_kv, right)
@@ -391,7 +389,7 @@
             kv = window_kv[t * TILE : (t + 1) * TILE]
             both = contents[t * TILE : (t + 1) * TILE]
             query_x = pl.multiple_of(2 * halo * TILE + delta - t * TILE, TILE)
-            s_k = nn(kv, pq[:, pl.ds(query_x, 2 * TILE)])
+            s_k = nn(kv[:, :HD], pq[:, pl.ds(query_x, 2 * TILE)])
             key_term = pltpu.roll(
                 jnp.where(wrap, s_k[:, :TILE], s_k[:, TILE:]), 1, 1, stride=1, stride_axis=0
             )
@@ -427,36 +425,36 @@
         pair = jnp.concatenate([lows, jnp.where(low, jnp.zeros_like(qd), qd)], 0)
         dq_t = jnp.zeros((HD, TILE), F32)
         before = jnp.zeros((TILE, TILE), BF)
-        ahead_part = None
+        near = held = None
         for t in range(span):
             prob = st[t] * inverse
             dscore = (prob * (dp[t] - row_dot)).astype(BF)
             pairs[t] = jnp.concatenate([dscore, prob.astype(BF)], 1)
-            stacked = nn(jnp.concatenate([k_t[first + t], swap], 0), dscore)
-            dq_t = dq_t + stacked[:HD]
+            stacked = nn(
+                jnp.concatenate([k_t[first + t], swap], 0),
+                jnp.concatenate([dscore, dscore.T], 1),
+            )
+            dq_t = dq_t + stacked[:HD, :TILE]
             query_x = pl.multiple_of(2 * halo * TILE + delta - t * TILE, TILE)
-            y = pltpu.roll(stacked[HD:], 0, 1, stride=1, stride_axis=0)
-            y = y.astype(BF)
+            y = pltpu.roll(stacked[HD:, :TILE], 0, 1, stride=1, stride_axis=0).astype(BF)
+            last = near
             near = y * keep
             far = y - near
-            back = nn(jnp.concatenate([near, far], 1), rows_ref[pl.ds(query_x, 2 * TILE), :])
-            acc_pos[first + t] += back[:, HD:]
-            turned_keys = k_rev[first + t]
-            chunk = pl.ds(query_x + TILE, TILE)
-            if ahead_part is None:
-                g_query[:, chunk] += nn(turned_keys, far)
+            g_query[:, pl.ds(query_x, 2 * TILE)] += nn(
+                k_rev[first + t], jnp.concatenate([near, far], 1)
+            )
+            chunk = pq[:, pl.ds(query_x + TILE, TILE)]
+            if t == 0:
+                held = nt(chunk, far)
             else:
-                g_query[:, chunk] += nn(
-                    jnp.concatenate([ahead_part[0], turned_keys], 1),
-                    jnp.concatenate([ahead_part[1], far], 0),
-                )
-            ahead_part = (turned_keys, near)
-            z = pltpu.roll(nt(swap, dscore), 0, 1, stride=1, stride_axis=0)
-            z = z.astype(BF)
+                back = nt(chunk, jnp.concatenate([last, far], 0))
+                acc_pos[first + t - 1] += held + back[:, :TILE]
+                held = back[:, TILE:]
+            z = pltpu.roll(stacked[HD:, TILE:], 0, 1, stride=1, stride_axis=0).astype(BF)
             here = z * keep
             dtile[:, t * TILE : (t + 1) * TILE] = here + before
             before = z - here
-        g_query[:, pl.ds(query_x, TILE)] += nn(*ahead_part)
+        acc_pos[first + span - 1] += held + nt(pq[:, pl.ds(query_x, TILE)], near)
         acc[pl.ds(first, span)] += nn(
             pairs[0:span].reshape(span * TILE, 2 * TILE), pair
         ).reshape(span, TILE, 2 * HD)
@@ -464,9 +462,7 @@
         spread_q = dtile[:, 0 : (span + 1) * TILE]
         window = pl.ds(key_x, (span + 1) * TILE)
         g_key[:, window] += nn(q_rev, spread_q)
-        back = nn(spread_q, rows_ref[window, :])[:, :HD]
-        high = back.astype(BF)
-        dq_pos[b] = jnp.concatenate([high, (back - high.astype(F32)).astype(BF)], 1)
+        dq_pos[b] = nt(pk[:, window], spread_q)
         dq_nat[b] = dq_t
 
     lax.fori_loop(0, blocks, block, 0)
@@ -485,20 +481,20 @@
     send_ref[blocks * TILE :, :] = bucket
     factor = jnp.where(low, scale, 1.0)
 
+    def unreversed(part):
+        high = part.astype(BF)
+        both = nn(jnp.concatenate([high, (part - high.astype(F32)).astype(BF)], 0), swap)
+        return both[:HD] + both[HD:]
+
     def gradients(tile):
-        back = acc_pos[tile]
-        high = back.astype(BF)
-        both = nn(swap, jnp.concatenate([high, (back - high.astype(F32)).astype(BF)], 1))
-        extra = both[:, :HD] + both[:, HD:]
+        extra = unreversed(acc_pos[tile]).T
         extra = jnp.concatenate([extra, jnp.zeros_like(extra)], 1)
         return (acc[tile] + extra) * factor
 
     def finish(b, carry):
         keep_ref[b] = gradients(2 * b + half)
         send_ref[pl.ds(b * TILE, TILE), :] = gradients(2 * b + 1 - half).astype(BF)
-        both = nn(swap, dq_pos[b])
-        extra = both[:, :HD] + both[:, HD:]
-        grad = scale * (dq_nat[b].T + extra)
+        grad = scale * (dq_nat[b] + unreversed(dq_pos[b])).T
         query_ref[b] = jnp.concatenate([grad[: TILE // 2], grad[TILE // 2 :]], 1).astype(BF)
         return carry
 
@@ -645,12 +641,11 @@
             shape((heads, TILE // 2, 2 * HD), BF),
         ],
         [
-            vm((2 * HD, line), BF),
-            vm((2 * HD, line), BF),
-            vm((line, 2 * HD), BF),
+            vm((HD, line), BF),
+            vm((HD, line), BF),
             vm((seq_count, TILE, 2 * HD), BF),
             vm((seq_count, TILE, 2 * HD), F32),
-            vm((seq_count, TILE, HD), F32),
+            vm((seq_count, HD, TILE), F32),
             vm((HD, line), F32),
             vm((HD, line), F32),
             vm((seq_count, HD, TILE), BF),
@@ -661,7 +656,7 @@
             vm((TILE, (span + 1) * TILE), BF),
             vm((span, TILE, 2 * TILE), BF),
             vm((heads, HD, TILE), F32),
-            vm((heads, TILE, 2 * HD), BF),
+            vm((heads, HD, TILE), F32),
         ],
         scalars=1,
     )

time: 90.2 us -> 85.7 us (0.950)
  Pallas kernels: 27.1 us -> 23.8 us
  starting transfers between devices: 14.3 us -> 12.9 us
    pallas_call x8, Pallas kernels: 27.1 us -> 23.8 us  [whole_call(): pl.pallas_call(kernel, out_shape=outputs, in_specs=[SMEM] * scalars + [so...]
    ppermute x1, starting transfers between devices: 1.5 us -> 0.07 us  [head_body(): came = lax.ppermute(sent, 'seq', partners)]
where the time goes in v7:
time: 85.7 us; the launch traced here: 85 us
  waiting for transfers between devices  32.6 us (38%)
  Pallas kernels  23.8 us (28%)
  starting transfers between devices  12.9 us (15%)
  blocking collectives  11.6 us (14%)
  local copies, waits for them, and re-layouts  2.7 us (3%)
    all_to_all x2, waiting for transfers between devices, spread(): lax.all_to_all(pieces, 'seq', 0, 0, axis_index_groups=halves, tiled=True)  26.6 us
    pallas_call x8, Pallas kernels, whole_call(): pl.pallas_call(kernel, out_shape=outputs, in_specs=[SMEM] * scalars + [so...  23.8 us
    all_to_all x1, blocking collectives, spread(): lax.all_to_all(pieces, 'seq', 0, 0, axis_index_groups=halves, tiled=True)  11.6 us
    all_to_all x2, starting transfers between devices, spread(): lax.all_to_all(pieces, 'seq', 0, 0, axis_index_groups=halves, tiled=True)  11.2 us
    ppermute x1, waiting for transfers between devices, head_body(): far_rel = lax.ppermute(far_rel, 'head', [(0, 1), (1, 0)])  2.43 us
  transfers between devices with their start and end apart: 6, of which 6 were waited for; matrix products, arithmetic and copies ran while one was open for 2% of the time, Pallas kernels for 2%

profile of v7, /device:TPU:0, one launch (start us, length us, event | category | flops | bytes accessed | tf_op | source)
XLA Modules:
  0.0 85.0 jit_solution(18144196525481176383)
XLA Ops:
  0.6 2.1 %shard_map.136 = bf16[8,128,256]{2,1,0:T(8,128)(2,1)} custom-call(bf16[128,512]{1,0:T(8,128)(2,1)} %q_ref.1, bf16[128,512]{1,0:T(8,128)(2,1)} %g_ref.1, bf16[128,512]{1,0:T(8,128)(2,1)} %k_ref.1, bf16[128,512]{1,0:T(8,128)(2,1)} %v_ref.1), custom_call_target="tpu_custom_call" | custom-call | tf_op jit(solution)/shard_map/pallas_call | solution.py:567
  2.7 7.4 %all-to-all-start = ((bf16[8,128,256]{2,1,0:T(8,128)(2,1)}), bf16[8,128,256]{2,1,0:T(8,128)(2,1)S(1)}, u32[]{:S(2)}, u32[]{:S(2)}) async-start(bf16[8,128,256]{2,1,0:T(8,128)(2,1)} %shard_map.136), calls=%async_computation | async-start | bytes 1048576 | tf_op jit(solution)/shard_map/all_to_all | solution.py:593
  10.1 0.7 copy-done.3
  10.8 0.1 rev.4
  10.9 0.7 copy-done.4
  11.6 0.1 pad_add_fusion.scalars_ref
  11.6 1.2 %constant_dynamic-slice_fusion.1 = (bf16[1024,64]{1,0:T(8,128)(2,1)S(1)}, bf16[1024,64]{1,0:T(8,128)(2,1)S(1)}) fusion(bf16[1024,512]{1,0:T(8,128)(2,1)} %wq_ref.1, s32[]{:T(128)S(6)} %select_n.16, bf16[1024,512]{1,0:T(8,128)(2,1)} %wk_ref.1), kind=kLoop, calls=%fused_computation.7 | loop fusion | bytes 524292 | tf_op jit(solution)/shard_map/dynamic_slice | solution.py:613
  12.9 0.5 fusion.pos_ref
  13.4 0.9 %shard_map.137 = (bf16[512,1024]{1,0:T(8,128)(2,1)S(1)}, bf16[128,1024]{1,0:T(8,128)(2,1)S(1)}) custom-call(s32[9]{0:T(128)S(1)} %pad_add_fusion.scalars_ref, bf16[512,128]{1,0:T(8,128)(2,1)S(1)} %fusion.pos_ref, s32[1,1024]{1,0:T(1,128)S(1)} %bitcast.5), custom_call_target="tpu_custom_call" | custom-call | tf_op jit(solution)/shard_map/pallas_call | solution.py:567
  14.4 10.3 %all-to-all-done.own_ref = bf16[8,128,256]{2,1,0:T(8,128)(2,1)S(1)} async-done(((bf16[8,128,256]{2,1,0:T(8,128)(2,1)}), bf16[8,128,256]{2,1,0:T(8,128)(2,1)S(1)}, u32[]{:S(2)}, u32[]{:S(2)}) %all-to-all-start) | async-done | bytes 524320 | tf_op jit(solution)/shard_map/all_to_all | solution.py:593
  24.7 0.1 collective-permute-start
  24.8 1.5 %collective-permute-done.other_ref = bf16[8,128,128]{2,1,0:T(8,128)(2,1)S(1)} collective-permute-done((bf16[8,128,128]{2,1,0:T(8,128)(2,1)S(1)}, bf16[8,128,128]{2,1,0:T(8,128)(2,1)S(1)}, u32[]{:S(2)}, u32[]{:S(2)}) %collective-permute-start) | collective-permute-done | bytes 262176 | tf_op jit(solution)/shard_map/ppermute | solution.py:629
  26.3 16.6 %shard_map.139 = (bf16[1536,128]{1,0:T(8,128)(2,1)S(1)}, f32[8,128,128]{2,1,0:T(8,128)S(1)}, bf16[512,128]{1,0:T(8,128)(2,1)S(1)}, bf16[8,64,128]{2,1,0:T(8,128)(2,1)S(1)}) custom-call(s32[9]{0:T(128)S(1)} %pad_add_fusion.scalars_ref, bf16[8,128,256]{2,1,0:T(8,128)(2,1)S(1)} %all-to-all-done.own_ref, ...), custom_call_target="tpu_custom_call" | custom-call | tf_op jit(solution)/shard_map/pallas_call | solution.py:567
  42.9 1.7 %collective-permute-done.1.came_ref = bf16[1536,128]{1,0:T(8,128)(2,1)S(1)} collective-permute-done((bf16[1536,128]{1,0:T(8,128)(2,1)S(1)}, bf16[1536,128]{1,0:T(8,128)(2,1)S(1)}, u32[]{:S(2)}, u32[]{:S(2)}) %collective-permute-start.1) | collective-permute-done | bytes 393248 | tf_op jit(solution)/shard_map/ppermute | solution.py:663
  44.6 1.3 %shard_map.140 = bf16[8,288,128]{2,1,0:T(8,128)(2,1)} custom-call(s32[1]{0:T(128)} %bitcast.half_ref, f32[8,128,128]{2,1,0:T(8,128)S(1)} %get-tuple-element.19.keep_ref, bf16[512,128]{1,0:T(8,128)(2,1)S(1)} %get-tuple-element.20.bucket_ref, bf16[8,64,128]{2,1,0:T(8,128)(2,1)S(1)} %get-tuple-element.21.query_ref, ...), custom_call_target="tpu_custom_call" | custom-call | tf_op jit(solution)/shard_map/pallas_call | solution.py:567
  45.9 3.8 %all-to-all-start.1 = ((bf16[8,288,128]{2,1,0:T(8,128)(2,1)}), bf16[8,288,128]{2,1,0:T(8,128)(2,1)S(1)}, u32[]{:S(2)}, u32[]{:S(2)}) async-start(bf16[8,288,128]{2,1,0:T(8,128)(2,1)} %shard_map.140), calls=%async_computation.1 | async-start | bytes 1179648 | tf_op jit(solution)/shard_map/all_to_all | solution.py:593
  49.7 16.3 %all-to-all-done.1.got_ref = bf16[8,288,128]{2,1,0:T(8,128)(2,1)S(1)} async-done(((bf16[8,288,128]{2,1,0:T(8,128)(2,1)}), bf16[8,288,128]{2,1,0:T(8,128)(2,1)S(1)}, u32[]{:S(2)}, u32[]{:S(2)}) %all-to-all-start.1) | async-done | bytes 589856 | tf_op jit(solution)/shard_map/all_to_all | solution.py:593
  66.0 0.7 shard_map.142
  66.7 1.6 %collective-permute-start.2 = (bf16[32,512]{1,0:T(8,128)(2,1)S(1)}, bf16[32,512]{1,0:T(8,128)(2,1)S(1)}, u32[]{:S(2)}, u32[]{:S(2)}) collective-permute-start(bf16[32,512]{1,0:T(8,128)(2,1)S(1)} %constant_dynamic-slice_fusion), channel_id=1, source_target_pairs={{0,1},{1,0},{2,3},{3,2},{4,5},{5,4},{6,7},{7,6},{8,9},{9,8},{10,11... | collective-permute-start | bytes 98312 | tf_op jit(solution)/shard_map/ppermute | solution.py:680
  68.3 2.4 %collective-permute-done.2 = bf16[32,512]{1,0:T(8,128)(2,1)S(1)} collective-permute-done((bf16[32,512]{1,0:T(8,128)(2,1)S(1)}, bf16[32,512]{1,0:T(8,128)(2,1)S(1)}, u32[]{:S(2)}, u32[]{:S(2)}) %collective-permute-start.2) | collective-permute-done | bytes 32800 | tf_op jit(solution)/shard_map/ppermute | solution.py:680
  70.7 11.6 %all_to_all.15.near_ref = bf16[8,32,512]{2,1,0:T(8,128)(2,1)S(1)} all-to-all(bf16[8,32,512]{2,1,0:T(8,128)(2,1)S(1)} %broadcast_in_dim.2), channel_id=1, replica_groups={{0,4,8,12,16,20,24,28},{2,6,10,14,18,22,26,30},{1,5,9,13,17,21,25,29},{..., dimensions={0} | all-to-all | bytes 524288 | tf_op jit(solution)/shard_map/all_to_all | solution.py:593
  82.4 1.1 %shard_map.141 = (bf16[128,512]{1,0:T(8,128)(2,1)}, bf16[128,512]{1,0:T(8,128)(2,1)}, bf16[128,512]{1,0:T(8,128)(2,1)}, f32[64,512]{1,0:T(8,128)}, f32[64,512]{1,0:T(8,128)}) custom-call(bf16[8,288,128]{2,1,0:T(8,128)(2,1)S(1)} %all-to-all-done.1.got_ref), custom_call_target="tpu_custom_call" | custom-call | tf_op jit(solution)/shard_map/pallas_call | solution.py:567
  83.5 0.4 collective-permute-done.3.far_ref
  83.9 1.0 %shard_map.143 = f32[512,512]{1,0:T(8,128)} custom-call(s32[1]{0:T(128)} %bitcast.half_ref, bf16[8,32,512]{2,1,0:T(8,128)(2,1)S(1)} %all_to_all.15.near_ref, bf16[8,32,512]{2,1,0:T(8,128)(2,1)S(1)} %collective-permute-done.3.far_ref), custom_call_target="tpu_custom_call" | custom-call | tf_op jit(solution)/shard_map/pallas_call | solution.py:567
  (14 shorter events, 0.2 us)
Async XLA Ops:
  2.7 10.2 %copy-start = (bf16[512,1024]{1,0:T(8,128)(2,1)S(1)}, bf16[512,1024]{1,0:T(8,128)(2,1)}, u32[]{:S(2)}) copy-start(bf16[512,1024]{1,0:T(8,128)(2,1)} %rel_ref.1) | copy-start | bytes 3145732
  2.7 21.9 %all-to-all-start = ((bf16[8,128,256]{2,1,0:T(8,128)(2,1)}), bf16[8,128,256]{2,1,0:T(8,128)(2,1)S(1)}, u32[]{:S(2)}, u32[]{:S(2)}) async-start(bf16[8,128,256]{2,1,0:T(8,128)(2,1)} %shard_map.136), calls=%async_computation | async-start | bytes 1048576 | tf_op jit(solution)/shard_map/all_to_all | solution.py:593
  10.1 0.7 copy-start.3
  10.9 0.7 copy-start.4
  24.7 1.6 %collective-permute-start = (bf16[8,128,128]{2,1,0:T(8,128)(2,1)S(1)}, bf16[8,128,128]{2,1,0:T(8,128)(2,1)S(1)}, u32[]{:S(2)}, u32[]{:S(2)}) collective-permute-start(bf16[8,128,128]{2,1,0:T(8,128)(2,1)S(1)} %shard_map.138), channel_id=1, source_target_pairs={{0,2},{2,0},{4,6},{6,4},{8,10},{10,8},{12,14},{14,12},{16,18},{18,... | collective-permute-start | bytes 786440 | tf_op jit(solution)/shard_map/ppermute | solution.py:629
  42.8 1.8 %collective-permute-start.1 = (bf16[1536,128]{1,0:T(8,128)(2,1)S(1)}, bf16[1536,128]{1,0:T(8,128)(2,1)S(1)}, u32[]{:S(2)}, u32[]{:S(2)}) collective-permute-start(bf16[1536,128]{1,0:T(8,128)(2,1)S(1)} %get-tuple-element.22), channel_id=1, source_target_pairs={{0,2},{2,0},{4,6},{6,4},{8,10},{10,8},{12,14},{14,12},{16,18},{18,... | collective-permute-start | bytes 1179656 | tf_op jit(solution)/shard_map/ppermute | solution.py:663
  44.6 21.4 %copy-start.2 = (bf16[1024,512]{1,0:T(8,128)(2,1)S(1)}, bf16[1024,512]{1,0:T(8,128)(2,1)}, u32[]{:S(2)}) copy-start(bf16[1024,512]{1,0:T(8,128)(2,1)} %wk_ref.1) | copy-start | bytes 3145732
  45.9 20.1 %copy-start.1 = (bf16[1024,512]{1,0:T(8,128)(2,1)S(1)}, bf16[1024,512]{1,0:T(8,128)(2,1)}, u32[]{:S(2)}) copy-start(bf16[1024,512]{1,0:T(8,128)(2,1)} %wq_ref.1) | copy-start | bytes 3145732
  45.9 20.1 %all-to-all-start.1 = ((bf16[8,288,128]{2,1,0:T(8,128)(2,1)}), bf16[8,288,128]{2,1,0:T(8,128)(2,1)S(1)}, u32[]{:S(2)}, u32[]{:S(2)}) async-start(bf16[8,288,128]{2,1,0:T(8,128)(2,1)} %shard_map.140), calls=%async_computation.1 | async-start | bytes 1179648 | tf_op jit(solution)/shard_map/all_to_all | solution.py:593
  66.7 4.0 %collective-permute-start.2 = (bf16[32,512]{1,0:T(8,128)(2,1)S(1)}, bf16[32,512]{1,0:T(8,128)(2,1)S(1)}, u32[]{:S(2)}, u32[]{:S(2)}) collective-permute-start(bf16[32,512]{1,0:T(8,128)(2,1)S(1)} %constant_dynamic-slice_fusion), channel_id=1, source_target_pairs={{0,1},{1,0},{2,3},{3,2},{4,5},{5,4},{6,7},{7,6},{8,9},{9,8},{10,11... | collective-permute-start | bytes 98312 | tf_op jit(solution)/shard_map/ppermute | solution.py:680
  82.4 1.5 %collective-permute-start.3 = (bf16[8,32,512]{2,1,0:T(8,128)(2,1)S(1)}, bf16[8,32,512]{2,1,0:T(8,128)(2,1)S(1)}, u32[]{:S(2)}, u32[]{:S(2)}) collective-permute-start(bf16[8,32,512]{2,1,0:T(8,128)(2,1)S(1)} %all_to_all.15.near_ref), channel_id=1, source_target_pairs={{0,2},{2,0},{4,6},{6,4},{8,10},{10,8},{12,14},{14,12},{16,18},{18,... | collective-permute-start | bytes 786440 | tf_op jit(solution)/shard_map/ppermute | solution.py:683

commit v8 on v7

--- a/solution.py
+++ b/solution.py
@@ -255,20 +255,29 @@
 
 
 def pack_kernel(q_ref, g_ref, k_ref, v_ref, out_ref, held, pieces, came, left):
-    loads = [
-        pltpu.make_async_copy(ref, held.at[i], came.at[i])
-        for i, ref in enumerate((q_ref, g_ref, k_ref, v_ref))
-    ]
-    for load in loads:
-        load.start()
-    for load in loads:
-        load.wait()
+    heads = out_ref.shape[0]
+    wide = 2 * HD
+    loads = []
+    for g in range(heads // 2):
+        cols = pl.ds(g * wide, wide)
+        loads.append(
+            [
+                pltpu.make_async_copy(ref.at[:, cols], held.at[i, :, cols], came.at[g, i])
+                for i, ref in enumerate((q_ref, g_ref, k_ref, v_ref))
+            ]
+        )
+        for load in loads[g]:
+            load.start()
     stores = []
-    for head in range(out_ref.shape[0]):
-        cols = slice(head * HD, (head + 1) * HD)
-        pieces[head] = jnp.concatenate([held[i, :, cols] for i in range(4)], 1)
-        stores.append(pltpu.make_async_copy(pieces.at[head], out_ref.at[head], left.at[head]))
-        stores[-1].start()
+    for g in range(heads // 2):
+        for load in loads[g]:
+            load.wait()
+        for head in (2 * g, 2 * g + 1):
+            cols = slice(head * HD, (head + 1) * HD)
+            pieces[head] = jnp.concatenate([held[i, :, cols] for i in range(4)], 1)
+        two = pl.ds(2 * g, 2)
+        stores.append(pltpu.make_async_copy(pieces.at[two], out_ref.at[two], left.at[g]))
+        stores[g].start()
     for store in stores:
         store.wait()
 
@@ -313,18 +322,16 @@
     g_key[...] = jnp.zeros_like(g_key)
     g_query[...] = jnp.zeros_like(g_query)
 
-    def transpose_tile(b, carry):
+    for b in range(blocks):
         for kv, tile in (
             (own_ref[b, :, 2 * HD : 4 * HD], 2 * b + half),
             (other_ref[b], 2 * b + 1 - half),
         ):
             kvs[tile] = kv
-            turned = kv.astype(F32).T.astype(BF)
-            k_t[tile] = turned[:HD]
-            k_rev[tile] = nn(turned[:HD], swap).astype(BF)
-        return carry
-
-    lax.fori_loop(0, blocks, transpose_tile, 0, unroll=True)
+            k_t[tile] = kv.astype(F32).T[:HD].astype(BF)
+    k_rev[...] = (
+        nn(k_t[...].reshape(tiles * HD, TILE), swap).astype(BF).reshape(tiles, HD, TILE)
+    )
 
     def block(b, carry):
         own = 2 * b + half
@@ -481,24 +488,25 @@
     send_ref[blocks * TILE :, :] = bucket
     factor = jnp.where(low, scale, 1.0)
 
-    def unreversed(part):
+    def unreverse(ref):
+        part = ref[...].reshape(ref.shape[0] * HD, TILE)
         high = part.astype(BF)
-        both = nn(jnp.concatenate([high, (part - high.astype(F32)).astype(BF)], 0), swap)
-        return both[:HD] + both[HD:]
+        low_part = (part - high.astype(F32)).astype(BF)
+        ref[...] = (nn(high, swap) + nn(low_part, swap)).reshape(ref.shape)
+
+    unreverse(acc_pos)
+    unreverse(dq_pos)
 
     def gradients(tile):
-        extra = unreversed(acc_pos[tile]).T
+        extra = acc_pos[tile].T
         extra = jnp.concatenate([extra, jnp.zeros_like(extra)], 1)
         return (acc[tile] + extra) * factor
 
-    def finish(b, carry):
+    for b in range(blocks):
         keep_ref[b] = gradients(2 * b + half)
-        send_ref[pl.ds(b * TILE, TILE), :] = gradients(2 * b + 1 - half).astype(BF)
-        grad = scale * (dq_nat[b] + unreversed(dq_pos[b])).T
+        send_ref[b * TILE : (b + 1) * TILE, :] = gradients(2 * b + 1 - half).astype(BF)
+        grad = scale * (dq_nat[b] + dq_pos[b]).T
         query_ref[b] = jnp.concatenate([grad[: TILE // 2], grad[TILE // 2 :]], 1).astype(BF)
-        return carry
-
-    lax.fori_loop(0, blocks, finish, 0, unroll=True)
 
 
 def join_kernel(half_ref, keep_ref, bucket_ref, query_ref, came_ref, rel_ref, out_ref, weight, bucket):
@@ -530,16 +538,27 @@
             out_ref[pl.ds(start, rows), :] = ref[shard].astype(F32)
 
 
-def rel_kernel(got_ref, wk_ref, wq_ref, rel_ref):
+def rel_kernel(side_ref, got_ref, wk_ref, wq_ref, kept_ref, away_ref):
     heads = range(got_ref.shape[0])
-    base_b = got_ref.shape[1] - rel_ref.shape[0]
+    rows, width = kept_ref.shape
+    base_b = got_ref.shape[1] - rows
     rel = nt(jnp.concatenate([got_ref[h, base_b:, :HD] for h in heads], 1), wk_ref[...]) + nt(
         jnp.concatenate([got_ref[h, base_b:, HD:] for h in heads], 1), wq_ref[...]
     )
-    rel_ref[...] = rel.astype(BF)
-
-
-def unpack_kernel(got_ref, dq_ref, dk_ref, dv_ref, dwq_ref, dwk_ref):
+    left, right = rel[:, :width], rel[:, width:]
+    first = jnp.full(left.shape, side_ref[0], jnp.int32) == 0
+    kept_ref[...] = jnp.where(first, left, right).astype(BF)
+    away_ref[...] = jnp.where(first, right, left).astype(BF)
+
+
+def total_kernel(kept_ref, came_ref, after_ref, out_ref):
+    total = (kept_ref[...].astype(F32) + came_ref[...].astype(F32)).astype(BF)
+    for shard in range(out_ref.shape[0]):
+        out_ref[shard] = total
+
+
+def unpack_kernel(got_ref, dq_ref, dk_ref, dv_ref, dwq_ref, dwk_ref, done_ref):
+    done_ref[...] = jnp.zeros_like(done_ref)
     base_w = TILE + TILE // 2
     base_b = base_w + dwk_ref.shape[0]
     for g in range(got_ref.shape[0] // 2):
@@ -599,8 +618,8 @@
         [
             vm((4, tokens_dev, width), BF),
             vm((heads, tokens_dev, 4 * HD), BF),
-            pltpu.SemaphoreType.DMA((4,)),
-            pltpu.SemaphoreType.DMA((heads,)),
+            pltpu.SemaphoreType.DMA((heads // 2, 4)),
+            pltpu.SemaphoreType.DMA((heads // 2,)),
         ],
         source=HBM,
         target=HBM,
@@ -669,23 +688,26 @@
         scalars=1,
     )
     returned = spread(joined)
-    rel_rows = whole_call(
-        rel_kernel, (returned, w_key, w_query), shape((b_rows, depth), BF)
-    )
+    side = lax.axis_index("head").astype(jnp.int32).reshape(1)
+    rel_half = shape((b_rows, width), BF)
+    kept_rel, away_rel = whole_call(
+        rel_kernel, (side, returned, w_key, w_query), [rel_half, rel_half], scalars=1
+    )
+    came_rel = lax.ppermute(away_rel, "head", [(0, 1), (1, 0)])
     tokens = shape((tokens_dev, width), BF)
     weights = shape((w_rows, width), F32)
-    head_index = lax.axis_index("head")
-    mine_rel = lax.dynamic_slice_in_dim(rel_rows, head_index * width, width, 1)
-    far_rel = lax.dynamic_slice_in_dim(rel_rows, (1 - head_index) * width, width, 1)
-    far_rel = lax.ppermute(far_rel, "head", [(0, 1), (1, 0)])
-    rel_own = (mine_rel.astype(F32) + far_rel.astype(F32)).astype(BF)
-    near = spread(jnp.broadcast_to(rel_own[None], (heads, b_rows, width)))
+    query_grad, key_grad, value_grad, w_query_grad, w_key_grad, done = whole_call(
+        unpack_kernel,
+        (returned,),
+        [tokens, tokens, tokens, weights, weights, shape((8, TILE), F32)],
+    )
+    totals = whole_call(
+        total_kernel, (kept_rel, came_rel, done), shape((heads, b_rows, width), BF)
+    )
+    near = spread(totals)
     far = lax.ppermute(near, "seq", partners)
     rel_emb_grad = whole_call(
         weave_kernel, (half, near, far), shape((buckets, width), F32), scalars=1
-    )
-    query_grad, key_grad, value_grad, w_query_grad, w_key_grad = whole_call(
-        unpack_kernel, (returned,), [tokens, tokens, tokens, weights, weights]
     )
     return (query_grad, key_grad, value_grad, rel_emb_grad, w_query_grad, w_key_grad)
 

time: 85.7 us -> 84.8 us (0.989)
  Pallas kernels: 23.8 us -> 22.5 us
    pallas_call x8 -> x9, Pallas kernels: 23.8 us -> 22.5 us  [whole_call(): pl.pallas_call(kernel, out_shape=outputs, in_specs=[SMEM] * scalars + [so...]
    ppermute x1, waiting for transfers between devices: 0.41 us -> 1.53 us  [head_body(): far = lax.ppermute(near, 'seq', partners)]
    ppermute x1, waiting for transfers between devices: 2.43 us -> 1.3 us  [head_body(): came_rel = lax.ppermute(away_rel, 'head', [(0, 1), (1, 0)])]
where the time goes in v8:
time: 84.8 us; the launch traced here: 83.7 us
  waiting for transfers between devices  32.6 us (38%)
  Pallas kernels  22.5 us (27%)
  starting transfers between devices  12.9 us (15%)
  blocking collectives  11.6 us (14%)
  local copies, waits for them, and re-layouts  2.67 us (3%)
    all_to_all x2, waiting for transfers between devices, spread(): lax.all_to_all(pieces, 'seq', 0, 0, axis_index_groups=halves, tiled=True)  26.6 us
    pallas_call x9, Pallas kernels, whole_call(): pl.pallas_call(kernel, out_shape=outputs, in_specs=[SMEM] * scalars + [so...  22.5 us
    all_to_all x1, blocking collectives, spread(): lax.all_to_all(pieces, 'seq', 0, 0, axis_index_groups=halves, tiled=True)  11.6 us
    all_to_all x2, starting transfers between devices, spread(): lax.all_to_all(pieces, 'seq', 0, 0, axis_index_groups=halves, tiled=True)  11.2 us
    ppermute x1, waiting for transfers between devices, head_body(): came = lax.ppermute(sent, 'seq', partners)  1.71 us
  transfers between devices with their start and end apart: 6, of which 6 were waited for; matrix products, arithmetic and copies ran while one was open for 2% of the time, Pallas kernels for 2%

profile of v8, /device:TPU:0, one launch (start us, length us, event | category | flops | bytes accessed | tf_op | source)
XLA Modules:
  0.0 83.7 jit_solution(8083733356378867671)
XLA Ops:
  0.6 2.1 %shard_map.136 = bf16[8,128,256]{2,1,0:T(8,128)(2,1)} custom-call(bf16[128,512]{1,0:T(8,128)(2,1)} %q_ref.1, bf16[128,512]{1,0:T(8,128)(2,1)} %g_ref.1, bf16[128,512]{1,0:T(8,128)(2,1)} %k_ref.1, bf16[128,512]{1,0:T(8,128)(2,1)} %v_ref.1), custom_call_target="tpu_custom_call" | custom-call | tf_op jit(solution)/shard_map/pallas_call | solution.py:586
  2.7 7.4 %all-to-all-start = ((bf16[8,128,256]{2,1,0:T(8,128)(2,1)}), bf16[8,128,256]{2,1,0:T(8,128)(2,1)S(1)}, u32[]{:S(2)}, u32[]{:S(2)}) async-start(bf16[8,128,256]{2,1,0:T(8,128)(2,1)} %shard_map.136), calls=%async_computation | async-start | bytes 1048576 | tf_op jit(solution)/shard_map/all_to_all | solution.py:612
  10.2 0.7 copy-done.3
  10.8 0.1 rev.4
  10.9 0.7 copy-done.4
  11.6 0.1 pad_add_fusion.scalars_ref
  11.6 1.2 %constant_dynamic-slice_fusion = (bf16[1024,64]{1,0:T(8,128)(2,1)S(1)}, bf16[1024,64]{1,0:T(8,128)(2,1)S(1)}) fusion(bf16[1024,512]{1,0:T(8,128)(2,1)} %wq_ref.1, s32[]{:T(128)S(6)} %select_n.10, bf16[1024,512]{1,0:T(8,128)(2,1)} %wk_ref.1), kind=kLoop, calls=%fused_computation.6 | loop fusion | bytes 524292 | tf_op jit(solution)/shard_map/dynamic_slice | solution.py:632
  12.9 0.5 fusion.pos_ref
  13.4 0.9 %shard_map.137 = (bf16[512,1024]{1,0:T(8,128)(2,1)S(1)}, bf16[128,1024]{1,0:T(8,128)(2,1)S(1)}) custom-call(s32[9]{0:T(128)S(1)} %pad_add_fusion.scalars_ref, bf16[512,128]{1,0:T(8,128)(2,1)S(1)} %fusion.pos_ref, s32[1,1024]{1,0:T(1,128)S(1)} %bitcast.6), custom_call_target="tpu_custom_call" | custom-call | tf_op jit(solution)/shard_map/pallas_call | solution.py:586
  14.4 10.3 %all-to-all-done.own_ref = bf16[8,128,256]{2,1,0:T(8,128)(2,1)S(1)} async-done(((bf16[8,128,256]{2,1,0:T(8,128)(2,1)}), bf16[8,128,256]{2,1,0:T(8,128)(2,1)S(1)}, u32[]{:S(2)}, u32[]{:S(2)}) %all-to-all-start) | async-done | bytes 524320 | tf_op jit(solution)/shard_map/all_to_all | solution.py:612
  24.7 0.1 collective-permute-start
  24.8 1.5 %collective-permute-done.other_ref = bf16[8,128,128]{2,1,0:T(8,128)(2,1)S(1)} collective-permute-done((bf16[8,128,128]{2,1,0:T(8,128)(2,1)S(1)}, bf16[8,128,128]{2,1,0:T(8,128)(2,1)S(1)}, u32[]{:S(2)}, u32[]{:S(2)}) %collective-permute-start) | collective-permute-done | bytes 262176 | tf_op jit(solution)/shard_map/ppermute | solution.py:648
  26.3 15.3 %shard_map.139 = (bf16[1536,128]{1,0:T(8,128)(2,1)S(1)}, f32[8,128,128]{2,1,0:T(8,128)S(1)}, bf16[512,128]{1,0:T(8,128)(2,1)S(1)}, bf16[8,64,128]{2,1,0:T(8,128)(2,1)S(1)}) custom-call(s32[9]{0:T(128)S(1)} %pad_add_fusion.scalars_ref, bf16[8,128,256]{2,1,0:T(8,128)(2,1)S(1)} %all-to-all-done.own_ref, ...), custom_call_target="tpu_custom_call" | custom-call | tf_op jit(solution)/shard_map/pallas_call | solution.py:586
  41.6 1.7 %collective-permute-done.1.came_ref = bf16[1536,128]{1,0:T(8,128)(2,1)S(1)} collective-permute-done((bf16[1536,128]{1,0:T(8,128)(2,1)S(1)}, bf16[1536,128]{1,0:T(8,128)(2,1)S(1)}, u32[]{:S(2)}, u32[]{:S(2)}) %collective-permute-start.1) | collective-permute-done | bytes 393248 | tf_op jit(solution)/shard_map/ppermute | solution.py:682
  43.3 1.3 %shard_map.140 = bf16[8,288,128]{2,1,0:T(8,128)(2,1)} custom-call(s32[1]{0:T(128)} %bitcast.half_ref, f32[8,128,128]{2,1,0:T(8,128)S(1)} %get-tuple-element.22.keep_ref, bf16[512,128]{1,0:T(8,128)(2,1)S(1)} %get-tuple-element.23.bucket_ref, bf16[8,64,128]{2,1,0:T(8,128)(2,1)S(1)} %get-tuple-element.24.query_ref, ...), custom_call_target="tpu_custom_call" | custom-call | tf_op jit(solution)/shard_map/pallas_call | solution.py:586
  44.6 3.8 %all-to-all-start.1 = ((bf16[8,288,128]{2,1,0:T(8,128)(2,1)}), bf16[8,288,128]{2,1,0:T(8,128)(2,1)S(1)}, u32[]{:S(2)}, u32[]{:S(2)}) async-start(bf16[8,288,128]{2,1,0:T(8,128)(2,1)} %shard_map.140), calls=%async_computation.1 | async-start | bytes 1179648 | tf_op jit(solution)/shard_map/all_to_all | solution.py:612
  48.4 16.3 %all-to-all-done.1.got_ref = bf16[8,288,128]{2,1,0:T(8,128)(2,1)S(1)} async-done(((bf16[8,288,128]{2,1,0:T(8,128)(2,1)}), bf16[8,288,128]{2,1,0:T(8,128)(2,1)S(1)}, u32[]{:S(2)}, u32[]{:S(2)}) %all-to-all-start.1) | async-done | bytes 589856 | tf_op jit(solution)/shard_map/all_to_all | solution.py:612
  64.7 0.7 shard_map.142
  65.4 1.6 %collective-permute-start.2 = (bf16[32,512]{1,0:T(8,128)(2,1)S(1)}, bf16[32,512]{1,0:T(8,128)(2,1)S(1)}, u32[]{:S(2)}, u32[]{:S(2)}) collective-permute-start(bf16[32,512]{1,0:T(8,128)(2,1)S(1)} %get-tuple-element.30), channel_id=1, source_target_pairs={{0,1},{1,0},{2,3},{3,2},{4,5},{5,4},{6,7},{7,6},{8,9},{9,8},{10,11... | collective-permute-start | bytes 98312 | tf_op jit(solution)/shard_map/ppermute | solution.py:696
  67.0 1.1 %shard_map.141 = (bf16[128,512]{1,0:T(8,128)(2,1)}, bf16[128,512]{1,0:T(8,128)(2,1)}, bf16[128,512]{1,0:T(8,128)(2,1)}, f32[64,512]{1,0:T(8,128)}, f32[64,512]{1,0:T(8,128)}, /*index=5*/f32[8,128]{1,0:T(8,128)S(1)}) custom-call(bf16[8,288,128]{2,1,0:T(8,128)(2,1)S(1)} %all-to-all-done.1.got_ref), custom_call_target="tpu_custom_call" | custom-call | tf_op jit(solution)/shard_map/pallas_call | solution.py:586
  68.1 1.3 %collective-permute-done.2.came_ref = bf16[32,512]{1,0:T(8,128)(2,1)S(1)} collective-permute-done((bf16[32,512]{1,0:T(8,128)(2,1)S(1)}, bf16[32,512]{1,0:T(8,128)(2,1)S(1)}, u32[]{:S(2)}, u32[]{:S(2)}) %collective-permute-start.2) | collective-permute-done | bytes 32800 | tf_op jit(solution)/shard_map/ppermute | solution.py:696
  69.4 11.6 %all_to_all.15.near_ref = bf16[8,32,512]{2,1,0:T(8,128)(2,1)S(1)} all-to-all(bf16[8,32,512]{2,1,0:T(8,128)(2,1)S(1)} %shard_map.143), channel_id=1, replica_groups={{0,4,8,12,16,20,24,28},{2,6,10,14,18,22,26,30},{1,5,9,13,17,21,25,29},{..., dimensions={0} | all-to-all | bytes 524288 | tf_op jit(solution)/shard_map/all_to_all | solution.py:612
  81.1 1.5 %collective-permute-done.3.far_ref = bf16[8,32,512]{2,1,0:T(8,128)(2,1)S(1)} collective-permute-done((bf16[8,32,512]{2,1,0:T(8,128)(2,1)S(1)}, bf16[8,32,512]{2,1,0:T(8,128)(2,1)S(1)}, u32[]{:S(2)}, u32[]{:S(2)}) %collective-permute-start.3) | collective-permute-done | bytes 262176 | tf_op jit(solution)/shard_map/ppermute | solution.py:708
  82.6 1.0 %shard_map.144 = f32[512,512]{1,0:T(8,128)} custom-call(s32[1]{0:T(128)} %bitcast.half_ref, bf16[8,32,512]{2,1,0:T(8,128)(2,1)S(1)} %all_to_all.15.near_ref, bf16[8,32,512]{2,1,0:T(8,128)(2,1)S(1)} %collective-permute-done.3.far_ref), custom_call_target="tpu_custom_call" | custom-call | tf_op jit(solution)/shard_map/pallas_call | solution.py:586
  (12 shorter events, 0.2 us)
Async XLA Ops:
  2.7 10.2 %copy-start = (bf16[512,1024]{1,0:T(8,128)(2,1)S(1)}, bf16[512,1024]{1,0:T(8,128)(2,1)}, u32[]{:S(2)}) copy-start(bf16[512,1024]{1,0:T(8,128)(2,1)} %rel_ref.1) | copy-start | bytes 3145732
  2.7 21.9 %all-to-all-start = ((bf16[8,128,256]{2,1,0:T(8,128)(2,1)}), bf16[8,128,256]{2,1,0:T(8,128)(2,1)S(1)}, u32[]{:S(2)}, u32[]{:S(2)}) async-start(bf16[8,128,256]{2,1,0:T(8,128)(2,1)} %shard_map.136), calls=%async_computation | async-start | bytes 1048576 | tf_op jit(solution)/shard_map/all_to_all | solution.py:612
  10.1 0.7 copy-start.3
  10.9 0.7 copy-start.4
  24.7 1.6 %collective-permute-start = (bf16[8,128,128]{2,1,0:T(8,128)(2,1)S(1)}, bf16[8,128,128]{2,1,0:T(8,128)(2,1)S(1)}, u32[]{:S(2)}, u32[]{:S(2)}) collective-permute-start(bf16[8,128,128]{2,1,0:T(8,128)(2,1)S(1)} %shard_map.138), channel_id=1, source_target_pairs={{0,2},{2,0},{4,6},{6,4},{8,10},{10,8},{12,14},{14,12},{16,18},{18,... | collective-permute-start | bytes 786440 | tf_op jit(solution)/shard_map/ppermute | solution.py:648
  41.6 1.8 %collective-permute-start.1 = (bf16[1536,128]{1,0:T(8,128)(2,1)S(1)}, bf16[1536,128]{1,0:T(8,128)(2,1)S(1)}, u32[]{:S(2)}, u32[]{:S(2)}) collective-permute-start(bf16[1536,128]{1,0:T(8,128)(2,1)S(1)} %get-tuple-element.25), channel_id=1, source_target_pairs={{0,2},{2,0},{4,6},{6,4},{8,10},{10,8},{12,14},{14,12},{16,18},{18,... | collective-permute-start | bytes 1179656 | tf_op jit(solution)/shard_map/ppermute | solution.py:682
  43.3 21.4 %copy-start.2 = (bf16[1024,512]{1,0:T(8,128)(2,1)S(1)}, bf16[1024,512]{1,0:T(8,128)(2,1)}, u32[]{:S(2)}) copy-start(bf16[1024,512]{1,0:T(8,128)(2,1)} %wk_ref.1) | copy-start | bytes 3145732
  44.6 20.1 %copy-start.1 = (bf16[1024,512]{1,0:T(8,128)(2,1)S(1)}, bf16[1024,512]{1,0:T(8,128)(2,1)}, u32[]{:S(2)}) copy-start(bf16[1024,512]{1,0:T(8,128)(2,1)} %wq_ref.1) | copy-start | bytes 3145732
  44.6 20.1 %all-to-all-start.1 = ((bf16[8,288,128]{2,1,0:T(8,128)(2,1)}), bf16[8,288,128]{2,1,0:T(8,128)(2,1)S(1)}, u32[]{:S(2)}, u32[]{:S(2)}) async-start(bf16[8,288,128]{2,1,0:T(8,128)(2,1)} %shard_map.140), calls=%async_computation.1 | async-start | bytes 1179648 | tf_op jit(solution)/shard_map/all_to_all | solution.py:612
  65.4 4.0 %collective-permute-start.2 = (bf16[32,512]{1,0:T(8,128)(2,1)S(1)}, bf16[32,512]{1,0:T(8,128)(2,1)S(1)}, u32[]{:S(2)}, u32[]{:S(2)}) collective-permute-start(bf16[32,512]{1,0:T(8,128)(2,1)S(1)} %get-tuple-element.30), channel_id=1, source_target_pairs={{0,1},{1,0},{2,3},{3,2},{4,5},{5,4},{6,7},{7,6},{8,9},{9,8},{10,11... | collective-permute-start | bytes 98312 | tf_op jit(solution)/shard_map/ppermute | solution.py:696
  81.1 1.5 %collective-permute-start.3 = (bf16[8,32,512]{2,1,0:T(8,128)(2,1)S(1)}, bf16[8,32,512]{2,1,0:T(8,128)(2,1)S(1)}, u32[]{:S(2)}, u32[]{:S(2)}) collective-permute-start(bf16[8,32,512]{2,1,0:T(8,128)(2,1)S(1)} %all_to_all.15.near_ref), channel_id=1, source_target_pairs={{0,2},{2,0},{4,6},{6,4},{8,10},{10,8},{12,14},{14,12},{16,18},{18,... | collective-permute-start | bytes 786440 | tf_op jit(solution)/shard_map/ppermute | solution.py:708

commit v9 on v8

--- a/solution.py
+++ b/solution.py
@@ -298,7 +298,7 @@
 def head_kernel(
     scalars_ref, own_ref, other_ref, onehot, expanded,
     send_ref, keep_ref, bucket_ref, query_ref,
-    pk, pq, kvs, acc, acc_pos, g_key, g_query, k_t, k_rev, s_q, st, dp, dtile, pairs, dq_nat, dq_pos,
+    pk, pq, kvs, acc, acc_pos, g_key, g_query, k_t, k_rev, s_q, st, both, turns, dtile, pairs, moves, spreads, dq_nat, dq_pos,
 ):
     blocks = own_ref.shape[0]
     tiles = 2 * blocks
@@ -391,16 +391,18 @@
         s_q[:, 0 : (span + 1) * TILE] = nn(qd[:, :HD], pk[:, pl.ds(key_x, (span + 1) * TILE)])
         best = jnp.full((8, TILE), masked_score, F32)
         window_kv = kvs[pl.ds(first, span)].reshape(span * TILE, 2 * HD)
-        contents = nn(window_kv, right)
+        both[0 : span * TILE, :] = nn(window_kv, right)
+
+        def query_window(t):
+            return pl.multiple_of(2 * halo * TILE + delta - t * TILE, TILE)
+
         for t in range(span):
-            kv = window_kv[t * TILE : (t + 1) * TILE]
-            both = contents[t * TILE : (t + 1) * TILE]
-            query_x = pl.multiple_of(2 * halo * TILE + delta - t * TILE, TILE)
-            s_k = nn(kv[:, :HD], pq[:, pl.ds(query_x, 2 * TILE)])
-            key_term = pltpu.roll(
-                jnp.where(wrap, s_k[:, :TILE], s_k[:, TILE:]), 1, 1, stride=1, stride_axis=0
+            s_k = nn(
+                window_kv[t * TILE : (t + 1) * TILE, :HD], pq[:, pl.ds(query_window(t), 2 * TILE)]
             )
-            query_term = pltpu.roll(
+            st[t] = jnp.where(wrap, s_k[:, :TILE], s_k[:, TILE:])
+        for t in range(span):
+            turns[t] = pltpu.roll(
                 jnp.where(
                     wrap,
                     s_q[:, t * TILE : (t + 1) * TILE],
@@ -411,11 +413,12 @@
                 stride=1,
                 stride_axis=0,
             )
-            score = both[:, :TILE] + key_term + query_term.T
+        for t in range(span):
+            key_term = pltpu.roll(st[t], 1, 1, stride=1, stride_axis=0)
+            score = both[t * TILE : (t + 1) * TILE, :TILE] + key_term + turns[t].T
             inside = (row >= start - t * TILE) & (row < stop - t * TILE)
             score = jnp.where(inside, score, masked_score)
             st[t] = score
-            dp[t] = both[:, TILE:]
             best = jnp.maximum(best, jnp.max(score.reshape(TILE // 8, 8, TILE), 0))
         top = jnp.max(best, 0, keepdims=True)
         total = jnp.zeros((8, TILE), F32)
@@ -424,44 +427,48 @@
             expd = jnp.exp2((st[t] - top) * (scale * math.log2(math.e)))
             st[t] = expd
             total = total + jnp.sum(expd.reshape(TILE // 8, 8, TILE), 0)
-            dot = dot + jnp.sum((expd * dp[t]).reshape(TILE // 8, 8, TILE), 0)
+            dot = dot + jnp.sum((expd * both[t * TILE : (t + 1) * TILE, TILE:]).reshape(TILE // 8, 8, TILE), 0)
         inverse = 1.0 / jnp.sum(total, 0, keepdims=True)
         row_dot = jnp.sum(dot, 0, keepdims=True) * inverse
 
         lows = jnp.where(low, qd, jnp.zeros_like(qd))
         pair = jnp.concatenate([lows, jnp.where(low, jnp.zeros_like(qd), qd)], 0)
-        dq_t = jnp.zeros((HD, TILE), F32)
-        before = jnp.zeros((TILE, TILE), BF)
-        near = held = None
         for t in range(span):
             prob = st[t] * inverse
-            dscore = (prob * (dp[t] - row_dot)).astype(BF)
+            dscore = (prob * (both[t * TILE : (t + 1) * TILE, TILE:] - row_dot)).astype(BF)
             pairs[t] = jnp.concatenate([dscore, prob.astype(BF)], 1)
-            stacked = nn(
-                jnp.concatenate([k_t[first + t], swap], 0),
-                jnp.concatenate([dscore, dscore.T], 1),
-            )
+            moves[t] = jnp.concatenate([dscore, dscore.T], 1)
+        dq_t = jnp.zeros((HD, TILE), F32)
+        for t in range(span):
+            stacked = nn(jnp.concatenate([k_t[first + t], swap], 0), moves[t])
             dq_t = dq_t + stacked[:HD, :TILE]
-            query_x = pl.multiple_of(2 * halo * TILE + delta - t * TILE, TILE)
-            y = pltpu.roll(stacked[HD:, :TILE], 0, 1, stride=1, stride_axis=0).astype(BF)
-            last = near
+            st[t] = stacked[HD:, :TILE]
+            turns[t] = stacked[HD:, TILE:]
+        before = jnp.zeros((TILE, TILE), BF)
+        for t in range(span):
+            y = pltpu.roll(st[t], 0, 1, stride=1, stride_axis=0).astype(BF)
             near = y * keep
-            far = y - near
-            g_query[:, pl.ds(query_x, 2 * TILE)] += nn(
-                k_rev[first + t], jnp.concatenate([near, far], 1)
-            )
-            chunk = pq[:, pl.ds(query_x + TILE, TILE)]
-            if t == 0:
-                held = nt(chunk, far)
-            else:
-                back = nt(chunk, jnp.concatenate([last, far], 0))
-                acc_pos[first + t - 1] += held + back[:, :TILE]
-                held = back[:, TILE:]
-            z = pltpu.roll(stacked[HD:, TILE:], 0, 1, stride=1, stride_axis=0).astype(BF)
+            spreads[t] = jnp.concatenate([near, y - near], 1)
+            z = pltpu.roll(turns[t], 0, 1, stride=1, stride_axis=0).astype(BF)
             here = z * keep
             dtile[:, t * TILE : (t + 1) * TILE] = here + before
             before = z - here
-        acc_pos[first + span - 1] += held + nt(pq[:, pl.ds(query_x, TILE)], near)
+        held = None
+        for t in range(span):
+            query_x = query_window(t)
+            g_query[:, pl.ds(query_x, 2 * TILE)] += nn(k_rev[first + t], spreads[t])
+            chunk = pq[:, pl.ds(query_x + TILE, TILE)]
+            if t == 0:
+                held = nt(chunk, spreads[t, :, TILE:])
+            else:
+                back = nt(
+                    chunk, jnp.concatenate([spreads[t - 1, :, :TILE], spreads[t, :, TILE:]], 0)
+                )
+                acc_pos[first + t - 1] += held + back[:, :TILE]
+                held = back[:, TILE:]
+        acc_pos[first + span - 1] += held + nt(
+            pq[:, pl.ds(query_window(span - 1), TILE)], spreads[span - 1, :, :TILE]
+        )
         acc[pl.ds(first, span)] += nn(
             pairs[0:span].reshape(span * TILE, 2 * TILE), pair
         ).reshape(span, TILE, 2 * HD)
@@ -671,8 +678,11 @@
             vm((seq_count, HD, TILE), BF),
             vm((TILE, (span + 1) * TILE), F32),
             vm((span, TILE, TILE), F32),
+            vm((span * TILE, 2 * TILE), F32),
             vm((span, TILE, TILE), F32),
             vm((TILE, (span + 1) * TILE), BF),
+            vm((span, TILE, 2 * TILE), BF),
+            vm((span, TILE, 2 * TILE), BF),
             vm((span, TILE, 2 * TILE), BF),
             vm((heads, HD, TILE), F32),
             vm((heads, HD, TILE), F32),

time: 84.8 us -> 84.7 us (level); the launches traced: 83.7 us -> 84.6 us
  Pallas kernels: 22.5 us -> 23.4 us
    pallas_call x9, Pallas kernels: 22.5 us -> 23.4 us  [whole_call(): pl.pallas_call(kernel, out_shape=outputs, in_specs=[SMEM] * scalars + [so...]
where the time goes in v9:
time: 84.7 us; the launch traced here: 84.6 us
  waiting for transfers between devices  32.6 us (38%)
  Pallas kernels  23.4 us (28%)
  starting transfers between devices  12.9 us (15%)
  blocking collectives  11.6 us (14%)
  local copies, waits for them, and re-layouts  2.67 us (3%)
    all_to_all x2, waiting for transfers between devices, spread(): lax.all_to_all(pieces, 'seq', 0, 0, axis_index_groups=halves, tiled=True)  26.6 us
    pallas_call x9, Pallas kernels, whole_call(): pl.pallas_call(kernel, out_shape=outputs, in_specs=[SMEM] * scalars + [so...  23.4 us
    all_to_all x1, blocking collectives, spread(): lax.all_to_all(pieces, 'seq', 0, 0, axis_index_groups=halves, tiled=True)  11.6 us
    all_to_all x2, starting transfers between devices, spread(): lax.all_to_all(pieces, 'seq', 0, 0, axis_index_groups=halves, tiled=True)  11.2 us
    ppermute x1, waiting for transfers between devices, head_body(): came = lax.ppermute(sent, 'seq', partners)  1.71 us
  transfers between devices with their start and end apart: 6, of which 6 were waited for; matrix products, arithmetic and copies ran while one was open for 2% of the time, Pallas kernels for 2%

profile of v9, /device:TPU:0, one launch (start us, length us, event | category | flops | bytes accessed | tf_op | source)
XLA Modules:
  0.0 84.6 jit_solution(5648057022208858234)
XLA Ops:
  0.6 2.1 %shard_map.136 = bf16[8,128,256]{2,1,0:T(8,128)(2,1)} custom-call(bf16[128,512]{1,0:T(8,128)(2,1)} %q_ref.1, bf16[128,512]{1,0:T(8,128)(2,1)} %g_ref.1, bf16[128,512]{1,0:T(8,128)(2,1)} %k_ref.1, bf16[128,512]{1,0:T(8,128)(2,1)} %v_ref.1), custom_call_target="tpu_custom_call" | custom-call | tf_op jit(solution)/shard_map/pallas_call | solution.py:593
  2.7 7.4 %all-to-all-start = ((bf16[8,128,256]{2,1,0:T(8,128)(2,1)}), bf16[8,128,256]{2,1,0:T(8,128)(2,1)S(1)}, u32[]{:S(2)}, u32[]{:S(2)}) async-start(bf16[8,128,256]{2,1,0:T(8,128)(2,1)} %shard_map.136), calls=%async_computation | async-start | bytes 1048576 | tf_op jit(solution)/shard_map/all_to_all | solution.py:619
  10.2 0.7 copy-done.3
  10.8 0.1 rev.4
  10.9 0.7 copy-done.4
  11.6 0.1 pad_add_fusion.scalars_ref
  11.6 1.2 %constant_dynamic-slice_fusion = (bf16[1024,64]{1,0:T(8,128)(2,1)S(1)}, bf16[1024,64]{1,0:T(8,128)(2,1)S(1)}) fusion(bf16[1024,512]{1,0:T(8,128)(2,1)} %wq_ref.1, s32[]{:T(128)S(6)} %select_n.10, bf16[1024,512]{1,0:T(8,128)(2,1)} %wk_ref.1), kind=kLoop, calls=%fused_computation.6 | loop fusion | bytes 524292 | tf_op jit(solution)/shard_map/dynamic_slice | solution.py:639
  12.9 0.5 fusion.pos_ref
  13.4 0.9 %shard_map.137 = (bf16[512,1024]{1,0:T(8,128)(2,1)S(1)}, bf16[128,1024]{1,0:T(8,128)(2,1)S(1)}) custom-call(s32[9]{0:T(128)S(1)} %pad_add_fusion.scalars_ref, bf16[512,128]{1,0:T(8,128)(2,1)S(1)} %fusion.pos_ref, s32[1,1024]{1,0:T(1,128)S(1)} %bitcast.6), custom_call_target="tpu_custom_call" | custom-call | tf_op jit(solution)/shard_map/pallas_call | solution.py:593
  14.4 10.3 %all-to-all-done.own_ref = bf16[8,128,256]{2,1,0:T(8,128)(2,1)S(1)} async-done(((bf16[8,128,256]{2,1,0:T(8,128)(2,1)}), bf16[8,128,256]{2,1,0:T(8,128)(2,1)S(1)}, u32[]{:S(2)}, u32[]{:S(2)}) %all-to-all-start) | async-done | bytes 524320 | tf_op jit(solution)/shard_map/all_to_all | solution.py:619
  24.7 0.1 collective-permute-start
  24.8 1.5 %collective-permute-done.other_ref = bf16[8,128,128]{2,1,0:T(8,128)(2,1)S(1)} collective-permute-done((bf16[8,128,128]{2,1,0:T(8,128)(2,1)S(1)}, bf16[8,128,128]{2,1,0:T(8,128)(2,1)S(1)}, u32[]{:S(2)}, u32[]{:S(2)}) %collective-permute-start) | collective-permute-done | bytes 262176 | tf_op jit(solution)/shard_map/ppermute | solution.py:655
  26.3 16.2 %shard_map.139 = (bf16[1536,128]{1,0:T(8,128)(2,1)S(1)}, f32[8,128,128]{2,1,0:T(8,128)S(1)}, bf16[512,128]{1,0:T(8,128)(2,1)S(1)}, bf16[8,64,128]{2,1,0:T(8,128)(2,1)S(1)}) custom-call(s32[9]{0:T(128)S(1)} %pad_add_fusion.scalars_ref, bf16[8,128,256]{2,1,0:T(8,128)(2,1)S(1)} %all-to-all-done.own_ref, ...), custom_call_target="tpu_custom_call" | custom-call | tf_op jit(solution)/shard_map/pallas_call | solution.py:593
  42.5 1.7 %collective-permute-done.1.came_ref = bf16[1536,128]{1,0:T(8,128)(2,1)S(1)} collective-permute-done((bf16[1536,128]{1,0:T(8,128)(2,1)S(1)}, bf16[1536,128]{1,0:T(8,128)(2,1)S(1)}, u32[]{:S(2)}, u32[]{:S(2)}) %collective-permute-start.1) | collective-permute-done | bytes 393248 | tf_op jit(solution)/shard_map/ppermute | solution.py:692
  44.2 1.3 %shard_map.140 = bf16[8,288,128]{2,1,0:T(8,128)(2,1)} custom-call(s32[1]{0:T(128)} %bitcast.half_ref, f32[8,128,128]{2,1,0:T(8,128)S(1)} %get-tuple-element.22.keep_ref, bf16[512,128]{1,0:T(8,128)(2,1)S(1)} %get-tuple-element.23.bucket_ref, bf16[8,64,128]{2,1,0:T(8,128)(2,1)S(1)} %get-tuple-element.24.query_ref, ...), custom_call_target="tpu_custom_call" | custom-call | tf_op jit(solution)/shard_map/pallas_call | solution.py:593
  45.5 3.8 %all-to-all-start.1 = ((bf16[8,288,128]{2,1,0:T(8,128)(2,1)}), bf16[8,288,128]{2,1,0:T(8,128)(2,1)S(1)}, u32[]{:S(2)}, u32[]{:S(2)}) async-start(bf16[8,288,128]{2,1,0:T(8,128)(2,1)} %shard_map.140), calls=%async_computation.1 | async-start | bytes 1179648 | tf_op jit(solution)/shard_map/all_to_all | solution.py:619
  49.3 16.3 %all-to-all-done.1.got_ref = bf16[8,288,128]{2,1,0:T(8,128)(2,1)S(1)} async-done(((bf16[8,288,128]{2,1,0:T(8,128)(2,1)}), bf16[8,288,128]{2,1,0:T(8,128)(2,1)S(1)}, u32[]{:S(2)}, u32[]{:S(2)}) %all-to-all-start.1) | async-done | bytes 589856 | tf_op jit(solution)/shard_map/all_to_all | solution.py:619
  65.6 0.7 shard_map.142
  66.3 1.6 %collective-permute-start.2 = (bf16[32,512]{1,0:T(8,128)(2,1)S(1)}, bf16[32,512]{1,0:T(8,128)(2,1)S(1)}, u32[]{:S(2)}, u32[]{:S(2)}) collective-permute-start(bf16[32,512]{1,0:T(8,128)(2,1)S(1)} %get-tuple-element.30), channel_id=1, source_target_pairs={{0,1},{1,0},{2,3},{3,2},{4,5},{5,4},{6,7},{7,6},{8,9},{9,8},{10,11... | collective-permute-start | bytes 98312 | tf_op jit(solution)/shard_map/ppermute | solution.py:706
  67.9 1.1 %shard_map.141 = (bf16[128,512]{1,0:T(8,128)(2,1)}, bf16[128,512]{1,0:T(8,128)(2,1)}, bf16[128,512]{1,0:T(8,128)(2,1)}, f32[64,512]{1,0:T(8,128)}, f32[64,512]{1,0:T(8,128)}, /*index=5*/f32[8,128]{1,0:T(8,128)S(1)}) custom-call(bf16[8,288,128]{2,1,0:T(8,128)(2,1)S(1)} %all-to-all-done.1.got_ref), custom_call_target="tpu_custom_call" | custom-call | tf_op jit(solution)/shard_map/pallas_call | solution.py:593
  69.0 1.3 %collective-permute-done.2.came_ref = bf16[32,512]{1,0:T(8,128)(2,1)S(1)} collective-permute-done((bf16[32,512]{1,0:T(8,128)(2,1)S(1)}, bf16[32,512]{1,0:T(8,128)(2,1)S(1)}, u32[]{:S(2)}, u32[]{:S(2)}) %collective-permute-start.2) | collective-permute-done | bytes 32800 | tf_op jit(solution)/shard_map/ppermute | solution.py:706
  70.3 11.6 %all_to_all.15.near_ref = bf16[8,32,512]{2,1,0:T(8,128)(2,1)S(1)} all-to-all(bf16[8,32,512]{2,1,0:T(8,128)(2,1)S(1)} %shard_map.143), channel_id=1, replica_groups={{0,4,8,12,16,20,24,28},{2,6,10,14,18,22,26,30},{1,5,9,13,17,21,25,29},{..., dimensions={0} | all-to-all | bytes 524288 | tf_op jit(solution)/shard_map/all_to_all | solution.py:619
  82.0 1.5 %collective-permute-done.3.far_ref = bf16[8,32,512]{2,1,0:T(8,128)(2,1)S(1)} collective-permute-done((bf16[8,32,512]{2,1,0:T(8,128)(2,1)S(1)}, bf16[8,32,512]{2,1,0:T(8,128)(2,1)S(1)}, u32[]{:S(2)}, u32[]{:S(2)}) %collective-permute-start.3) | collective-permute-done | bytes 262176 | tf_op jit(solution)/shard_map/ppermute | solution.py:718
  83.5 1.0 %shard_map.144 = f32[512,512]{1,0:T(8,128)} custom-call(s32[1]{0:T(128)} %bitcast.half_ref, bf16[8,32,512]{2,1,0:T(8,128)(2,1)S(1)} %all_to_all.15.near_ref, bf16[8,32,512]{2,1,0:T(8,128)(2,1)S(1)} %collective-permute-done.3.far_ref), custom_call_target="tpu_custom_call" | custom-call | tf_op jit(solution)/shard_map/pallas_call | solution.py:593
  (12 shorter events, 0.2 us)
Async XLA Ops:
  2.7 10.2 %copy-start = (bf16[512,1024]{1,0:T(8,128)(2,1)S(1)}, bf16[512,1024]{1,0:T(8,128)(2,1)}, u32[]{:S(2)}) copy-start(bf16[512,1024]{1,0:T(8,128)(2,1)} %rel_ref.1) | copy-start | bytes 3145732
  2.7 21.9 %all-to-all-start = ((bf16[8,128,256]{2,1,0:T(8,128)(2,1)}), bf16[8,128,256]{2,1,0:T(8,128)(2,1)S(1)}, u32[]{:S(2)}, u32[]{:S(2)}) async-start(bf16[8,128,256]{2,1,0:T(8,128)(2,1)} %shard_map.136), calls=%async_computation | async-start | bytes 1048576 | tf_op jit(solution)/shard_map/all_to_all | solution.py:619
  10.1 0.7 copy-start.3
  10.9 0.7 copy-start.4
  24.7 1.6 %collective-permute-start = (bf16[8,128,128]{2,1,0:T(8,128)(2,1)S(1)}, bf16[8,128,128]{2,1,0:T(8,128)(2,1)S(1)}, u32[]{:S(2)}, u32[]{:S(2)}) collective-permute-start(bf16[8,128,128]{2,1,0:T(8,128)(2,1)S(1)} %shard_map.138), channel_id=1, source_target_pairs={{0,2},{2,0},{4,6},{6,4},{8,10},{10,8},{12,14},{14,12},{16,18},{18,... | collective-permute-start | bytes 786440 | tf_op jit(solution)/shard_map/ppermute | solution.py:655
  42.4 1.8 %collective-permute-start.1 = (bf16[1536,128]{1,0:T(8,128)(2,1)S(1)}, bf16[1536,128]{1,0:T(8,128)(2,1)S(1)}, u32[]{:S(2)}, u32[]{:S(2)}) collective-permute-start(bf16[1536,128]{1,0:T(8,128)(2,1)S(1)} %get-tuple-element.25), channel_id=1, source_target_pairs={{0,2},{2,0},{4,6},{6,4},{8,10},{10,8},{12,14},{14,12},{16,18},{18,... | collective-permute-start | bytes 1179656 | tf_op jit(solution)/shard_map/ppermute | solution.py:692
  44.2 21.4 %copy-start.2 = (bf16[1024,512]{1,0:T(8,128)(2,1)S(1)}, bf16[1024,512]{1,0:T(8,128)(2,1)}, u32[]{:S(2)}) copy-start(bf16[1024,512]{1,0:T(8,128)(2,1)} %wk_ref.1) | copy-start | bytes 3145732
  45.5 20.1 %copy-start.1 = (bf16[1024,512]{1,0:T(8,128)(2,1)S(1)}, bf16[1024,512]{1,0:T(8,128)(2,1)}, u32[]{:S(2)}) copy-start(bf16[1024,512]{1,0:T(8,128)(2,1)} %wq_ref.1) | copy-start | bytes 3145732
  45.5 20.1 %all-to-all-start.1 = ((bf16[8,288,128]{2,1,0:T(8,128)(2,1)}), bf16[8,288,128]{2,1,0:T(8,128)(2,1)S(1)}, u32[]{:S(2)}, u32[]{:S(2)}) async-start(bf16[8,288,128]{2,1,0:T(8,128)(2,1)} %shard_map.140), calls=%async_computation.1 | async-start | bytes 1179648 | tf_op jit(solution)/shard_map/all_to_all | solution.py:619
  66.3 4.0 %collective-permute-start.2 = (bf16[32,512]{1,0:T(8,128)(2,1)S(1)}, bf16[32,512]{1,0:T(8,128)(2,1)S(1)}, u32[]{:S(2)}, u32[]{:S(2)}) collective-permute-start(bf16[32,512]{1,0:T(8,128)(2,1)S(1)} %get-tuple-element.30), channel_id=1, source_target_pairs={{0,1},{1,0},{2,3},{3,2},{4,5},{5,4},{6,7},{7,6},{8,9},{9,8},{10,11... | collective-permute-start | bytes 98312 | tf_op jit(solution)/shard_map/ppermute | solution.py:706
  82.0 1.5 %collective-permute-start.3 = (bf16[8,32,512]{2,1,0:T(8,128)(2,1)S(1)}, bf16[8,32,512]{2,1,0:T(8,128)(2,1)S(1)}, u32[]{:S(2)}, u32[]{:S(2)}) collective-permute-start(bf16[8,32,512]{2,1,0:T(8,128)(2,1)S(1)} %all_to_all.15.near_ref), channel_id=1, source_target_pairs={{0,2},{2,0},{4,6},{6,4},{8,10},{10,8},{12,14},{14,12},{16,18},{18,... | collective-permute-start | bytes 786440 | tf_op jit(solution)/shard_map/ppermute | solution.py:718

commit v10 on v8

--- a/solution.py
+++ b/solution.py
@@ -298,7 +298,7 @@
 def head_kernel(
     scalars_ref, own_ref, other_ref, onehot, expanded,
     send_ref, keep_ref, bucket_ref, query_ref,
-    pk, pq, kvs, acc, acc_pos, g_key, g_query, k_t, k_rev, s_q, st, dp, dtile, pairs, dq_nat, dq_pos,
+    pk, pq, kvs, acc, acc_pos, g_key, g_query, k_t, s_q, st, dp, dtile, pairs, dq_nat, dq_pos,
 ):
     blocks = own_ref.shape[0]
     tiles = 2 * blocks
@@ -313,6 +313,7 @@
     swap = jnp.where(row + col == TILE - 1, 1.0, 0.0).astype(BF)
     wrap = row + col >= TILE - 1
     keep = jnp.where(col >= row, 1.0, 0.0).astype(BF)
+    keep_keys = jnp.where(wrap, 1.0, 0.0).astype(BF)
     low = col < HD
     for table, part in ((pk, expanded[:HD]), (pq, expanded[HD:])):
         table[...] = jnp.zeros_like(table)
@@ -328,10 +329,20 @@
             (other_ref[b], 2 * b + 1 - half),
         ):
             kvs[tile] = kv
-            k_t[tile] = kv.astype(F32).T[:HD].astype(BF)
-    k_rev[...] = (
-        nn(k_t[...].reshape(tiles * HD, TILE), swap).astype(BF).reshape(tiles, HD, TILE)
-    )
+            start = pl.multiple_of(tile * TILE, TILE)
+            k_t[:, pl.ds(start, TILE)] = kv.astype(F32).T[:HD].astype(BF)
+
+    def unskew(tile):
+        moved = jnp.concatenate(
+            [
+                pltpu.roll(tile[r : r + 8], TILE - 8 - r, 1) if r < TILE - 8 else tile[r : r + 8]
+                for r in range(0, TILE, 8)
+            ],
+            0,
+        )
+        for step in (4, 2, 1):
+            moved = jnp.where((row & step) == 0, pltpu.roll(moved, step, 1), moved)
+        return moved
 
     def block(b, carry):
         own = 2 * b + half
@@ -429,26 +440,26 @@
         row_dot = jnp.sum(dot, 0, keepdims=True) * inverse
 
         lows = jnp.where(low, qd, jnp.zeros_like(qd))
-        pair = jnp.concatenate([lows, jnp.where(low, jnp.zeros_like(qd), qd)], 0)
-        dq_t = jnp.zeros((HD, TILE), F32)
-        before = jnp.zeros((TILE, TILE), BF)
+        pair = jnp.concatenate(
+            [
+                jnp.concatenate([lows, swap], 1),
+                jnp.concatenate([qd - lows, jnp.zeros_like(swap)], 1),
+            ],
+            0,
+        )
         near = held = None
         for t in range(span):
             prob = st[t] * inverse
-            dscore = (prob * (dp[t] - row_dot)).astype(BF)
-            pairs[t] = jnp.concatenate([dscore, prob.astype(BF)], 1)
-            stacked = nn(
-                jnp.concatenate([k_t[first + t], swap], 0),
-                jnp.concatenate([dscore, dscore.T], 1),
-            )
-            dq_t = dq_t + stacked[:HD, :TILE]
+            exact = prob * (dp[t] - row_dot)
+            pairs[t] = jnp.concatenate([exact.astype(BF), prob.astype(BF)], 1)
             query_x = pl.multiple_of(2 * halo * TILE + delta - t * TILE, TILE)
-            y = pltpu.roll(stacked[HD:, :TILE], 0, 1, stride=1, stride_axis=0).astype(BF)
+            y = unskew(exact).astype(BF)
             last = near
-            near = y * keep
+            near = y * keep_keys
             far = y - near
             g_query[:, pl.ds(query_x, 2 * TILE)] += nn(
-                k_rev[first + t], jnp.concatenate([near, far], 1)
+                k_t[:, pl.ds(pl.multiple_of((first + t) * TILE, TILE), TILE)],
+                jnp.concatenate([near, far], 1),
             )
             chunk = pq[:, pl.ds(query_x + TILE, TILE)]
             if t == 0:
@@ -457,20 +468,25 @@
                 back = nt(chunk, jnp.concatenate([last, far], 0))
                 acc_pos[first + t - 1] += held + back[:, :TILE]
                 held = back[:, TILE:]
-            z = pltpu.roll(stacked[HD:, TILE:], 0, 1, stride=1, stride_axis=0).astype(BF)
+        acc_pos[first + span - 1] += held + nt(pq[:, pl.ds(query_x, TILE)], near)
+        lines = span * TILE
+        every = pairs[0:span].reshape(lines, 2 * TILE)
+        result = nn(every, pair)
+        acc[pl.ds(first, span)] += result[:, : 2 * HD].reshape(span, TILE, 2 * HD)
+        keys_t = k_t[:, pl.ds(pl.multiple_of(first * TILE, TILE), lines)]
+        dq_nat[b] = nn(keys_t, every[:, :TILE])
+        before = jnp.zeros((TILE, TILE), BF)
+        for t in range(span):
+            turned = result[t * TILE : (t + 1) * TILE, 2 * HD :].T
+            z = pltpu.roll(turned, 0, 1, stride=1, stride_axis=0).astype(BF)
             here = z * keep
             dtile[:, t * TILE : (t + 1) * TILE] = here + before
             before = z - here
-        acc_pos[first + span - 1] += held + nt(pq[:, pl.ds(query_x, TILE)], near)
-        acc[pl.ds(first, span)] += nn(
-            pairs[0:span].reshape(span * TILE, 2 * TILE), pair
-        ).reshape(span, TILE, 2 * HD)
         dtile[:, span * TILE : (span + 1) * TILE] = before
         spread_q = dtile[:, 0 : (span + 1) * TILE]
         window = pl.ds(key_x, (span + 1) * TILE)
         g_key[:, window] += nn(q_rev, spread_q)
         dq_pos[b] = nt(pk[:, window], spread_q)
-        dq_nat[b] = dq_t
 
     lax.fori_loop(0, blocks, block, 0)
 
@@ -494,7 +510,6 @@
         low_part = (part - high.astype(F32)).astype(BF)
         ref[...] = (nn(high, swap) + nn(low_part, swap)).reshape(ref.shape)
 
-    unreverse(acc_pos)
     unreverse(dq_pos)
 
     def gradients(tile):
@@ -667,8 +682,7 @@
             vm((seq_count, HD, TILE), F32),
             vm((HD, line), F32),
             vm((HD, line), F32),
-            vm((seq_count, HD, TILE), BF),
-            vm((seq_count, HD, TILE), BF),
+            vm((HD, seq_count * TILE), BF),
             vm((TILE, (span + 1) * TILE), F32),
             vm((span, TILE, TILE), F32),
             vm((span, TILE, TILE), F32),

time: 84.8 us -> 87 us (1.026)
  Pallas kernels: 22.5 us -> 24.9 us
    pallas_call x9, Pallas kernels: 22.5 us -> 24.9 us  [whole_call(): pl.pallas_call(kernel, out_shape=outputs, in_specs=[SMEM] * scalars + [so...]
where the time goes in v10:
time: 87 us; the launch traced here: 86 us
  waiting for transfers between devices  32.6 us (37%)
  Pallas kernels  24.9 us (29%)
  starting transfers between devices  12.9 us (15%)
  blocking collectives  11.6 us (13%)
  local copies, waits for them, and re-layouts  2.67 us (3%)
    all_to_all x2, waiting for transfers between devices, spread(): lax.all_to_all(pieces, 'seq', 0, 0, axis_index_groups=halves, tiled=True)  26.6 us
    pallas_call x9, Pallas kernels, whole_call(): pl.pallas_call(kernel, out_shape=outputs, in_specs=[SMEM] * scalars + [so...  24.9 us
    all_to_all x1, blocking collectives, spread(): lax.all_to_all(pieces, 'seq', 0, 0, axis_index_groups=halves, tiled=True)  11.6 us
    all_to_all x2, starting transfers between devices, spread(): lax.all_to_all(pieces, 'seq', 0, 0, axis_index_groups=halves, tiled=True)  11.2 us
  transfers between devices with their start and end apart: 6, of which 6 were waited for; matrix products, arithmetic and copies ran while one was open for 2% of the time, Pallas kernels for 2%

profile of v10, /device:TPU:0, one launch (start us, length us, event | category | flops | bytes accessed | tf_op | source)
XLA Modules:
  0.0 86.0 jit_solution(11376410034306455679)
XLA Ops:
  0.6 2.1 %shard_map.136 = bf16[8,128,256]{2,1,0:T(8,128)(2,1)} custom-call(bf16[128,512]{1,0:T(8,128)(2,1)} %q_ref.1, bf16[128,512]{1,0:T(8,128)(2,1)} %g_ref.1, bf16[128,512]{1,0:T(8,128)(2,1)} %k_ref.1, bf16[128,512]{1,0:T(8,128)(2,1)} %v_ref.1), custom_call_target="tpu_custom_call" | custom-call | tf_op jit(solution)/shard_map/pallas_call | solution.py:601
  2.7 7.4 %all-to-all-start = ((bf16[8,128,256]{2,1,0:T(8,128)(2,1)}), bf16[8,128,256]{2,1,0:T(8,128)(2,1)S(1)}, u32[]{:S(2)}, u32[]{:S(2)}) async-start(bf16[8,128,256]{2,1,0:T(8,128)(2,1)} %shard_map.136), calls=%async_computation | async-start | bytes 1048576 | tf_op jit(solution)/shard_map/all_to_all | solution.py:627
  10.2 0.7 copy-done.3
  10.8 0.1 rev.4
  10.9 0.7 copy-done.4
  11.6 0.1 pad_add_fusion.scalars_ref
  11.6 1.2 %constant_dynamic-slice_fusion = (bf16[1024,64]{1,0:T(8,128)(2,1)S(1)}, bf16[1024,64]{1,0:T(8,128)(2,1)S(1)}) fusion(bf16[1024,512]{1,0:T(8,128)(2,1)} %wq_ref.1, s32[]{:T(128)S(6)} %select_n.10, bf16[1024,512]{1,0:T(8,128)(2,1)} %wk_ref.1), kind=kLoop, calls=%fused_computation.6 | loop fusion | bytes 524292 | tf_op jit(solution)/shard_map/dynamic_slice | solution.py:647
  12.9 0.5 fusion.pos_ref
  13.4 0.9 %shard_map.137 = (bf16[512,1024]{1,0:T(8,128)(2,1)S(1)}, bf16[128,1024]{1,0:T(8,128)(2,1)S(1)}) custom-call(s32[9]{0:T(128)S(1)} %pad_add_fusion.scalars_ref, bf16[512,128]{1,0:T(8,128)(2,1)S(1)} %fusion.pos_ref, s32[1,1024]{1,0:T(1,128)S(1)} %bitcast.6), custom_call_target="tpu_custom_call" | custom-call | tf_op jit(solution)/shard_map/pallas_call | solution.py:601
  14.4 10.3 %all-to-all-done.own_ref = bf16[8,128,256]{2,1,0:T(8,128)(2,1)S(1)} async-done(((bf16[8,128,256]{2,1,0:T(8,128)(2,1)}), bf16[8,128,256]{2,1,0:T(8,128)(2,1)S(1)}, u32[]{:S(2)}, u32[]{:S(2)}) %all-to-all-start) | async-done | bytes 524320 | tf_op jit(solution)/shard_map/all_to_all | solution.py:627
  24.7 0.1 collective-permute-start
  24.8 1.5 %collective-permute-done.other_ref = bf16[8,128,128]{2,1,0:T(8,128)(2,1)S(1)} collective-permute-done((bf16[8,128,128]{2,1,0:T(8,128)(2,1)S(1)}, bf16[8,128,128]{2,1,0:T(8,128)(2,1)S(1)}, u32[]{:S(2)}, u32[]{:S(2)}) %collective-permute-start) | collective-permute-done | bytes 262176 | tf_op jit(solution)/shard_map/ppermute | solution.py:663
  26.3 17.6 %shard_map.139 = (bf16[1536,128]{1,0:T(8,128)(2,1)S(1)}, f32[8,128,128]{2,1,0:T(8,128)S(1)}, bf16[512,128]{1,0:T(8,128)(2,1)S(1)}, bf16[8,64,128]{2,1,0:T(8,128)(2,1)S(1)}) custom-call(s32[9]{0:T(128)S(1)} %pad_add_fusion.scalars_ref, bf16[8,128,256]{2,1,0:T(8,128)(2,1)S(1)} %all-to-all-done.own_ref, ...), custom_call_target="tpu_custom_call" | custom-call | tf_op jit(solution)/shard_map/pallas_call | solution.py:601
  44.0 1.7 %collective-permute-done.1.came_ref = bf16[1536,128]{1,0:T(8,128)(2,1)S(1)} collective-permute-done((bf16[1536,128]{1,0:T(8,128)(2,1)S(1)}, bf16[1536,128]{1,0:T(8,128)(2,1)S(1)}, u32[]{:S(2)}, u32[]{:S(2)}) %collective-permute-start.1) | collective-permute-done | bytes 393248 | tf_op jit(solution)/shard_map/ppermute | solution.py:696
  45.7 1.3 %shard_map.140 = bf16[8,288,128]{2,1,0:T(8,128)(2,1)} custom-call(s32[1]{0:T(128)} %bitcast.half_ref, f32[8,128,128]{2,1,0:T(8,128)S(1)} %get-tuple-element.22.keep_ref, bf16[512,128]{1,0:T(8,128)(2,1)S(1)} %get-tuple-element.23.bucket_ref, bf16[8,64,128]{2,1,0:T(8,128)(2,1)S(1)} %get-tuple-element.24.query_ref, ...), custom_call_target="tpu_custom_call" | custom-call | tf_op jit(solution)/shard_map/pallas_call | solution.py:601
  47.0 3.8 %all-to-all-start.1 = ((bf16[8,288,128]{2,1,0:T(8,128)(2,1)}), bf16[8,288,128]{2,1,0:T(8,128)(2,1)S(1)}, u32[]{:S(2)}, u32[]{:S(2)}) async-start(bf16[8,288,128]{2,1,0:T(8,128)(2,1)} %shard_map.140), calls=%async_computation.1 | async-start | bytes 1179648 | tf_op jit(solution)/shard_map/all_to_all | solution.py:627
  50.8 16.3 %all-to-all-done.1.got_ref = bf16[8,288,128]{2,1,0:T(8,128)(2,1)S(1)} async-done(((bf16[8,288,128]{2,1,0:T(8,128)(2,1)}), bf16[8,288,128]{2,1,0:T(8,128)(2,1)S(1)}, u32[]{:S(2)}, u32[]{:S(2)}) %all-to-all-start.1) | async-done | bytes 589856 | tf_op jit(solution)/shard_map/all_to_all | solution.py:627
  67.1 0.7 shard_map.142
  67.8 1.6 %collective-permute-start.2 = (bf16[32,512]{1,0:T(8,128)(2,1)S(1)}, bf16[32,512]{1,0:T(8,128)(2,1)S(1)}, u32[]{:S(2)}, u32[]{:S(2)}) collective-permute-start(bf16[32,512]{1,0:T(8,128)(2,1)S(1)} %get-tuple-element.30), channel_id=1, source_target_pairs={{0,1},{1,0},{2,3},{3,2},{4,5},{5,4},{6,7},{7,6},{8,9},{9,8},{10,11... | collective-permute-start | bytes 98312 | tf_op jit(solution)/shard_map/ppermute | solution.py:710
  69.4 1.1 %shard_map.141 = (bf16[128,512]{1,0:T(8,128)(2,1)}, bf16[128,512]{1,0:T(8,128)(2,1)}, bf16[128,512]{1,0:T(8,128)(2,1)}, f32[64,512]{1,0:T(8,128)}, f32[64,512]{1,0:T(8,128)}, /*index=5*/f32[8,128]{1,0:T(8,128)S(1)}) custom-call(bf16[8,288,128]{2,1,0:T(8,128)(2,1)S(1)} %all-to-all-done.1.got_ref), custom_call_target="tpu_custom_call" | custom-call | tf_op jit(solution)/shard_map/pallas_call | solution.py:601
  70.5 1.3 %collective-permute-done.2.came_ref = bf16[32,512]{1,0:T(8,128)(2,1)S(1)} collective-permute-done((bf16[32,512]{1,0:T(8,128)(2,1)S(1)}, bf16[32,512]{1,0:T(8,128)(2,1)S(1)}, u32[]{:S(2)}, u32[]{:S(2)}) %collective-permute-start.2) | collective-permute-done | bytes 32800 | tf_op jit(solution)/shard_map/ppermute | solution.py:710
  71.8 11.6 %all_to_all.15.near_ref = bf16[8,32,512]{2,1,0:T(8,128)(2,1)S(1)} all-to-all(bf16[8,32,512]{2,1,0:T(8,128)(2,1)S(1)} %shard_map.143), channel_id=1, replica_groups={{0,4,8,12,16,20,24,28},{2,6,10,14,18,22,26,30},{1,5,9,13,17,21,25,29},{..., dimensions={0} | all-to-all | bytes 524288 | tf_op jit(solution)/shard_map/all_to_all | solution.py:627
  83.5 1.5 %collective-permute-done.3.far_ref = bf16[8,32,512]{2,1,0:T(8,128)(2,1)S(1)} collective-permute-done((bf16[8,32,512]{2,1,0:T(8,128)(2,1)S(1)}, bf16[8,32,512]{2,1,0:T(8,128)(2,1)S(1)}, u32[]{:S(2)}, u32[]{:S(2)}) %collective-permute-start.3) | collective-permute-done | bytes 262176 | tf_op jit(solution)/shard_map/ppermute | solution.py:722
  85.0 1.0 %shard_map.144 = f32[512,512]{1,0:T(8,128)} custom-call(s32[1]{0:T(128)} %bitcast.half_ref, bf16[8,32,512]{2,1,0:T(8,128)(2,1)S(1)} %all_to_all.15.near_ref, bf16[8,32,512]{2,1,0:T(8,128)(2,1)S(1)} %collective-permute-done.3.far_ref), custom_call_target="tpu_custom_call" | custom-call | tf_op jit(solution)/shard_map/pallas_call | solution.py:601
  (12 shorter events, 0.2 us)
Async XLA Ops:
  2.7 10.2 %copy-start = (bf16[512,1024]{1,0:T(8,128)(2,1)S(1)}, bf16[512,1024]{1,0:T(8,128)(2,1)}, u32[]{:S(2)}) copy-start(bf16[512,1024]{1,0:T(8,128)(2,1)} %rel_ref.1) | copy-start | bytes 3145732
  2.7 21.9 %all-to-all-start = ((bf16[8,128,256]{2,1,0:T(8,128)(2,1)}), bf16[8,128,256]{2,1,0:T(8,128)(2,1)S(1)}, u32[]{:S(2)}, u32[]{:S(2)}) async-start(bf16[8,128,256]{2,1,0:T(8,128)(2,1)} %shard_map.136), calls=%async_computation | async-start | bytes 1048576 | tf_op jit(solution)/shard_map/all_to_all | solution.py:627
  10.1 0.7 copy-start.3
  10.9 0.7 copy-start.4
  24.7 1.6 %collective-permute-start = (bf16[8,128,128]{2,1,0:T(8,128)(2,1)S(1)}, bf16[8,128,128]{2,1,0:T(8,128)(2,1)S(1)}, u32[]{:S(2)}, u32[]{:S(2)}) collective-permute-start(bf16[8,128,128]{2,1,0:T(8,128)(2,1)S(1)} %shard_map.138), channel_id=1, source_target_pairs={{0,2},{2,0},{4,6},{6,4},{8,10},{10,8},{12,14},{14,12},{16,18},{18,... | collective-permute-start | bytes 786440 | tf_op jit(solution)/shard_map/ppermute | solution.py:663
  43.9 1.8 %collective-permute-start.1 = (bf16[1536,128]{1,0:T(8,128)(2,1)S(1)}, bf16[1536,128]{1,0:T(8,128)(2,1)S(1)}, u32[]{:S(2)}, u32[]{:S(2)}) collective-permute-start(bf16[1536,128]{1,0:T(8,128)(2,1)S(1)} %get-tuple-element.25), channel_id=1, source_target_pairs={{0,2},{2,0},{4,6},{6,4},{8,10},{10,8},{12,14},{14,12},{16,18},{18,... | collective-permute-start | bytes 1179656 | tf_op jit(solution)/shard_map/ppermute | solution.py:696
  45.7 21.4 %copy-start.2 = (bf16[1024,512]{1,0:T(8,128)(2,1)S(1)}, bf16[1024,512]{1,0:T(8,128)(2,1)}, u32[]{:S(2)}) copy-start(bf16[1024,512]{1,0:T(8,128)(2,1)} %wk_ref.1) | copy-start | bytes 3145732
  47.0 20.1 %copy-start.1 = (bf16[1024,512]{1,0:T(8,128)(2,1)S(1)}, bf16[1024,512]{1,0:T(8,128)(2,1)}, u32[]{:S(2)}) copy-start(bf16[1024,512]{1,0:T(8,128)(2,1)} %wq_ref.1) | copy-start | bytes 3145732
  47.0 20.1 %all-to-all-start.1 = ((bf16[8,288,128]{2,1,0:T(8,128)(2,1)}), bf16[8,288,128]{2,1,0:T(8,128)(2,1)S(1)}, u32[]{:S(2)}, u32[]{:S(2)}) async-start(bf16[8,288,128]{2,1,0:T(8,128)(2,1)} %shard_map.140), calls=%async_computation.1 | async-start | bytes 1179648 | tf_op jit(solution)/shard_map/all_to_all | solution.py:627
  67.8 4.0 %collective-permute-start.2 = (bf16[32,512]{1,0:T(8,128)(2,1)S(1)}, bf16[32,512]{1,0:T(8,128)(2,1)S(1)}, u32[]{:S(2)}, u32[]{:S(2)}) collective-permute-start(bf16[32,512]{1,0:T(8,128)(2,1)S(1)} %get-tuple-element.30), channel_id=1, source_target_pairs={{0,1},{1,0},{2,3},{3,2},{4,5},{5,4},{6,7},{7,6},{8,9},{9,8},{10,11... | collective-permute-start | bytes 98312 | tf_op jit(solution)/shard_map/ppermute | solution.py:710
  83.5 1.5 %collective-permute-start.3 = (bf16[8,32,512]{2,1,0:T(8,128)(2,1)S(1)}, bf16[8,32,512]{2,1,0:T(8,128)(2,1)S(1)}, u32[]{:S(2)}, u32[]{:S(2)}) collective-permute-start(bf16[8,32,512]{2,1,0:T(8,128)(2,1)S(1)} %all_to_all.15.near_ref), channel_id=1, source_target_pairs={{0,2},{2,0},{4,6},{6,4},{8,10},{10,8},{12,14},{14,12},{16,18},{18,... | collective-permute-start | bytes 786440 | tf_op jit(solution)/shard_map/ppermute | solution.py:722

commit v11 on v8

--- a/solution.py
+++ b/solution.py
@@ -315,12 +315,14 @@
     keep = jnp.where(col >= row, 1.0, 0.0).astype(BF)
     low = col < HD
     for table, part in ((pk, expanded[:HD]), (pq, expanded[HD:])):
-        table[...] = jnp.zeros_like(table)
+        table[:, 0:valid0] = jnp.zeros((HD, valid0), BF)
         table[:, valid0 : valid0 + valid] = part
+        rest = table.shape[1] - valid0 - valid
+        table[:, valid0 + valid :] = jnp.zeros((HD, rest), BF)
     acc[...] = jnp.zeros_like(acc)
     acc_pos[...] = jnp.zeros_like(acc_pos)
-    g_key[...] = jnp.zeros_like(g_key)
-    g_query[...] = jnp.zeros_like(g_query)
+    for g in (g_key, g_query):
+        g[:, valid0 : valid0 + valid] = jnp.zeros((HD, valid), F32)
 
     for b in range(blocks):
         for kv, tile in (
@@ -328,7 +330,7 @@
             (other_ref[b], 2 * b + 1 - half),
         ):
             kvs[tile] = kv
-            k_t[tile] = kv.astype(F32).T[:HD].astype(BF)
+            k_t[tile] = kv[:, :HD].astype(F32).T.astype(BF)
     k_rev[...] = (
         nn(k_t[...].reshape(tiles * HD, TILE), swap).astype(BF).reshape(tiles, HD, TILE)
     )
@@ -509,7 +511,9 @@
         query_ref[b] = jnp.concatenate([grad[: TILE // 2], grad[TILE // 2 :]], 1).astype(BF)
 
 
-def join_kernel(half_ref, keep_ref, bucket_ref, query_ref, came_ref, rel_ref, out_ref, weight, bucket):
+def join_kernel(
+    half_ref, keep_ref, bucket_ref, query_ref, came_ref, rel_ref, out_ref, weight, bucket, pieces, sems
+):
     blocks = keep_ref.shape[0]
     tiles = 2 * blocks
     half = half_ref[0]
@@ -517,16 +521,26 @@
     b_rows = bucket.shape[0] // tiles
     base_w = TILE + TILE // 2
     base_b = base_w + w_rows
+    for b in range(blocks):
+        came = came_ref[b * TILE : (b + 1) * TILE, :].astype(F32)
+        pieces[b, 0:TILE, :] = (keep_ref[b] + came).astype(BF)
+        pieces[b, TILE:base_w, :] = query_ref[b]
+    rows = (pl.ds(0, base_w), pl.ds(base_w, w_rows + b_rows))
+    stores = [
+        pltpu.make_async_copy(pieces.at[:, part], out_ref.at[:, part], sems.at[i])
+        for i, part in enumerate(rows)
+    ]
+    stores[0].start()
     total = bucket_ref[...].astype(F32) + came_ref[blocks * TILE :, :].astype(F32)
     bucket[...] = total
     weight[...] = nn(total.T.astype(BF), rel_ref[...]).T
     for b in range(blocks):
-        came = came_ref[b * TILE : (b + 1) * TILE, :].astype(F32)
         tile = 2 * b + half
-        out_ref[b, 0:TILE, :] = (keep_ref[b] + came).astype(BF)
-        out_ref[b, TILE:base_w, :] = query_ref[b]
-        out_ref[b, base_w:base_b, :] = weight[pl.ds(tile * w_rows, w_rows), :].astype(BF)
-        out_ref[b, base_b:, :] = bucket[pl.ds(tile * b_rows, b_rows), :].astype(BF)
+        pieces[b, base_w:base_b, :] = weight[pl.ds(tile * w_rows, w_rows), :].astype(BF)
+        pieces[b, base_b:, :] = bucket[pl.ds(tile * b_rows, b_rows), :].astype(BF)
+    stores[1].start()
+    for store in stores:
+        store.wait()
 
 
 def weave_kernel(half_ref, near_ref, far_ref, out_ref):
@@ -684,8 +698,14 @@
         join_kernel,
         (half, kept, bucket, query, came, rel_emb),
         shape((heads, rows, 2 * HD), BF),
-        [vm((depth, 2 * HD), F32), vm((buckets, 2 * HD), F32)],
+        [
+            vm((depth, 2 * HD), F32),
+            vm((buckets, 2 * HD), F32),
+            vm((heads, rows, 2 * HD), BF),
+            pltpu.SemaphoreType.DMA((2,)),
+        ],
         scalars=1,
+        target=HBM,
     )
     returned = spread(joined)
     side = lax.axis_index("head").astype(jnp.int32).reshape(1)

time: 84.8 us -> 85.1 us (level)
  no operation moved by 1% of the time
where the time goes in v11:
time: 85.1 us; the launch traced here: 83.8 us
  waiting for transfers between devices  32.6 us (38%)
  Pallas kernels  22.6 us (27%)
  starting transfers between devices  12.9 us (15%)
  blocking collectives  11.6 us (14%)
  local copies, waits for them, and re-layouts  2.67 us (3%)
    all_to_all x2, waiting for transfers between devices, spread(): lax.all_to_all(pieces, 'seq', 0, 0, axis_index_groups=halves, tiled=True)  26.6 us
    pallas_call x9, Pallas kernels, whole_call(): pl.pallas_call(kernel, out_shape=outputs, in_specs=[SMEM] * scalars + [so...  22.6 us
    all_to_all x1, blocking collectives, spread(): lax.all_to_all(pieces, 'seq', 0, 0, axis_index_groups=halves, tiled=True)  11.6 us
    all_to_all x2, starting transfers between devices, spread(): lax.all_to_all(pieces, 'seq', 0, 0, axis_index_groups=halves, tiled=True)  11.2 us
    ppermute x1, waiting for transfers between devices, head_body(): came = lax.ppermute(sent, 'seq', partners)  1.71 us
  transfers between devices with their start and end apart: 6, of which 6 were waited for; matrix products, arithmetic and copies ran while one was open for 2% of the time, Pallas kernels for 2%

profile of v11, /device:TPU:0, one launch (start us, length us, event | category | flops | bytes accessed | tf_op | source)
XLA Modules:
  0.0 83.8 jit_solution(3161593858974088314)
XLA Ops:
  0.6 2.1 %shard_map.136 = bf16[8,128,256]{2,1,0:T(8,128)(2,1)} custom-call(bf16[128,512]{1,0:T(8,128)(2,1)} %q_ref.1, bf16[128,512]{1,0:T(8,128)(2,1)} %g_ref.1, bf16[128,512]{1,0:T(8,128)(2,1)} %k_ref.1, bf16[128,512]{1,0:T(8,128)(2,1)} %v_ref.1), custom_call_target="tpu_custom_call" | custom-call | tf_op jit(solution)/shard_map/pallas_call | solution.py:600
  2.7 7.4 %all-to-all-start = ((bf16[8,128,256]{2,1,0:T(8,128)(2,1)}), bf16[8,128,256]{2,1,0:T(8,128)(2,1)S(1)}, u32[]{:S(2)}, u32[]{:S(2)}) async-start(bf16[8,128,256]{2,1,0:T(8,128)(2,1)} %shard_map.136), calls=%async_computation | async-start | bytes 1048576 | tf_op jit(solution)/shard_map/all_to_all | solution.py:626
  10.2 0.7 copy-done.3
  10.8 0.1 rev.4
  10.9 0.7 copy-done.4
  11.6 0.1 pad_add_fusion.scalars_ref
  11.6 1.2 %constant_dynamic-slice_fusion = (bf16[1024,64]{1,0:T(8,128)(2,1)S(1)}, bf16[1024,64]{1,0:T(8,128)(2,1)S(1)}) fusion(bf16[1024,512]{1,0:T(8,128)(2,1)} %wq_ref.1, s32[]{:T(128)S(6)} %select_n.10, bf16[1024,512]{1,0:T(8,128)(2,1)} %wk_ref.1), kind=kLoop, calls=%fused_computation.6 | loop fusion | bytes 524292 | tf_op jit(solution)/shard_map/dynamic_slice | solution.py:646
  12.9 0.5 fusion.pos_ref
  13.4 0.9 %shard_map.137 = (bf16[512,1024]{1,0:T(8,128)(2,1)S(1)}, bf16[128,1024]{1,0:T(8,128)(2,1)S(1)}) custom-call(s32[9]{0:T(128)S(1)} %pad_add_fusion.scalars_ref, bf16[512,128]{1,0:T(8,128)(2,1)S(1)} %fusion.pos_ref, s32[1,1024]{1,0:T(1,128)S(1)} %bitcast.6), custom_call_target="tpu_custom_call" | custom-call | tf_op jit(solution)/shard_map/pallas_call | solution.py:600
  14.4 10.3 %all-to-all-done.own_ref = bf16[8,128,256]{2,1,0:T(8,128)(2,1)S(1)} async-done(((bf16[8,128,256]{2,1,0:T(8,128)(2,1)}), bf16[8,128,256]{2,1,0:T(8,128)(2,1)S(1)}, u32[]{:S(2)}, u32[]{:S(2)}) %all-to-all-start) | async-done | bytes 524320 | tf_op jit(solution)/shard_map/all_to_all | solution.py:626
  24.7 0.1 collective-permute-start
  24.8 1.5 %collective-permute-done.other_ref = bf16[8,128,128]{2,1,0:T(8,128)(2,1)S(1)} collective-permute-done((bf16[8,128,128]{2,1,0:T(8,128)(2,1)S(1)}, bf16[8,128,128]{2,1,0:T(8,128)(2,1)S(1)}, u32[]{:S(2)}, u32[]{:S(2)}) %collective-permute-start) | collective-permute-done | bytes 262176 | tf_op jit(solution)/shard_map/ppermute | solution.py:662
  26.3 15.4 %shard_map.139 = (bf16[1536,128]{1,0:T(8,128)(2,1)S(1)}, f32[8,128,128]{2,1,0:T(8,128)S(1)}, bf16[512,128]{1,0:T(8,128)(2,1)S(1)}, bf16[8,64,128]{2,1,0:T(8,128)(2,1)S(1)}) custom-call(s32[9]{0:T(128)S(1)} %pad_add_fusion.scalars_ref, bf16[8,128,256]{2,1,0:T(8,128)(2,1)S(1)} %all-to-all-done.own_ref, ...), custom_call_target="tpu_custom_call" | custom-call | tf_op jit(solution)/shard_map/pallas_call | solution.py:600
  41.8 1.7 %collective-permute-done.1.came_ref = bf16[1536,128]{1,0:T(8,128)(2,1)S(1)} collective-permute-done((bf16[1536,128]{1,0:T(8,128)(2,1)S(1)}, bf16[1536,128]{1,0:T(8,128)(2,1)S(1)}, u32[]{:S(2)}, u32[]{:S(2)}) %collective-permute-start.1) | collective-permute-done | bytes 393248 | tf_op jit(solution)/shard_map/ppermute | solution.py:696
  43.5 1.3 %shard_map.140 = bf16[8,288,128]{2,1,0:T(8,128)(2,1)} custom-call(s32[1]{0:T(128)} %bitcast.half_ref, f32[8,128,128]{2,1,0:T(8,128)S(1)} %get-tuple-element.22.keep_ref, bf16[512,128]{1,0:T(8,128)(2,1)S(1)} %get-tuple-element.23.bucket_ref, bf16[8,64,128]{2,1,0:T(8,128)(2,1)S(1)} %get-tuple-element.24.query_ref, ...), custom_call_target="tpu_custom_call" | custom-call | tf_op jit(solution)/shard_map/pallas_call | solution.py:600
  44.8 3.8 %all-to-all-start.1 = ((bf16[8,288,128]{2,1,0:T(8,128)(2,1)}), bf16[8,288,128]{2,1,0:T(8,128)(2,1)S(1)}, u32[]{:S(2)}, u32[]{:S(2)}) async-start(bf16[8,288,128]{2,1,0:T(8,128)(2,1)} %shard_map.140), calls=%async_computation.1 | async-start | bytes 1179648 | tf_op jit(solution)/shard_map/all_to_all | solution.py:626
  48.5 16.3 %all-to-all-done.1.got_ref = bf16[8,288,128]{2,1,0:T(8,128)(2,1)S(1)} async-done(((bf16[8,288,128]{2,1,0:T(8,128)(2,1)}), bf16[8,288,128]{2,1,0:T(8,128)(2,1)S(1)}, u32[]{:S(2)}, u32[]{:S(2)}) %all-to-all-start.1) | async-done | bytes 589856 | tf_op jit(solution)/shard_map/all_to_all | solution.py:626
  64.8 0.7 shard_map.142
  65.6 1.5 %collective-permute-start.2 = (bf16[32,512]{1,0:T(8,128)(2,1)S(1)}, bf16[32,512]{1,0:T(8,128)(2,1)S(1)}, u32[]{:S(2)}, u32[]{:S(2)}) collective-permute-start(bf16[32,512]{1,0:T(8,128)(2,1)S(1)} %get-tuple-element.30), channel_id=1, source_target_pairs={{0,1},{1,0},{2,3},{3,2},{4,5},{5,4},{6,7},{7,6},{8,9},{9,8},{10,11... | collective-permute-start | bytes 98312 | tf_op jit(solution)/shard_map/ppermute | solution.py:716
  67.1 1.1 %shard_map.141 = (bf16[128,512]{1,0:T(8,128)(2,1)}, bf16[128,512]{1,0:T(8,128)(2,1)}, bf16[128,512]{1,0:T(8,128)(2,1)}, f32[64,512]{1,0:T(8,128)}, f32[64,512]{1,0:T(8,128)}, /*index=5*/f32[8,128]{1,0:T(8,128)S(1)}) custom-call(bf16[8,288,128]{2,1,0:T(8,128)(2,1)S(1)} %all-to-all-done.1.got_ref), custom_call_target="tpu_custom_call" | custom-call | tf_op jit(solution)/shard_map/pallas_call | solution.py:600
  68.2 1.3 %collective-permute-done.2.came_ref = bf16[32,512]{1,0:T(8,128)(2,1)S(1)} collective-permute-done((bf16[32,512]{1,0:T(8,128)(2,1)S(1)}, bf16[32,512]{1,0:T(8,128)(2,1)S(1)}, u32[]{:S(2)}, u32[]{:S(2)}) %collective-permute-start.2) | collective-permute-done | bytes 32800 | tf_op jit(solution)/shard_map/ppermute | solution.py:716
  69.6 11.6 %all_to_all.15.near_ref = bf16[8,32,512]{2,1,0:T(8,128)(2,1)S(1)} all-to-all(bf16[8,32,512]{2,1,0:T(8,128)(2,1)S(1)} %shard_map.143), channel_id=1, replica_groups={{0,4,8,12,16,20,24,28},{2,6,10,14,18,22,26,30},{1,5,9,13,17,21,25,29},{..., dimensions={0} | all-to-all | bytes 524288 | tf_op jit(solution)/shard_map/all_to_all | solution.py:626
  81.2 1.5 %collective-permute-done.3.far_ref = bf16[8,32,512]{2,1,0:T(8,128)(2,1)S(1)} collective-permute-done((bf16[8,32,512]{2,1,0:T(8,128)(2,1)S(1)}, bf16[8,32,512]{2,1,0:T(8,128)(2,1)S(1)}, u32[]{:S(2)}, u32[]{:S(2)}) %collective-permute-start.3) | collective-permute-done | bytes 262176 | tf_op jit(solution)/shard_map/ppermute | solution.py:728
  82.7 1.0 %shard_map.144 = f32[512,512]{1,0:T(8,128)} custom-call(s32[1]{0:T(128)} %bitcast.half_ref, bf16[8,32,512]{2,1,0:T(8,128)(2,1)S(1)} %all_to_all.15.near_ref, bf16[8,32,512]{2,1,0:T(8,128)(2,1)S(1)} %collective-permute-done.3.far_ref), custom_call_target="tpu_custom_call" | custom-call | tf_op jit(solution)/shard_map/pallas_call | solution.py:600
  (12 shorter events, 0.2 us)
Async XLA Ops:
  2.7 10.2 %copy-start = (bf16[512,1024]{1,0:T(8,128)(2,1)S(1)}, bf16[512,1024]{1,0:T(8,128)(2,1)}, u32[]{:S(2)}) copy-start(bf16[512,1024]{1,0:T(8,128)(2,1)} %rel_ref.1) | copy-start | bytes 3145732
  2.7 21.9 %all-to-all-start = ((bf16[8,128,256]{2,1,0:T(8,128)(2,1)}), bf16[8,128,256]{2,1,0:T(8,128)(2,1)S(1)}, u32[]{:S(2)}, u32[]{:S(2)}) async-start(bf16[8,128,256]{2,1,0:T(8,128)(2,1)} %shard_map.136), calls=%async_computation | async-start | bytes 1048576 | tf_op jit(solution)/shard_map/all_to_all | solution.py:626
  10.1 0.7 copy-start.3
  10.9 0.7 copy-start.4
  24.7 1.6 %collective-permute-start = (bf16[8,128,128]{2,1,0:T(8,128)(2,1)S(1)}, bf16[8,128,128]{2,1,0:T(8,128)(2,1)S(1)}, u32[]{:S(2)}, u32[]{:S(2)}) collective-permute-start(bf16[8,128,128]{2,1,0:T(8,128)(2,1)S(1)} %shard_map.138), channel_id=1, source_target_pairs={{0,2},{2,0},{4,6},{6,4},{8,10},{10,8},{12,14},{14,12},{16,18},{18,... | collective-permute-start | bytes 786440 | tf_op jit(solution)/shard_map/ppermute | solution.py:662
  41.7 1.8 %collective-permute-start.1 = (bf16[1536,128]{1,0:T(8,128)(2,1)S(1)}, bf16[1536,128]{1,0:T(8,128)(2,1)S(1)}, u32[]{:S(2)}, u32[]{:S(2)}) collective-permute-start(bf16[1536,128]{1,0:T(8,128)(2,1)S(1)} %get-tuple-element.25), channel_id=1, source_target_pairs={{0,2},{2,0},{4,6},{6,4},{8,10},{10,8},{12,14},{14,12},{16,18},{18,... | collective-permute-start | bytes 1179656 | tf_op jit(solution)/shard_map/ppermute | solution.py:696
  43.5 21.4 %copy-start.2 = (bf16[1024,512]{1,0:T(8,128)(2,1)S(1)}, bf16[1024,512]{1,0:T(8,128)(2,1)}, u32[]{:S(2)}) copy-start(bf16[1024,512]{1,0:T(8,128)(2,1)} %wk_ref.1) | copy-start | bytes 3145732
  44.7 20.1 %copy-start.1 = (bf16[1024,512]{1,0:T(8,128)(2,1)S(1)}, bf16[1024,512]{1,0:T(8,128)(2,1)}, u32[]{:S(2)}) copy-start(bf16[1024,512]{1,0:T(8,128)(2,1)} %wq_ref.1) | copy-start | bytes 3145732
  44.8 20.1 %all-to-all-start.1 = ((bf16[8,288,128]{2,1,0:T(8,128)(2,1)}), bf16[8,288,128]{2,1,0:T(8,128)(2,1)S(1)}, u32[]{:S(2)}, u32[]{:S(2)}) async-start(bf16[8,288,128]{2,1,0:T(8,128)(2,1)} %shard_map.140), calls=%async_computation.1 | async-start | bytes 1179648 | tf_op jit(solution)/shard_map/all_to_all | solution.py:626
  65.6 4.0 %collective-permute-start.2 = (bf16[32,512]{1,0:T(8,128)(2,1)S(1)}, bf16[32,512]{1,0:T(8,128)(2,1)S(1)}, u32[]{:S(2)}, u32[]{:S(2)}) collective-permute-start(bf16[32,512]{1,0:T(8,128)(2,1)S(1)} %get-tuple-element.30), channel_id=1, source_target_pairs={{0,1},{1,0},{2,3},{3,2},{4,5},{5,4},{6,7},{7,6},{8,9},{9,8},{10,11... | collective-permute-start | bytes 98312 | tf_op jit(solution)/shard_map/ppermute | solution.py:716
  81.2 1.5 %collective-permute-start.3 = (bf16[8,32,512]{2,1,0:T(8,128)(2,1)S(1)}, bf16[8,32,512]{2,1,0:T(8,128)(2,1)S(1)}, u32[]{:S(2)}, u32[]{:S(2)}) collective-permute-start(bf16[8,32,512]{2,1,0:T(8,128)(2,1)S(1)} %all_to_all.15.near_ref), channel_id=1, source_target_pairs={{0,2},{2,0},{4,6},{6,4},{8,10},{10,8},{12,14},{14,12},{16,18},{18,... | collective-permute-start | bytes 786440 | tf_op jit(solution)/shard_map/ppermute | solution.py:728

commit v12 on v8

--- a/solution.py
+++ b/solution.py
@@ -391,10 +391,9 @@
         s_q[:, 0 : (span + 1) * TILE] = nn(qd[:, :HD], pk[:, pl.ds(key_x, (span + 1) * TILE)])
         best = jnp.full((8, TILE), masked_score, F32)
         window_kv = kvs[pl.ds(first, span)].reshape(span * TILE, 2 * HD)
-        contents = nn(window_kv, right)
+        dp[0 : span * TILE, :] = nn(window_kv, right)
         for t in range(span):
             kv = window_kv[t * TILE : (t + 1) * TILE]
-            both = contents[t * TILE : (t + 1) * TILE]
             query_x = pl.multiple_of(2 * halo * TILE + delta - t * TILE, TILE)
             s_k = nn(kv[:, :HD], pq[:, pl.ds(query_x, 2 * TILE)])
             key_term = pltpu.roll(
@@ -411,11 +410,10 @@
                 stride=1,
                 stride_axis=0,
             )
-            score = both[:, :TILE] + key_term + query_term.T
+            score = dp[t * TILE : (t + 1) * TILE, :TILE] + key_term + query_term.T
             inside = (row >= start - t * TILE) & (row < stop - t * TILE)
             score = jnp.where(inside, score, masked_score)
             st[t] = score
-            dp[t] = both[:, TILE:]
             best = jnp.maximum(best, jnp.max(score.reshape(TILE // 8, 8, TILE), 0))
         top = jnp.max(best, 0, keepdims=True)
         total = jnp.zeros((8, TILE), F32)
@@ -424,7 +422,7 @@
             expd = jnp.exp2((st[t] - top) * (scale * math.log2(math.e)))
             st[t] = expd
             total = total + jnp.sum(expd.reshape(TILE // 8, 8, TILE), 0)
-            dot = dot + jnp.sum((expd * dp[t]).reshape(TILE // 8, 8, TILE), 0)
+            dot = dot + jnp.sum((expd * dp[t * TILE : (t + 1) * TILE, TILE:]).reshape(TILE // 8, 8, TILE), 0)
         inverse = 1.0 / jnp.sum(total, 0, keepdims=True)
         row_dot = jnp.sum(dot, 0, keepdims=True) * inverse
 
@@ -435,7 +433,7 @@
         near = held = None
         for t in range(span):
             prob = st[t] * inverse
-            dscore = (prob * (dp[t] - row_dot)).astype(BF)
+            dscore = (prob * (dp[t * TILE : (t + 1) * TILE, TILE:] - row_dot)).astype(BF)
             pairs[t] = jnp.concatenate([dscore, prob.astype(BF)], 1)
             stacked = nn(
                 jnp.concatenate([k_t[first + t], swap], 0),
@@ -671,7 +669,7 @@
             vm((seq_count, HD, TILE), BF),
             vm((TILE, (span + 1) * TILE), F32),
             vm((span, TILE, TILE), F32),
-            vm((span, TILE, TILE), F32),
+            vm((span * TILE, 2 * TILE), F32),
             vm((TILE, (span + 1) * TILE), BF),
             vm((span, TILE, 2 * TILE), BF),
             vm((heads, HD, TILE), F32),

time: 84.8 us -> 86.2 us (1.017)
  Pallas kernels: 22.5 us -> 24.1 us
    pallas_call x9, Pallas kernels: 22.5 us -> 24.1 us  [whole_call(): pl.pallas_call(kernel, out_shape=outputs, in_specs=[SMEM] * scalars + [so...]
where the time goes in v12:
time: 86.2 us; the launch traced here: 85.3 us
  waiting for transfers between devices  32.6 us (38%)
  Pallas kernels  24.1 us (28%)
  starting transfers between devices  12.9 us (15%)
  blocking collectives  11.6 us (13%)
  local copies, waits for them, and re-layouts  2.67 us (3%)
    all_to_all x2, waiting for transfers between devices, spread(): lax.all_to_all(pieces, 'seq', 0, 0, axis_index_groups=halves, tiled=True)  26.6 us
    pallas_call x9, Pallas kernels, whole_call(): pl.pallas_call(kernel, out_shape=outputs, in_specs=[SMEM] * scalars + [so...  24.1 us
    all_to_all x1, blocking collectives, spread(): lax.all_to_all(pieces, 'seq', 0, 0, axis_index_groups=halves, tiled=True)  11.6 us
    all_to_all x2, starting transfers between devices, spread(): lax.all_to_all(pieces, 'seq', 0, 0, axis_index_groups=halves, tiled=True)  11.2 us
  transfers between devices with their start and end apart: 6, of which 6 were waited for; matrix products, arithmetic and copies ran while one was open for 2% of the time, Pallas kernels for 2%

profile of v12, /device:TPU:0, one launch (start us, length us, event | category | flops | bytes accessed | tf_op | source)
XLA Modules:
  0.0 85.3 jit_solution(10123351705800076490)
XLA Ops:
  0.6 2.1 %shard_map.136 = bf16[8,128,256]{2,1,0:T(8,128)(2,1)} custom-call(bf16[128,512]{1,0:T(8,128)(2,1)} %q_ref.1, bf16[128,512]{1,0:T(8,128)(2,1)} %g_ref.1, bf16[128,512]{1,0:T(8,128)(2,1)} %k_ref.1, bf16[128,512]{1,0:T(8,128)(2,1)} %v_ref.1), custom_call_target="tpu_custom_call" | custom-call | tf_op jit(solution)/shard_map/pallas_call | solution.py:584
  2.7 7.4 %all-to-all-start = ((bf16[8,128,256]{2,1,0:T(8,128)(2,1)}), bf16[8,128,256]{2,1,0:T(8,128)(2,1)S(1)}, u32[]{:S(2)}, u32[]{:S(2)}) async-start(bf16[8,128,256]{2,1,0:T(8,128)(2,1)} %shard_map.136), calls=%async_computation | async-start | bytes 1048576 | tf_op jit(solution)/shard_map/all_to_all | solution.py:610
  10.2 0.7 copy-done.3
  10.8 0.1 rev.4
  10.9 0.7 copy-done.4
  11.6 0.1 pad_add_fusion.scalars_ref
  11.6 1.2 %constant_dynamic-slice_fusion = (bf16[1024,64]{1,0:T(8,128)(2,1)S(1)}, bf16[1024,64]{1,0:T(8,128)(2,1)S(1)}) fusion(bf16[1024,512]{1,0:T(8,128)(2,1)} %wq_ref.1, s32[]{:T(128)S(6)} %select_n.10, bf16[1024,512]{1,0:T(8,128)(2,1)} %wk_ref.1), kind=kLoop, calls=%fused_computation.6 | loop fusion | bytes 524292 | tf_op jit(solution)/shard_map/dynamic_slice | solution.py:630
  12.9 0.5 fusion.pos_ref
  13.4 0.9 %shard_map.137 = (bf16[512,1024]{1,0:T(8,128)(2,1)S(1)}, bf16[128,1024]{1,0:T(8,128)(2,1)S(1)}) custom-call(s32[9]{0:T(128)S(1)} %pad_add_fusion.scalars_ref, bf16[512,128]{1,0:T(8,128)(2,1)S(1)} %fusion.pos_ref, s32[1,1024]{1,0:T(1,128)S(1)} %bitcast.6), custom_call_target="tpu_custom_call" | custom-call | tf_op jit(solution)/shard_map/pallas_call | solution.py:584
  14.4 10.3 %all-to-all-done.own_ref = bf16[8,128,256]{2,1,0:T(8,128)(2,1)S(1)} async-done(((bf16[8,128,256]{2,1,0:T(8,128)(2,1)}), bf16[8,128,256]{2,1,0:T(8,128)(2,1)S(1)}, u32[]{:S(2)}, u32[]{:S(2)}) %all-to-all-start) | async-done | bytes 524320 | tf_op jit(solution)/shard_map/all_to_all | solution.py:610
  24.7 0.1 collective-permute-start
  24.8 1.5 %collective-permute-done.other_ref = bf16[8,128,128]{2,1,0:T(8,128)(2,1)S(1)} collective-permute-done((bf16[8,128,128]{2,1,0:T(8,128)(2,1)S(1)}, bf16[8,128,128]{2,1,0:T(8,128)(2,1)S(1)}, u32[]{:S(2)}, u32[]{:S(2)}) %collective-permute-start) | collective-permute-done | bytes 262176 | tf_op jit(solution)/shard_map/ppermute | solution.py:646
  26.3 16.9 %shard_map.139 = (bf16[1536,128]{1,0:T(8,128)(2,1)S(1)}, f32[8,128,128]{2,1,0:T(8,128)S(1)}, bf16[512,128]{1,0:T(8,128)(2,1)S(1)}, bf16[8,64,128]{2,1,0:T(8,128)(2,1)S(1)}) custom-call(s32[9]{0:T(128)S(1)} %pad_add_fusion.scalars_ref, bf16[8,128,256]{2,1,0:T(8,128)(2,1)S(1)} %all-to-all-done.own_ref, ...), custom_call_target="tpu_custom_call" | custom-call | tf_op jit(solution)/shard_map/pallas_call | solution.py:584
  43.2 1.7 %collective-permute-done.1.came_ref = bf16[1536,128]{1,0:T(8,128)(2,1)S(1)} collective-permute-done((bf16[1536,128]{1,0:T(8,128)(2,1)S(1)}, bf16[1536,128]{1,0:T(8,128)(2,1)S(1)}, u32[]{:S(2)}, u32[]{:S(2)}) %collective-permute-start.1) | collective-permute-done | bytes 393248 | tf_op jit(solution)/shard_map/ppermute | solution.py:680
  44.9 1.3 %shard_map.140 = bf16[8,288,128]{2,1,0:T(8,128)(2,1)} custom-call(s32[1]{0:T(128)} %bitcast.half_ref, f32[8,128,128]{2,1,0:T(8,128)S(1)} %get-tuple-element.22.keep_ref, bf16[512,128]{1,0:T(8,128)(2,1)S(1)} %get-tuple-element.23.bucket_ref, bf16[8,64,128]{2,1,0:T(8,128)(2,1)S(1)} %get-tuple-element.24.query_ref, ...), custom_call_target="tpu_custom_call" | custom-call | tf_op jit(solution)/shard_map/pallas_call | solution.py:584
  46.2 3.8 %all-to-all-start.1 = ((bf16[8,288,128]{2,1,0:T(8,128)(2,1)}), bf16[8,288,128]{2,1,0:T(8,128)(2,1)S(1)}, u32[]{:S(2)}, u32[]{:S(2)}) async-start(bf16[8,288,128]{2,1,0:T(8,128)(2,1)} %shard_map.140), calls=%async_computation.1 | async-start | bytes 1179648 | tf_op jit(solution)/shard_map/all_to_all | solution.py:610
  50.0 16.3 %all-to-all-done.1.got_ref = bf16[8,288,128]{2,1,0:T(8,128)(2,1)S(1)} async-done(((bf16[8,288,128]{2,1,0:T(8,128)(2,1)}), bf16[8,288,128]{2,1,0:T(8,128)(2,1)S(1)}, u32[]{:S(2)}, u32[]{:S(2)}) %all-to-all-start.1) | async-done | bytes 589856 | tf_op jit(solution)/shard_map/all_to_all | solution.py:610
  66.3 0.7 shard_map.142
  67.0 1.6 %collective-permute-start.2 = (bf16[32,512]{1,0:T(8,128)(2,1)S(1)}, bf16[32,512]{1,0:T(8,128)(2,1)S(1)}, u32[]{:S(2)}, u32[]{:S(2)}) collective-permute-start(bf16[32,512]{1,0:T(8,128)(2,1)S(1)} %get-tuple-element.30), channel_id=1, source_target_pairs={{0,1},{1,0},{2,3},{3,2},{4,5},{5,4},{6,7},{7,6},{8,9},{9,8},{10,11... | collective-permute-start | bytes 98312 | tf_op jit(solution)/shard_map/ppermute | solution.py:694
  68.6 1.1 %shard_map.141 = (bf16[128,512]{1,0:T(8,128)(2,1)}, bf16[128,512]{1,0:T(8,128)(2,1)}, bf16[128,512]{1,0:T(8,128)(2,1)}, f32[64,512]{1,0:T(8,128)}, f32[64,512]{1,0:T(8,128)}, /*index=5*/f32[8,128]{1,0:T(8,128)S(1)}) custom-call(bf16[8,288,128]{2,1,0:T(8,128)(2,1)S(1)} %all-to-all-done.1.got_ref), custom_call_target="tpu_custom_call" | custom-call | tf_op jit(solution)/shard_map/pallas_call | solution.py:584
  69.7 1.3 %collective-permute-done.2.came_ref = bf16[32,512]{1,0:T(8,128)(2,1)S(1)} collective-permute-done((bf16[32,512]{1,0:T(8,128)(2,1)S(1)}, bf16[32,512]{1,0:T(8,128)(2,1)S(1)}, u32[]{:S(2)}, u32[]{:S(2)}) %collective-permute-start.2) | collective-permute-done | bytes 32800 | tf_op jit(solution)/shard_map/ppermute | solution.py:694
  71.0 11.6 %all_to_all.15.near_ref = bf16[8,32,512]{2,1,0:T(8,128)(2,1)S(1)} all-to-all(bf16[8,32,512]{2,1,0:T(8,128)(2,1)S(1)} %shard_map.143), channel_id=1, replica_groups={{0,4,8,12,16,20,24,28},{2,6,10,14,18,22,26,30},{1,5,9,13,17,21,25,29},{..., dimensions={0} | all-to-all | bytes 524288 | tf_op jit(solution)/shard_map/all_to_all | solution.py:610
  82.7 1.5 %collective-permute-done.3.far_ref = bf16[8,32,512]{2,1,0:T(8,128)(2,1)S(1)} collective-permute-done((bf16[8,32,512]{2,1,0:T(8,128)(2,1)S(1)}, bf16[8,32,512]{2,1,0:T(8,128)(2,1)S(1)}, u32[]{:S(2)}, u32[]{:S(2)}) %collective-permute-start.3) | collective-permute-done | bytes 262176 | tf_op jit(solution)/shard_map/ppermute | solution.py:706
  84.2 1.0 %shard_map.144 = f32[512,512]{1,0:T(8,128)} custom-call(s32[1]{0:T(128)} %bitcast.half_ref, bf16[8,32,512]{2,1,0:T(8,128)(2,1)S(1)} %all_to_all.15.near_ref, bf16[8,32,512]{2,1,0:T(8,128)(2,1)S(1)} %collective-permute-done.3.far_ref), custom_call_target="tpu_custom_call" | custom-call | tf_op jit(solution)/shard_map/pallas_call | solution.py:584
  (12 shorter events, 0.2 us)
Async XLA Ops:
  2.7 10.2 %copy-start = (bf16[512,1024]{1,0:T(8,128)(2,1)S(1)}, bf16[512,1024]{1,0:T(8,128)(2,1)}, u32[]{:S(2)}) copy-start(bf16[512,1024]{1,0:T(8,128)(2,1)} %rel_ref.1) | copy-start | bytes 3145732
  2.7 21.9 %all-to-all-start = ((bf16[8,128,256]{2,1,0:T(8,128)(2,1)}), bf16[8,128,256]{2,1,0:T(8,128)(2,1)S(1)}, u32[]{:S(2)}, u32[]{:S(2)}) async-start(bf16[8,128,256]{2,1,0:T(8,128)(2,1)} %shard_map.136), calls=%async_computation | async-start | bytes 1048576 | tf_op jit(solution)/shard_map/all_to_all | solution.py:610
  10.1 0.7 copy-start.3
  10.9 0.7 copy-start.4
  24.7 1.6 %collective-permute-start = (bf16[8,128,128]{2,1,0:T(8,128)(2,1)S(1)}, bf16[8,128,128]{2,1,0:T(8,128)(2,1)S(1)}, u32[]{:S(2)}, u32[]{:S(2)}) collective-permute-start(bf16[8,128,128]{2,1,0:T(8,128)(2,1)S(1)} %shard_map.138), channel_id=1, source_target_pairs={{0,2},{2,0},{4,6},{6,4},{8,10},{10,8},{12,14},{14,12},{16,18},{18,... | collective-permute-start | bytes 786440 | tf_op jit(solution)/shard_map/ppermute | solution.py:646
  43.1 1.8 %collective-permute-start.1 = (bf16[1536,128]{1,0:T(8,128)(2,1)S(1)}, bf16[1536,128]{1,0:T(8,128)(2,1)S(1)}, u32[]{:S(2)}, u32[]{:S(2)}) collective-permute-start(bf16[1536,128]{1,0:T(8,128)(2,1)S(1)} %get-tuple-element.25), channel_id=1, source_target_pairs={{0,2},{2,0},{4,6},{6,4},{8,10},{10,8},{12,14},{14,12},{16,18},{18,... | collective-permute-start | bytes 1179656 | tf_op jit(solution)/shard_map/ppermute | solution.py:680
  44.9 21.4 %copy-start.2 = (bf16[1024,512]{1,0:T(8,128)(2,1)S(1)}, bf16[1024,512]{1,0:T(8,128)(2,1)}, u32[]{:S(2)}) copy-start(bf16[1024,512]{1,0:T(8,128)(2,1)} %wk_ref.1) | copy-start | bytes 3145732
  46.2 20.1 %copy-start.1 = (bf16[1024,512]{1,0:T(8,128)(2,1)S(1)}, bf16[1024,512]{1,0:T(8,128)(2,1)}, u32[]{:S(2)}) copy-start(bf16[1024,512]{1,0:T(8,128)(2,1)} %wq_ref.1) | copy-start | bytes 3145732
  46.2 20.1 %all-to-all-start.1 = ((bf16[8,288,128]{2,1,0:T(8,128)(2,1)}), bf16[8,288,128]{2,1,0:T(8,128)(2,1)S(1)}, u32[]{:S(2)}, u32[]{:S(2)}) async-start(bf16[8,288,128]{2,1,0:T(8,128)(2,1)} %shard_map.140), calls=%async_computation.1 | async-start | bytes 1179648 | tf_op jit(solution)/shard_map/all_to_all | solution.py:610
  67.0 4.0 %collective-permute-start.2 = (bf16[32,512]{1,0:T(8,128)(2,1)S(1)}, bf16[32,512]{1,0:T(8,128)(2,1)S(1)}, u32[]{:S(2)}, u32[]{:S(2)}) collective-permute-start(bf16[32,512]{1,0:T(8,128)(2,1)S(1)} %get-tuple-element.30), channel_id=1, source_target_pairs={{0,1},{1,0},{2,3},{3,2},{4,5},{5,4},{6,7},{7,6},{8,9},{9,8},{10,11... | collective-permute-start | bytes 98312 | tf_op jit(solution)/shard_map/ppermute | solution.py:694
  82.7 1.5 %collective-permute-start.3 = (bf16[8,32,512]{2,1,0:T(8,128)(2,1)S(1)}, bf16[8,32,512]{2,1,0:T(8,128)(2,1)S(1)}, u32[]{:S(2)}, u32[]{:S(2)}) collective-permute-start(bf16[8,32,512]{2,1,0:T(8,128)(2,1)S(1)} %all_to_all.15.near_ref), channel_id=1, source_target_pairs={{0,2},{2,0},{4,6},{6,4},{8,10},{10,8},{12,14},{14,12},{16,18},{18,... | collective-permute-start | bytes 786440 | tf_op jit(solution)/shard_map/ppermute | solution.py:706
